TPU v7x, 32 devices: a whole 2x2x4 slice. The times are simulated.
32 devices in a mesh: chan: 8 (over z, core), freq: 4 (over y, x).
Axes of the slice: x: 2, y: 2, z: 4, core: 2. Of those that a mesh axis runs over, the one named last changes fastest.
Arguments:
- strain: bfloat16 [512, 30720], P('chan', 'freq'), may hold values from -500 to 500
- quality: int32 [512], replicated, may hold values 0 or 1
- offset_reach: int32 [512], replicated, may hold values from 128 to 256, as said below
Outputs:
- stacked: float32 [8, 2, 3840, 256], P('chan', None, 'freq')
Inputs may be any that keep to these rules, and one draw needn't show every extreme that they name: `offset_reach`: 256 is reached by some channel.
All inputs are finite; a program needn't handle non-finite values.
Results may differ from a plain program's by a relative error of at most 0.011.
Values may be sent and summed in bfloat16 or wider, within the bound.
No kernel may reach another device: no remote copies, remote signals or barrier semaphores. Data moves between devices by JAX's collectives and lax.ppermute only.
A program may use at most 64 MiB of HBM per device.

v0:
```python
import math

import jax
import jax.numpy as jnp
from jax import lax
from jax.sharding import PartitionSpec as P

BAND = 256
TBLK = 128


band_low = 0.004
band_high = 0.48
level_eps = 1e-05
item_batch = 4
row_block = 32


def extended_2(cells, sides, width):
    for axis, dim in sides:
        count = lax.axis_size(axis)
        ends = count - 1
        head = lax.slice_in_dim(cells, 0, width, axis=dim)
        tail = lax.slice_in_dim(cells, cells.shape[dim] - width, cells.shape[dim], axis=dim)
        cells = jnp.concatenate(
            [
                lax.ppermute(tail, axis, [(i, (i + 1) % count) for i in range(ends)]),
                cells,
                lax.ppermute(head, axis, [((i + 1) % count, i) for i in range(ends)]),
            ],
            axis=dim,
        )
    return cells


def shifted(x, axis, by):
    size = lax.axis_size(axis)
    pairs = [(i, i + by) for i in range(size) if 0 <= i + by < size]
    return lax.ppermute(x, axis, pairs)


def tap_values(offset, half_span):
    window = 0.5 + 0.5 * jnp.cos(jnp.pi * offset / (half_span + 1))
    response = 2.0 * band_high * jnp.sinc(2.0 * band_high * offset) - 2.0 * band_low * jnp.sinc(
        2.0 * band_low * offset
    )
    return jnp.where(jnp.abs(offset) <= half_span, window * response, 0.0)


def stencil_tables(half_span, boxed):
    row_index = jnp.arange(half_span)[:, None]
    col_index = jnp.arange(half_span)[None, :]
    tables = []
    for shift_q in (-1, 0, 1):
        offset = (col_index - row_index - half_span * shift_q).astype(jnp.float32)
        if boxed:
            entry_value = jnp.where(jnp.abs(offset) <= half_span, 1.0, 0.0)
        else:
            entry_value = tap_values(offset, half_span)
        tables.append(entry_value)
    return jnp.stack(tables).astype(jnp.bfloat16)


def apply_stencil(blocks, tables):
    total = jnp.einsum("cbr,rp->cbp", blocks[:, :-2], tables[0], preferred_element_type=jnp.float32)
    total = total + jnp.einsum(
        "cbr,rp->cbp", blocks[:, 1:-1], tables[1], preferred_element_type=jnp.float32
    )
    total = total + jnp.einsum(
        "cbr,rp->cbp", blocks[:, 2:], tables[2], preferred_element_type=jnp.float32
    )
    return total


def whiten(padded, half_span):
    channel_count = padded.shape[0]
    blocks = padded.reshape(channel_count, -1, half_span)
    filtered = apply_stencil(blocks, stencil_tables(half_span, False))
    magnitude = jnp.abs(filtered).astype(jnp.bfloat16)
    level = apply_stencil(magnitude, stencil_tables(half_span, True)) / (2 * half_span + 1)
    whitened = filtered[:, 1:-1, :] / (level + level_eps)
    return whitened.astype(jnp.bfloat16)


def spectra(whitened):
    count_a = whitened.shape[-2]
    half_span = whitened.shape[-1]
    length = count_a * half_span
    a_index = jnp.arange(count_a, dtype=jnp.int32)
    b_index = jnp.arange(half_span, dtype=jnp.int32)
    k_index = jnp.arange(half_span // 2, dtype=jnp.int32)
    angle = (a_index[:, None] * a_index[None, :] % count_a).astype(jnp.float32) * (
        2.0 * math.pi / count_a
    )
    first = jnp.concatenate([jnp.cos(angle), -jnp.sin(angle)], axis=1).astype(jnp.bfloat16)
    section = jnp.einsum("...ab,ak->...kb", whitened, first, preferred_element_type=jnp.float32)
    section_re = section[..., :count_a, :]
    section_im = section[..., count_a:, :]
    twist = (a_index[:, None] * b_index[None, :] % length).astype(jnp.float32) * (
        2.0 * math.pi / length
    )
    cos_twist = jnp.cos(twist)
    sin_twist = jnp.sin(twist)
    twisted_re = (section_re * cos_twist + section_im * sin_twist).astype(jnp.bfloat16)
    twisted_im = (section_im * cos_twist - section_re * sin_twist).astype(jnp.bfloat16)
    turn = (b_index[:, None] * k_index[None, :] % half_span).astype(jnp.float32) * (
        2.0 * math.pi / half_span
    )
    cos_turn = jnp.cos(turn)
    sin_turn = jnp.sin(turn)
    upper = jnp.stack([cos_turn, -sin_turn], axis=2).astype(jnp.bfloat16)
    lower = jnp.stack([sin_turn, cos_turn], axis=2).astype(jnp.bfloat16)
    result = jnp.einsum("ckb,bjp->jkpc", twisted_re, upper, preferred_element_type=jnp.float32)
    result = result + jnp.einsum(
        "ckb,bjp->jkpc", twisted_im, lower, preferred_element_type=jnp.float32
    )
    return (result * (1.0 / math.sqrt(length))).astype(jnp.bfloat16)


def skew_rows(matrix, keep):
    leading = matrix.shape[:-2]
    height = matrix.shape[-2]
    width = matrix.shape[-1]
    flat = matrix.reshape(leading + (height * width,))
    flat = jnp.pad(flat, [(0, 0)] * len(leading) + [(0, height)])
    return flat.reshape(leading + (height, width + 1))[..., :keep]


def pair_weights(quality_ext, reach_own, band):
    channel_count = reach_own.shape[0]
    ext_len = quality_ext.shape[0]
    partner = skew_rows(jnp.broadcast_to(quality_ext[None, :], (channel_count, ext_len)), band)
    offsets = jnp.arange(band, dtype=jnp.int32)[None, :]
    inside = (offsets < reach_own[:, None]).astype(jnp.int32)
    weight = quality_ext[:channel_count, None] * partner * inside
    total = jnp.sum(weight.astype(jnp.float32), axis=0)
    return (weight.astype(jnp.bfloat16), jnp.maximum(total, 1.0))


def cross_item(item, weight, band):
    bin_count, two_parts, seg_count, ext_len = item.shape
    channel_count = weight.shape[0]
    right = item.reshape(bin_count, two_parts * seg_count, ext_len)
    own = right[:, :, :channel_count]
    swapped = jnp.concatenate([own[:, seg_count:], -own[:, :seg_count]], axis=1)
    left = jnp.stack([own, swapped], axis=1)
    block_count = channel_count // row_block
    left = left.reshape(bin_count, 2, 2 * seg_count, block_count, row_block)
    windows = jnp.stack(
        [
            right[:, :, row_block * block_index : row_block * block_index + row_block + band]
            for block_index in range(block_count)
        ],
        axis=2,
    )
    product = jnp.einsum(
        "kgqjr,kqjw->kgjrw", left, windows, preferred_element_type=jnp.float32
    ).astype(jnp.bfloat16)
    diagonal = skew_rows(product, band).reshape(bin_count, 2, channel_count, band)
    return jnp.einsum("kgio,io->kgo", diagonal, weight, preferred_element_type=jnp.float32)


def cross_total(extended, weight, band):
    items = jnp.moveaxis(extended, 1, 0)
    summed = lax.map(lambda item: cross_item(item, weight, band), items, batch_size=item_batch)
    return summed.transpose(2, 1, 0, 3)


def on_device(strain, quality, offset_reach):
    channel_count = strain.shape[0]
    hop_count = (BAND - 2) // channel_count + 1
    near_count = (hop_count + 1) // 2
    padded = extended_2(strain, (("freq", 1),), 2 * TBLK)
    whitened = whiten(padded, TBLK)
    spectrum = spectra(whitened)[:, :, :, None, :]
    block_index = lax.axis_index("chan")
    quality_pad = jnp.concatenate([quality, jnp.zeros((channel_count * hop_count,), jnp.int32)])

    def weights_from(first_block):
        begin = jnp.maximum(first_block, 0) * channel_count
        quality_ext = lax.dynamic_slice_in_dim(
            quality_pad, begin, channel_count * (hop_count + 1), 0
        )
        reach_own = lax.dynamic_slice_in_dim(offset_reach, begin, channel_count, 0)
        return pair_weights(quality_ext, reach_own, BAND)

    weight, count = weights_from(block_index)
    local_rows = jnp.arange(channel_count, dtype=jnp.int32)[:, None]
    offsets = jnp.arange(BAND, dtype=jnp.int32)[None, :]
    far_weights = []
    for step_index in range(near_count, hop_count):
        hop = step_index + 1
        lent_weight, unused = weights_from(block_index - hop)
        in_block = (local_rows + offsets) // channel_count == hop
        far_weights.append(jnp.where(in_block, lent_weight, jnp.zeros_like(lent_weight)))
    received = lax.all_to_all(spectrum, "freq", split_axis=0, concat_axis=3, tiled=True)
    pieces = [received]
    for step_index in range(hop_count):
        pieces.append(shifted(received, "chan", -(step_index + 1)))
    total = cross_total(jnp.concatenate(pieces, axis=4), weight, BAND)
    stacked = total / count[None, None, None, :]
    bin_count = stacked.shape[1] * stacked.shape[2]
    return stacked.reshape(1, 2, bin_count, BAND)


def solution(mesh):
    return jax.shard_map(
        on_device,
        mesh=mesh,
        in_specs=(P("chan", "freq"), P(), P()),
        out_specs=P("chan", None, "freq", None),
        check_vma=False,
    )
```

profile of v0, /device:TPU:9, one launch (start us, length us, event | category | flops | bytes accessed | tf_op | source)
XLA Modules:
  0.0 1206.1 jit_solution(11523326411900194915)
XLA Ops:
  24.4 14.3 %all_to_all.18 = bf16[4,2,61440]{2,1,0:T(2,128)(2,1)S(1)} all-to-all(bf16[4,2,61440]{2,1,0:T(2,128)(2,1)S(1)} %reshape.265), channel_id=1, replica_groups=mesh['chan'=8,'freq'=4] {'freq'}, dimensions={0} | all-to-all | bytes 1966080 | tf_op jit(solution)/shard_map/all_to_all | solution.py:196
  55.4 31.8 %collective-permute-done.5 = bf16[16,60,2,4,64]{4,0,3,2,1:T(8,128)(2,1)} collective-permute-done((bf16[16,60,2,4,64]{4,0,3,2,1:T(8,128)(2,1)S(1)}, bf16[16,60,2,4,64]{4,0,3,2,1:T(8,128)(2,1)}, u32[]{:S(2)}, u32[]{:S(2)}) %collective-permute-start.5) | collective-permute-done | bytes 983072 | tf_op jit(solution)/shard_map/ppermute | solution.py:39
  87.2 49.8 %collective-permute-done.4 = bf16[16,60,2,4,64]{4,0,3,2,1:T(8,128)(2,1)} collective-permute-done((bf16[16,60,2,4,64]{4,0,3,2,1:T(8,128)(2,1)S(1)}, bf16[16,60,2,4,64]{4,0,3,2,1:T(8,128)(2,1)}, u32[]{:S(2)}, u32[]{:S(2)}) %collective-permute-start.4) | collective-permute-done | bytes 983072 | tf_op jit(solution)/shard_map/ppermute | solution.py:39
  137.0 99.5 %collective-permute-done.3 = bf16[16,60,2,4,64]{4,0,3,2,1:T(8,128)(2,1)} collective-permute-done((bf16[16,60,2,4,64]{4,0,3,2,1:T(8,128)(2,1)S(1)}, bf16[16,60,2,4,64]{4,0,3,2,1:T(8,128)(2,1)}, u32[]{:S(2)}, u32[]{:S(2)}) %collective-permute-start.3) | collective-permute-done | bytes 983072 | tf_op jit(solution)/shard_map/ppermute | solution.py:39
  236.5 21.9 %collective-permute-done.2 = bf16[16,60,2,4,64]{4,0,3,2,1:T(8,128)(2,1)} collective-permute-done((bf16[16,60,2,4,64]{4,0,3,2,1:T(8,128)(2,1)S(1)}, bf16[16,60,2,4,64]{4,0,3,2,1:T(8,128)(2,1)}, u32[]{:S(2)}, u32[]{:S(2)}) %collective-permute-start.2) | collective-permute-done | bytes 983072 | tf_op jit(solution)/shard_map/ppermute | solution.py:39
  258.4 12.1 %concatenate.25 = bf16[16,60,2,4,320]{4,0,3,2,1:T(8,128)(2,1)} concatenate(bf16[16,60,2,4,64]{4,0,3,2,1:T(8,128)(2,1)S(1)} %bitcast.124, bf16[16,60,2,4,64]{4,0,3,2,1:T(8,128)(2,1)} %collective-permute-done.2, bf16[16,60,2,4,64]{4,0,3,2,1:T(8,128)(2,1)} %collective-permute-done.3, bf16[16,60,2,4,64]{4,0,3,2,1:T(8,128)(2,1)} %collective-permute-done.4, ...), dimensions={4} | concatenate | bytes 9830400 | tf_op jit(solution)/shard_map/concatenate | solution.py:200
  270.5 930.9 %while.12 = (s32[]{:T(128)}, f32[15,4,16,2,256]{4,2,3,1,0:T(8,128)}, bf16[15,4,16,2,4,320]{5,2,4,3,1,0:T(8,128)(2,1)}, bf16[64,256]{1,0:T(8,128)(2,1)S(1)}, s32[]{:T(128)}, /*index=5*/bf16[]{:T(256)}) while((s32[]{:T(128)}, f32[15,4,16,2,256]{4,2,3,1,0:T(8,128)}, bf16[15,4,16,2,4,320]{5,2,4,3,1,0:T(8,128)(2,1)}, ...), condition=%wide.region_1.3_spmd, body=%wide.region_0.2_spmd.sunk | while | flops 47972352 | bytes 64634988 | solution.py:165
  277.2 15.0 %reshape.271 = bf16[4,16,2,2,9216]{4,2,3,1,0:T(2,128)(2,1)} reshape(bf16[4,16,2,2,32,288]{5,4,2,3,1,0:T(8,128)(2,1)} %convert_bitcast_fusion.2) | data formatting | bytes 9437184 | tf_op jit(solution)/shard_map/while/body/eval_jaxpr/vmap()/reshape | solution.py:124
  292.2 8.3 copy.133
  300.5 8.1 pad.10.clone.2
  308.6 19.3 %reshape.272 = bf16[4,16,2,2,32,289]{5,4,3,2,1,0:T(8,128)(2,1)} reshape(bf16[4,16,2,2,9248]{4,3,2,1,0:T(2,128)(2,1)} %pad.10.clone.2) | data formatting | bytes 9469952 | tf_op jit(solution)/shard_map/while/body/eval_jaxpr/vmap()/reshape | solution.py:126
  339.3 15.0 %reshape.271 = bf16[4,16,2,2,9216]{4,2,3,1,0:T(2,128)(2,1)} reshape(bf16[4,16,2,2,32,288]{5,4,2,3,1,0:T(8,128)(2,1)} %convert_bitcast_fusion.2) | data formatting | bytes 9437184 | tf_op jit(solution)/shard_map/while/body/eval_jaxpr/vmap()/reshape | solution.py:124
  354.3 8.3 copy.133
  362.6 8.1 pad.10.clone.2
  370.7 19.3 %reshape.272 = bf16[4,16,2,2,32,289]{5,4,3,2,1,0:T(8,128)(2,1)} reshape(bf16[4,16,2,2,9248]{4,3,2,1,0:T(2,128)(2,1)} %pad.10.clone.2) | data formatting | bytes 9469952 | tf_op jit(solution)/shard_map/while/body/eval_jaxpr/vmap()/reshape | solution.py:126
  401.4 15.0 %reshape.271 = bf16[4,16,2,2,9216]{4,2,3,1,0:T(2,128)(2,1)} reshape(bf16[4,16,2,2,32,288]{5,4,2,3,1,0:T(8,128)(2,1)} %convert_bitcast_fusion.2) | data formatting | bytes 9437184 | tf_op jit(solution)/shard_map/while/body/eval_jaxpr/vmap()/reshape | solution.py:124
  416.3 8.3 copy.133
  424.6 8.1 pad.10.clone.2
  432.7 19.3 %reshape.272 = bf16[4,16,2,2,32,289]{5,4,3,2,1,0:T(8,128)(2,1)} reshape(bf16[4,16,2,2,9248]{4,3,2,1,0:T(2,128)(2,1)} %pad.10.clone.2) | data formatting | bytes 9469952 | tf_op jit(solution)/shard_map/while/body/eval_jaxpr/vmap()/reshape | solution.py:126
  463.4 15.0 %reshape.271 = bf16[4,16,2,2,9216]{4,2,3,1,0:T(2,128)(2,1)} reshape(bf16[4,16,2,2,32,288]{5,4,2,3,1,0:T(8,128)(2,1)} %convert_bitcast_fusion.2) | data formatting | bytes 9437184 | tf_op jit(solution)/shard_map/while/body/eval_jaxpr/vmap()/reshape | solution.py:124
  478.4 8.3 copy.133
  486.7 8.1 pad.10.clone.2
  494.8 19.3 %reshape.272 = bf16[4,16,2,2,32,289]{5,4,3,2,1,0:T(8,128)(2,1)} reshape(bf16[4,16,2,2,9248]{4,3,2,1,0:T(2,128)(2,1)} %pad.10.clone.2) | data formatting | bytes 9469952 | tf_op jit(solution)/shard_map/while/body/eval_jaxpr/vmap()/reshape | solution.py:126
  525.5 15.0 %reshape.271 = bf16[4,16,2,2,9216]{4,2,3,1,0:T(2,128)(2,1)} reshape(bf16[4,16,2,2,32,288]{5,4,2,3,1,0:T(8,128)(2,1)} %convert_bitcast_fusion.2) | data formatting | bytes 9437184 | tf_op jit(solution)/shard_map/while/body/eval_jaxpr/vmap()/reshape | solution.py:124
  540.5 8.3 copy.133
  548.7 8.1 pad.10.clone.2
  556.8 19.3 %reshape.272 = bf16[4,16,2,2,32,289]{5,4,3,2,1,0:T(8,128)(2,1)} reshape(bf16[4,16,2,2,9248]{4,3,2,1,0:T(2,128)(2,1)} %pad.10.clone.2) | data formatting | bytes 9469952 | tf_op jit(solution)/shard_map/while/body/eval_jaxpr/vmap()/reshape | solution.py:126
  587.5 15.0 %reshape.271 = bf16[4,16,2,2,9216]{4,2,3,1,0:T(2,128)(2,1)} reshape(bf16[4,16,2,2,32,288]{5,4,2,3,1,0:T(8,128)(2,1)} %convert_bitcast_fusion.2) | data formatting | bytes 9437184 | tf_op jit(solution)/shard_map/while/body/eval_jaxpr/vmap()/reshape | solution.py:124
  602.5 8.3 copy.133
  610.8 8.1 pad.10.clone.2
  618.9 19.3 %reshape.272 = bf16[4,16,2,2,32,289]{5,4,3,2,1,0:T(8,128)(2,1)} reshape(bf16[4,16,2,2,9248]{4,3,2,1,0:T(2,128)(2,1)} %pad.10.clone.2) | data formatting | bytes 9469952 | tf_op jit(solution)/shard_map/while/body/eval_jaxpr/vmap()/reshape | solution.py:126
  649.6 15.0 %reshape.271 = bf16[4,16,2,2,9216]{4,2,3,1,0:T(2,128)(2,1)} reshape(bf16[4,16,2,2,32,288]{5,4,2,3,1,0:T(8,128)(2,1)} %convert_bitcast_fusion.2) | data formatting | bytes 9437184 | tf_op jit(solution)/shard_map/while/body/eval_jaxpr/vmap()/reshape | solution.py:124
  664.6 8.3 copy.133
  672.9 8.1 pad.10.clone.2
  681.0 19.3 %reshape.272 = bf16[4,16,2,2,32,289]{5,4,3,2,1,0:T(8,128)(2,1)} reshape(bf16[4,16,2,2,9248]{4,3,2,1,0:T(2,128)(2,1)} %pad.10.clone.2) | data formatting | bytes 9469952 | tf_op jit(solution)/shard_map/while/body/eval_jaxpr/vmap()/reshape | solution.py:126
  711.6 15.0 %reshape.271 = bf16[4,16,2,2,9216]{4,2,3,1,0:T(2,128)(2,1)} reshape(bf16[4,16,2,2,32,288]{5,4,2,3,1,0:T(8,128)(2,1)} %convert_bitcast_fusion.2) | data formatting | bytes 9437184 | tf_op jit(solution)/shard_map/while/body/eval_jaxpr/vmap()/reshape | solution.py:124
  726.6 8.3 copy.133
  734.9 8.1 pad.10.clone.2
  743.0 19.3 %reshape.272 = bf16[4,16,2,2,32,289]{5,4,3,2,1,0:T(8,128)(2,1)} reshape(bf16[4,16,2,2,9248]{4,3,2,1,0:T(2,128)(2,1)} %pad.10.clone.2) | data formatting | bytes 9469952 | tf_op jit(solution)/shard_map/while/body/eval_jaxpr/vmap()/reshape | solution.py:126
  773.7 15.0 %reshape.271 = bf16[4,16,2,2,9216]{4,2,3,1,0:T(2,128)(2,1)} reshape(bf16[4,16,2,2,32,288]{5,4,2,3,1,0:T(8,128)(2,1)} %convert_bitcast_fusion.2) | data formatting | bytes 9437184 | tf_op jit(solution)/shard_map/while/body/eval_jaxpr/vmap()/reshape | solution.py:124
  788.7 8.3 copy.133
  797.0 8.1 pad.10.clone.2
  805.1 19.3 %reshape.272 = bf16[4,16,2,2,32,289]{5,4,3,2,1,0:T(8,128)(2,1)} reshape(bf16[4,16,2,2,9248]{4,3,2,1,0:T(2,128)(2,1)} %pad.10.clone.2) | data formatting | bytes 9469952 | tf_op jit(solution)/shard_map/while/body/eval_jaxpr/vmap()/reshape | solution.py:126
  835.8 15.0 %reshape.271 = bf16[4,16,2,2,9216]{4,2,3,1,0:T(2,128)(2,1)} reshape(bf16[4,16,2,2,32,288]{5,4,2,3,1,0:T(8,128)(2,1)} %convert_bitcast_fusion.2) | data formatting | bytes 9437184 | tf_op jit(solution)/shard_map/while/body/eval_jaxpr/vmap()/reshape | solution.py:124
  850.8 8.3 copy.133
  859.0 8.1 pad.10.clone.2
  867.1 19.3 %reshape.272 = bf16[4,16,2,2,32,289]{5,4,3,2,1,0:T(8,128)(2,1)} reshape(bf16[4,16,2,2,9248]{4,3,2,1,0:T(2,128)(2,1)} %pad.10.clone.2) | data formatting | bytes 9469952 | tf_op jit(solution)/shard_map/while/body/eval_jaxpr/vmap()/reshape | solution.py:126
  897.8 15.0 %reshape.271 = bf16[4,16,2,2,9216]{4,2,3,1,0:T(2,128)(2,1)} reshape(bf16[4,16,2,2,32,288]{5,4,2,3,1,0:T(8,128)(2,1)} %convert_bitcast_fusion.2) | data formatting | bytes 9437184 | tf_op jit(solution)/shard_map/while/body/eval_jaxpr/vmap()/reshape | solution.py:124
  912.8 8.3 copy.133
  921.1 8.1 pad.10.clone.2
  929.2 19.3 %reshape.272 = bf16[4,16,2,2,32,289]{5,4,3,2,1,0:T(8,128)(2,1)} reshape(bf16[4,16,2,2,9248]{4,3,2,1,0:T(2,128)(2,1)} %pad.10.clone.2) | data formatting | bytes 9469952 | tf_op jit(solution)/shard_map/while/body/eval_jaxpr/vmap()/reshape | solution.py:126
  959.9 15.0 %reshape.271 = bf16[4,16,2,2,9216]{4,2,3,1,0:T(2,128)(2,1)} reshape(bf16[4,16,2,2,32,288]{5,4,2,3,1,0:T(8,128)(2,1)} %convert_bitcast_fusion.2) | data formatting | bytes 9437184 | tf_op jit(solution)/shard_map/while/body/eval_jaxpr/vmap()/reshape | solution.py:124
  974.9 8.3 copy.133
  983.2 8.1 pad.10.clone.2
  991.3 19.3 %reshape.272 = bf16[4,16,2,2,32,289]{5,4,3,2,1,0:T(8,128)(2,1)} reshape(bf16[4,16,2,2,9248]{4,3,2,1,0:T(2,128)(2,1)} %pad.10.clone.2) | data formatting | bytes 9469952 | tf_op jit(solution)/shard_map/while/body/eval_jaxpr/vmap()/reshape | solution.py:126
  1021.9 15.0 %reshape.271 = bf16[4,16,2,2,9216]{4,2,3,1,0:T(2,128)(2,1)} reshape(bf16[4,16,2,2,32,288]{5,4,2,3,1,0:T(8,128)(2,1)} %convert_bitcast_fusion.2) | data formatting | bytes 9437184 | tf_op jit(solution)/shard_map/while/body/eval_jaxpr/vmap()/reshape | solution.py:124
  1036.9 8.3 copy.133
  1053.3 19.3 %reshape.272 = bf16[4,16,2,2,32,289]{5,4,3,2,1,0:T(8,128)(2,1)} reshape(bf16[4,16,2,2,9248]{4,3,2,1,0:T(2,128)(2,1)} %pad.10.clone.2) | data formatting | bytes 9469952 | tf_op jit(solution)/shard_map/while/body/eval_jaxpr/vmap()/reshape | solution.py:126
  1084.0 15.0 %reshape.271 = bf16[4,16,2,2,9216]{4,2,3,1,0:T(2,128)(2,1)} reshape(bf16[4,16,2,2,32,288]{5,4,2,3,1,0:T(8,128)(2,1)} %convert_bitcast_fusion.2) | data formatting | bytes 9437184 | tf_op jit(solution)/shard_map/while/body/eval_jaxpr/vmap()/reshape | solution.py:124
  1099.0 8.3 copy.133
  1115.4 19.3 %reshape.272 = bf16[4,16,2,2,32,289]{5,4,3,2,1,0:T(8,128)(2,1)} reshape(bf16[4,16,2,2,9248]{4,3,2,1,0:T(2,128)(2,1)} %pad.10.clone.2) | data formatting | bytes 9469952 | tf_op jit(solution)/shard_map/while/body/eval_jaxpr/vmap()/reshape | solution.py:126
  1146.1 15.0 %reshape.271 = bf16[4,16,2,2,9216]{4,2,3,1,0:T(2,128)(2,1)} reshape(bf16[4,16,2,2,32,288]{5,4,2,3,1,0:T(8,128)(2,1)} %convert_bitcast_fusion.2) | data formatting | bytes 9437184 | tf_op jit(solution)/shard_map/while/body/eval_jaxpr/vmap()/reshape | solution.py:124
  1161.0 8.3 copy.133
  1177.4 19.3 %reshape.272 = bf16[4,16,2,2,32,289]{5,4,3,2,1,0:T(8,128)(2,1)} reshape(bf16[4,16,2,2,9248]{4,3,2,1,0:T(2,128)(2,1)} %pad.10.clone.2) | data formatting | bytes 9469952 | tf_op jit(solution)/shard_map/while/body/eval_jaxpr/vmap()/reshape | solution.py:126
  (319 shorter events, 239.6 us)
Async XLA Ops:
  0.8 5.0 collective-permute-start
  3.9 4.7 collective-permute-start.1
  41.3 12.7 %copy-start = (s32[512]{0:T(512)S(1)}, s32[512]{0:T(512)}, u32[]{:S(2)}) copy-start(s32[512]{0:T(512)} %param.7) | copy-start | bytes 6148
  43.4 43.8 %collective-permute-start.5 = (bf16[16,60,2,4,64]{4,0,3,2,1:T(8,128)(2,1)S(1)}, bf16[16,60,2,4,64]{4,0,3,2,1:T(8,128)(2,1)}, u32[]{:S(2)}, u32[]{:S(2)}) collective-permute-start(bf16[16,60,2,4,64]{4,0,3,2,1:T(8,128)(2,1)S(1)} %bitcast.120), channel_id=1, source_target_pairs={{16,0},{20,4},{24,8},{28,12},{17,1},{21,5},{25,9},{29,13},{18,2},{... | collective-permute-start | bytes 2949128 | tf_op jit(solution)/shard_map/ppermute | solution.py:39
  44.7 92.3 %collective-permute-start.4 = (bf16[16,60,2,4,64]{4,0,3,2,1:T(8,128)(2,1)S(1)}, bf16[16,60,2,4,64]{4,0,3,2,1:T(8,128)(2,1)}, u32[]{:S(2)}, u32[]{:S(2)}) collective-permute-start(bf16[16,60,2,4,64]{4,0,3,2,1:T(8,128)(2,1)S(1)} %bitcast.121), channel_id=1, source_target_pairs={{12,0},{16,4},{20,8},{24,12},{28,16},{13,1},{17,5},{21,9},{25,13},... | collective-permute-start | bytes 2949128 | tf_op jit(solution)/shard_map/ppermute | solution.py:39
  50.2 186.3 %collective-permute-start.3 = (bf16[16,60,2,4,64]{4,0,3,2,1:T(8,128)(2,1)S(1)}, bf16[16,60,2,4,64]{4,0,3,2,1:T(8,128)(2,1)}, u32[]{:S(2)}, u32[]{:S(2)}) collective-permute-start(bf16[16,60,2,4,64]{4,0,3,2,1:T(8,128)(2,1)S(1)} %bitcast.122), channel_id=1, source_target_pairs={{8,0},{12,4},{16,8},{20,12},{24,16},{28,20},{9,1},{13,5},{17,9},{2... | collective-permute-start | bytes 2949128 | tf_op jit(solution)/shard_map/ppermute | solution.py:39
  52.1 206.3 %collective-permute-start.2 = (bf16[16,60,2,4,64]{4,0,3,2,1:T(8,128)(2,1)S(1)}, bf16[16,60,2,4,64]{4,0,3,2,1:T(8,128)(2,1)}, u32[]{:S(2)}, u32[]{:S(2)}) collective-permute-start(bf16[16,60,2,4,64]{4,0,3,2,1:T(8,128)(2,1)S(1)} %bitcast.123), channel_id=1, source_target_pairs={{4,0},{8,4},{12,8},{16,12},{20,16},{24,20},{28,24},{5,1},{9,5},{13... | collective-permute-start | bytes 2949128 | tf_op jit(solution)/shard_map/ppermute | solution.py:39
  327.9 2.2 slice-start
  389.9 2.2 slice-start
  452.0 2.2 slice-start
  514.1 2.2 slice-start
  576.1 2.2 slice-start
  638.2 2.2 slice-start
  700.2 2.2 slice-start
  762.3 2.2 slice-start
  824.4 2.2 slice-start
  886.4 2.2 slice-start
  948.5 2.2 slice-start
  1010.5 2.2 slice-start
  1072.6 2.2 slice-start
  1134.6 2.2 slice-start
  1196.7 2.2 slice-start
where the time goes:
time: 1210 us
  local copies, waits for them, and re-layouts  858 us (71%)
  waiting for transfers between devices  206 us (17%)
  matrix products  77.3 us (6%)
  other arithmetic  33.7 us (3%)
  starting transfers between devices  15 us (1%)
  blocking collectives  14.3 us (1%)
    reshape x16, local copies, waits for them, and re-layouts, skew_rows(): return flat.reshape(leading + (height, width + 1))[..., :keep]  289 us
    reshape x16, local copies, waits for them, and re-layouts, skew_rows(): flat = matrix.reshape(leading + (height * width,))  225 us
    ppermute x4, waiting for transfers between devices, shifted(): return lax.ppermute(x, axis, pairs)  203 us
    while x30, local copies, waits for them, and re-layouts  125 us
    pad x16, local copies, waits for them, and re-layouts, skew_rows(): flat = jnp.pad(flat, [(0, 0)] * len(leading) + [(0, height)])  121 us
    dot_general x15, matrix products, cross_item(): jnp.einsum('kgqjr,kqjw->kgjrw', left, windows, preferred_element_type=jnp...  68.3 us
    slice x30, local copies, waits for them, and re-layouts, skew_rows(): return flat.reshape(leading + (height, width + 1))[..., :keep]  32.8 us
    dot_general x15, other arithmetic, cross_item(): jnp.einsum('kgio,io->kgo', diagonal, weight, preferred_element_type=jnp.f...  27.1 us
  transfers between devices with their start and end apart: 6, of which 5 were waited for; matrix products, arithmetic and copies ran while one was open for 0% of the time, Pallas kernels for 0%

commit v1 on v0

v1 whole, which is shorter than its diff:
```python
import functools
import math

import jax
import jax.numpy as jnp
import ml_dtypes
import numpy as np
from jax import lax
from jax.experimental import pallas as pl
from jax.experimental.pallas import tpu as pltpu
from jax.sharding import PartitionSpec as P

BAND = 256
TBLK = 128

band_low = 0.004
band_high = 0.48
level_eps = 1e-05
MIB = 1 << 20


def tap_values(offset, half_span):
    window = 0.5 + 0.5 * np.cos(np.pi * offset / (half_span + 1))
    response = 2.0 * band_high * np.sinc(2.0 * band_high * offset) - 2.0 * band_low * np.sinc(
        2.0 * band_low * offset
    )
    return np.where(np.abs(offset) <= half_span, window * response, 0.0)


def stencil_table(boxed):
    offset = np.arange(2 * TBLK)[None, :] + TBLK - np.arange(4 * TBLK)[:, None]
    if boxed:
        values = np.where(np.abs(offset) <= TBLK, 1.0, 0.0)
    else:
        values = tap_values(offset.astype(np.float64), TBLK)
    return values.astype(ml_dtypes.bfloat16)


def dft_tables(count_a, n_freq):
    pad_a = -(-count_a // 16) * 16
    length = count_a * TBLK
    index = np.arange(count_a)
    angle = (index[:, None] * index[None, :] % count_a) * (2.0 * np.pi / count_a)
    first = np.zeros((2, pad_a, pad_a))
    first[0, :count_a, :count_a] = np.cos(angle)
    first[1, :count_a, :count_a] = -np.sin(angle)
    first = first.reshape(2 * pad_a, pad_a).astype(ml_dtypes.bfloat16)
    twist = np.zeros((2, pad_a, TBLK), np.float32)
    turn = (index[:, None] * np.arange(TBLK)[None, :] % length) * (2.0 * np.pi / length)
    twist[0, :count_a] = np.cos(turn)
    twist[1, :count_a] = np.sin(turn)
    k2_count = TBLK // 2
    turn = (np.arange(k2_count)[:, None] * np.arange(TBLK)[None, :] % TBLK) * (2.0 * np.pi / TBLK)
    real = np.concatenate([np.cos(turn), np.sin(turn)], axis=1)
    imag = np.concatenate([-np.sin(turn), np.cos(turn)], axis=1)
    half = k2_count // n_freq // 2
    second = np.stack([real, imag]).reshape(2, n_freq, 2, half, 2 * TBLK)
    second = second.transpose(1, 2, 0, 3, 4).reshape(n_freq, 2, 2 * half, 2 * TBLK)
    return first, twist, second.astype(ml_dtypes.bfloat16)


def spectra_kernel(
    count_a,
    n_freq,
    meta,
    own,
    other,
    lo_own,
    lo_other,
    hi_own,
    hi_other,
    taps,
    box,
    first,
    twist,
    second,
    quality,
    *rest,
):
    outs = rest[:n_freq]
    padded, filtered, magnitude, whitened, tw_re, tw_im = rest[n_freq:]
    core, band = meta[0], meta[1]
    ch = own.shape[0]
    both = 2 * ch
    pad_a = first.shape[1]
    dot = functools.partial(jnp.dot, preferred_element_type=jnp.float32)

    for which, (lo, mid, hi) in enumerate(((lo_own, own, hi_own), (lo_other, other, hi_other))):
        base = core if which == 0 else 1 - core
        rows = pl.ds(pl.multiple_of(base * ch, ch), ch)
        for j in range(2):
            padded[j, rows, :] = lo[:, j * TBLK : (j + 1) * TBLK]
            padded[count_a + 2 + j, rows, :] = hi[:, j * TBLK : (j + 1) * TBLK]
        for j in range(count_a):
            padded[2 + j, rows, :] = mid[:, j * TBLK : (j + 1) * TBLK]

    def fir(i, carry):
        j = 2 * i
        window = jnp.concatenate([padded[j + n] for n in range(4)], axis=1)
        result = dot(window, taps[...])
        for n in range(2):
            part = result[:, n * TBLK : (n + 1) * TBLK]
            filtered[j + n] = part
            magnitude[j + n] = jnp.abs(part).astype(jnp.bfloat16)
        return carry

    lax.fori_loop(0, count_a // 2 + 1, fir, 0)

    def whiten(i, carry):
        j = 2 * i
        window = jnp.concatenate([magnitude[j + n] for n in range(4)], axis=1)
        level = dot(window, box[...]) / (2 * TBLK + 1)
        for n in range(2):
            part = filtered[j + n + 1] / (level[:, n * TBLK : (n + 1) * TBLK] + level_eps)
            rows = pl.ds(pl.multiple_of((j + n) * both, both), both)
            whitened[rows, :] = part
        return carry

    lax.fori_loop(0, count_a // 2, whiten, 0)
    whitened[count_a * both : pad_a * both, :] = jnp.zeros(
        ((pad_a - count_a) * both, TBLK), jnp.float32
    )

    def sections(i, carry):
        c = 2 * i
        pair = [
            whitened[pl.ds(c + n, pad_a, stride=both), :].astype(jnp.bfloat16) for n in range(2)
        ]
        section = dot(first[...], jnp.concatenate(pair, axis=1))
        for n in range(2):
            re = section[:pad_a, n * TBLK : (n + 1) * TBLK]
            im = section[pad_a:, n * TBLK : (n + 1) * TBLK]
            rows = pl.ds(pl.multiple_of((c + n) * pad_a, pad_a), pad_a)
            tw_re[rows, :] = re * twist[0] + im * twist[1]
            tw_im[rows, :] = im * twist[0] - re * twist[1]
        return carry

    lax.fori_loop(0, both // 2, sections, 0)

    rk = second.shape[2]
    group = max(1, 16 // rk)
    scale = quality[...] * (1.0 / math.sqrt(count_a * TBLK))
    turn = jnp.concatenate([second[band ^ d, core] for d in range(n_freq)], axis=0)

    def bins(i, carry):
        results = []
        for n in range(group):
            k1 = i * group + n
            re = tw_re[pl.ds(k1, both, stride=pad_a), :].astype(jnp.bfloat16)
            im = tw_im[pl.ds(k1, both, stride=pad_a), :].astype(jnp.bfloat16)
            result = lax.dot_general(
                turn,
                jnp.concatenate([re, im], axis=1),
                (((1,), (1,)), ((), ())),
                preferred_element_type=jnp.float32,
            )
            results.append(result * scale)
        rows = pl.ds(pl.multiple_of(i * group * rk, 16), group * rk)
        for d in range(n_freq):
            parts = [r[d * rk : (d + 1) * rk] for r in results]
            block = parts[0] if group == 1 else jnp.concatenate(parts, axis=0)
            outs[d][rows, :] = block.astype(jnp.bfloat16)
        return carry

    lax.fori_loop(0, count_a // group, bins, 0)


def spectra(meta, own, other, halos, quality, n_freq):
    ch, length = own.shape
    count_a = length // TBLK
    first, twist, second = dft_tables(count_a, n_freq)
    rk = second.shape[2]
    pad_a = first.shape[1]
    both = 2 * ch
    vmem = pl.BlockSpec(memory_space=pltpu.VMEM)
    return pl.pallas_call(
        functools.partial(spectra_kernel, count_a, n_freq),
        out_shape=[jax.ShapeDtypeStruct((count_a * rk, both), jnp.bfloat16)] * n_freq,
        in_specs=[pl.BlockSpec(memory_space=pltpu.SMEM)] + [vmem] * 12,
        out_specs=[vmem] * n_freq,
        scratch_shapes=[
            pltpu.VMEM((count_a + 4, both, TBLK), jnp.bfloat16),
            pltpu.VMEM((count_a + 2, both, TBLK), jnp.float32),
            pltpu.VMEM((count_a + 2, both, TBLK), jnp.bfloat16),
            pltpu.VMEM((pad_a * both, TBLK), jnp.float32),
            pltpu.VMEM((both * pad_a, TBLK), jnp.float32),
            pltpu.VMEM((both * pad_a, TBLK), jnp.float32),
        ],
        compiler_params=pltpu.CompilerParams(vmem_limit_bytes=48 * MIB),
        cost_estimate=pl.CostEstimate(
            flops=6 * 10**9, bytes_accessed=4 * 10**6, transcendentals=0
        ),
        name="spectra",
    )(
        meta,
        own,
        other,
        *halos,
        jnp.asarray(stencil_table(False)),
        jnp.asarray(stencil_table(True)),
        jnp.asarray(first),
        jnp.asarray(twist),
        jnp.asarray(second),
        quality,
    )


def cross_kernel(n_seg, rk, count_a, reach_own, reach_prev, *rest):
    turn_ref, pick_ref = rest[0], rest[1]
    own_refs = rest[2 : 2 + n_seg]
    prev_refs = rest[2 + n_seg : 2 + 2 * n_seg]
    next_refs = rest[2 + 2 * n_seg : 2 + 3 * n_seg]
    near_ref, far_ref, w_near, w_far, sums = rest[2 + 3 * n_seg :]
    step = pl.program_id(0)
    both = own_refs[0].shape[1]
    depth = turn_ref.shape[0]
    half = rk // 2
    nb = pick_ref.shape[0]
    nk1 = nb // half
    slabs = both // 8
    per_group = slabs // 2

    @pl.when(step == 0)
    def _():
        row = lax.broadcasted_iota(jnp.int32, (both, both), 0)
        col = lax.broadcasted_iota(jnp.int32, (both, both), 1)
        near = (col >= row) & (both + col - row < reach_own[...])
        far = (col < row) & (2 * both + col - row < reach_prev[...])
        w_near[...] = jnp.where(near, 1.0, 0.0)
        w_far[...] = jnp.where(far, 1.0, 0.0)

    def stacked(refs):
        return jnp.concatenate([r[...] for r in refs], axis=0)

    def left_rows(block):
        re = block.astype(jnp.float32).T.astype(jnp.bfloat16)
        im = jnp.dot(re, turn_ref[...], preferred_element_type=jnp.float32)
        re = re.astype(jnp.float32).reshape(slabs, 8, depth)
        im = im.reshape(slabs, 8, depth)
        return jnp.stack([re, im], axis=1).reshape(slabs, 16, depth).astype(jnp.bfloat16)

    own = stacked(own_refs)
    nxt = stacked(next_refs)
    right = jnp.concatenate([own, nxt], axis=1)
    left_own = left_rows(own)
    left_prev = left_rows(stacked(prev_refs))
    row = lax.broadcasted_iota(jnp.int32, (8, both), 0)
    col = lax.broadcasted_iota(jnp.int32, (8, both), 1)
    lead = col - row

    def bin_step(i, carry):
        pick = pick_ref[i][None]
        for g in range(2):
            here = slice(g * per_group, (g + 1) * per_group)
            rows = (left_own[here] * pick).reshape(per_group * 16, depth)
            near = jnp.dot(rows, right, preferred_element_type=jnp.float32)
            rows = (left_prev[here] * pick).reshape(per_group * 16, depth)
            far = jnp.dot(rows, nxt, preferred_element_type=jnp.float32)
            for p in range(2):
                acc = [None] * 3
                for n in range(per_group):
                    a = g * per_group + n
                    at = n * 16 + p * 8
                    local = near[at : at + 8, :both]
                    beyond = near[at : at + 8, both:]
                    distant = far[at : at + 8]
                    wn = w_near[a * 8 : a * 8 + 8, :]
                    wf = w_far[a * 8 : a * 8 + 8, :]
                    terms = (
                        jnp.where(lead >= 8 * a, local, beyond),
                        beyond * wn,
                        distant * wf,
                    )
                    shift = (both - 8 * a) % both
                    for r, term in enumerate(terms):
                        if shift:
                            term = pltpu.roll(term, shift, 1)
                        acc[r] = term if acc[r] is None else acc[r] + term
                for r in range(3):
                    sums[(r * 2 + g) * 2 + p, pl.ds(pl.multiple_of(i * 8, 8), 8), :] = acc[r]
        return carry

    lax.fori_loop(0, nb, bin_step, 0)

    def diagonal(r, g, p):
        total = None
        for b in range(8):
            part = sums[(r * 2 + g) * 2 + p, pl.ds(b, nb, stride=8), :]
            if b:
                part = pltpu.roll(part, both - b, 1)
            total = part if total is None else total + part
        return total

    far_parts = []
    for g in range(2):
        for p in range(2):
            for r in range(2):
                value = diagonal(r, g, p)
                for n in range(nk1):
                    near_ref[g, p, r, pl.ds(step * nk1 + n, half, stride=count_a), :] = value[
                        n * half : (n + 1) * half
                    ]
            far_parts.append(diagonal(2, g, p))
    far_ref[...] = jnp.concatenate(far_parts, axis=0).astype(jnp.bfloat16)


def cross(own, prev, nxt, reach_own, reach_prev, count_a, rk):
    n_seg = len(own)
    rows, both = own[0].shape
    half = rk // 2
    rb = 32 if n_seg <= 4 else 16
    depth = n_seg * rb
    nb = rb // 2
    steps = rows // rb
    lane = np.arange(depth)
    within = lane % rb
    part = within // half % 2
    bin_of = within // rk * half + within % half
    turn = np.zeros((depth, depth))
    turn[lane + np.where(part == 0, half, -half), lane] = np.where(part == 0, 1.0, -1.0)
    pick = (bin_of[None, None, :] == np.arange(nb)[:, None, None]).astype(np.float32)
    pick = np.broadcast_to(pick, (nb, 16, depth)).astype(ml_dtypes.bfloat16)
    whole = lambda shape: pl.BlockSpec(shape, lambda t: (0,) * len(shape))
    block = pl.BlockSpec((rb, both), lambda t: (t, 0))
    far_rows = 4 * nb
    return pl.pallas_call(
        functools.partial(cross_kernel, n_seg, rk, count_a),
        grid=(steps,),
        out_shape=[
            jax.ShapeDtypeStruct((2, 2, 2, rows // 2, both), jnp.float32),
            jax.ShapeDtypeStruct((steps * far_rows, both), jnp.bfloat16),
        ],
        in_specs=[
            whole((both, 1)),
            whole((both, 1)),
            whole(turn.shape),
            whole(pick.shape),
        ]
        + [block] * (3 * n_seg),
        out_specs=[
            whole((2, 2, 2, rows // 2, both)),
            pl.BlockSpec((far_rows, both), lambda t: (t, 0)),
        ],
        scratch_shapes=[
            pltpu.VMEM((both, both), jnp.float32),
            pltpu.VMEM((both, both), jnp.float32),
            pltpu.VMEM((12, nb * 8, both), jnp.float32),
        ],
        compiler_params=pltpu.CompilerParams(
            dimension_semantics=("arbitrary",), vmem_limit_bytes=48 * MIB
        ),
        cost_estimate=pl.CostEstimate(
            flops=30 * 10**9, bytes_accessed=6 * 10**6, transcendentals=0
        ),
        name="cross",
    )(
        reach_own,
        reach_prev,
        jnp.asarray(turn.astype(ml_dtypes.bfloat16)),
        jnp.asarray(pick),
        *own,
        *prev,
        *nxt,
    )


def finish_kernel(rk, count_a, nb, meta, mine, theirs, far_a, far_b, count, out_ref, total):
    core = meta[0]
    half = rk // 2
    nk1 = nb // half
    bins = mine.shape[2]
    inverse = 1.0 / count[...]
    both = far_a.shape[1]
    for which, (near, far) in enumerate(((mine, far_a), (theirs, far_b))):
        at = core if which == 0 else 1 - core
        rows = pl.ds(pl.multiple_of(at * bins, bins), bins)
        for p in range(2):
            total[p] = near[p, 1]

        def add(t, carry):
            for p in range(2):
                start = pl.multiple_of((t * 2 + p) * nb, nb)
                value = far[pl.ds(start, nb), :].astype(jnp.float32)
                for n in range(nk1):
                    place = pl.ds(t * nk1 + n, half, stride=count_a)
                    total[p, place, :] += value[n * half : (n + 1) * half]
            return carry

        lax.fori_loop(0, bins // nb, add, 0)
        for p in range(2):
            out_ref[p, rows, :both] = near[p, 0] * inverse[:, :both]
            out_ref[p, rows, both:] = total[p] * inverse[:, both:]


def finish(meta, mine, theirs, far_a, far_b, count, count_a, rk, nb):
    vmem = pl.BlockSpec(memory_space=pltpu.VMEM)
    bins = mine.shape[2]
    return pl.pallas_call(
        functools.partial(finish_kernel, rk, count_a, nb),
        out_shape=jax.ShapeDtypeStruct((2, 2 * bins, BAND), jnp.float32),
        in_specs=[pl.BlockSpec(memory_space=pltpu.SMEM)] + [vmem] * 5,
        out_specs=vmem,
        scratch_shapes=[pltpu.VMEM((2, bins, TBLK), jnp.float32)],
        compiler_params=pltpu.CompilerParams(vmem_limit_bytes=48 * MIB),
        name="finish",
    )(meta, mine, theirs, far_a, far_b, count)


def skew_rows(matrix, keep):
    height, width = matrix.shape
    flat = jnp.pad(matrix.reshape(height * width), (0, height))
    return flat.reshape(height, width + 1)[:, :keep]


def pair_count(quality_ext, reach_own, band):
    channel_count = reach_own.shape[0]
    ext_len = quality_ext.shape[0]
    partner = skew_rows(jnp.broadcast_to(quality_ext[None, :], (channel_count, ext_len)), band)
    offsets = jnp.arange(band, dtype=jnp.int32)[None, :]
    inside = (offsets < reach_own[:, None]).astype(jnp.int32)
    weight = quality_ext[:channel_count, None] * partner * inside
    return jnp.maximum(jnp.sum(weight.astype(jnp.float32), axis=0), 1.0)


def on_device(strain, quality, offset_reach):
    ch, length = strain.shape
    both = 2 * ch
    assert both == TBLK and BAND == 2 * both
    n_chan, n_freq = lax.axis_size("chan"), lax.axis_size("freq")
    count_a = length // TBLK
    rk = TBLK // 2 // n_freq
    me, band = lax.axis_index("chan"), lax.axis_index("freq")
    core, chip = me % 2, me // 2

    def moved(x, target):
        pairs = []
        for c in range(n_chan):
            for f in range(n_freq):
                to = target(c, f)
                if 0 <= to[0] < n_chan and 0 <= to[1] < n_freq:
                    pairs.append((c * n_freq + f, to[0] * n_freq + to[1]))
        return lax.ppermute(x, ("chan", "freq"), pairs)

    tail, head = strain[:, length - 2 * TBLK :], strain[:, : 2 * TBLK]
    other = moved(strain, lambda c, f: (c ^ 1, f))
    halos = [
        moved(tail, lambda c, f: (c, f + 1)),
        moved(tail, lambda c, f: (c ^ 1, f + 1)),
        moved(head, lambda c, f: (c, f - 1)),
        moved(head, lambda c, f: (c ^ 1, f - 1)),
    ]

    quality_pad = jnp.pad(quality, (0, BAND + both))
    reach_pad = jnp.pad(offset_reach, (both, 0))
    quality_both = lax.dynamic_slice_in_dim(quality_pad, chip * both, both, 0)
    reach_own = lax.dynamic_slice_in_dim(reach_pad, (chip + 1) * both, both, 0)[:, None]
    reach_prev = lax.dynamic_slice_in_dim(reach_pad, chip * both, both, 0)[:, None]
    quality_ext = lax.dynamic_slice_in_dim(quality_pad, me * ch, ch + BAND, 0)
    count = pair_count(quality_ext, lax.dynamic_slice_in_dim(offset_reach, me * ch, ch, 0), BAND)

    meta = jnp.stack([core, band]).astype(jnp.int32)
    parts = spectra(
        meta, strain, other, halos, quality_both.astype(jnp.float32)[None, :], n_freq
    )
    own = [parts[0]]
    for d in range(1, n_freq):
        own.append(moved(parts[d], lambda c, f, d=d: (c, f ^ d)))
    nxt = [moved(x, lambda c, f: (c - 2, f)) for x in own]
    prev = [moved(x, lambda c, f: (c + 2, f)) for x in own]
    near, far = cross(own, prev, nxt, reach_own, reach_prev, count_a, rk)
    nb = (32 if n_freq <= 4 else 16) // 2
    steps = far.shape[0] // (4 * nb)
    far = far.reshape(steps, 2, 2 * nb, both)
    pick = lambda x, axis, at: lax.dynamic_index_in_dim(x, at, axis, keepdims=False)
    theirs = moved(pick(near, 0, 1 - core), lambda c, f: (c ^ 1, f))
    far_a = moved(pick(far, 1, core).reshape(-1, both), lambda c, f: (c - 2, f))
    far_b = moved(pick(far, 1, 1 - core).reshape(-1, both), lambda c, f: ((c ^ 1) - 2, f))
    mine = pick(near, 0, core)
    out = finish(meta, mine, theirs, far_a, far_b, count[None, :], count_a, rk, nb)
    return out[None]


def solution(mesh):
    return jax.shard_map(
        on_device,
        mesh=mesh,
        in_specs=(P("chan", "freq"), P(), P()),
        out_specs=P("chan", None, "freq", None),
        check_vma=False,
    )
```

time: 1210 us -> 289 us (0.24)
  local copies, waits for them, and re-layouts: 858 us -> 11.1 us
  Pallas kernels: 0 us -> 209 us
  waiting for transfers between devices: 206 us -> 23.5 us
  matrix products: 77.3 us -> 0 us
  other arithmetic: 33.7 us -> 1.78 us
  starting transfers between devices: 15 us -> 41.3 us
  blocking collectives: 14.3 us -> 0 us
    reshape x33 -> x2, local copies, waits for them, and re-layouts: 516 us -> 1.57 us  [the longest x1 0.84 us: skew_rows(): return flat.reshape(height, width + 1)[:, :keep]]
    pallas_call x0 -> x3, Pallas kernels: none -> 209 us  [the longest x1 166 us: cross(): pl.pallas_call(functools.partial(cross_kernel, n_seg, rk, count_a), grid=...]
    ppermute x6 -> x19, waiting for transfers between devices: 206 us -> 23.5 us  [moved(): return lax.ppermute(x, ('chan', 'freq'), pairs)]
    while x30 -> x0, local copies, waits for them, and re-layouts: 125 us -> none
    pad x16 -> x1, local copies, waits for them, and re-layouts: 121 us -> 0.89 us  [skew_rows(): flat = jnp.pad(matrix.reshape(height * width), (0, height))]
    dot_general x24 -> x0, matrix products: 77.3 us -> none  [the longest x15 68.3 us: cross_item(): jnp.einsum('kgqjr,kqjw->kgjrw', left, windows, preferred_element_type=jnp...]
    slice x78 -> x2, local copies, waits for them, and re-layouts: 38.1 us -> 0.78 us  [the longest x1 0.78 us: on_device(): tail, head = (strain[:, length - 2 * TBLK:], strain[:, :2 * TBLK])]
    dot_general x15 -> x0, other arithmetic: 27.1 us -> none  [cross_item(): jnp.einsum('kgio,io->kgo', diagonal, weight, preferred_element_type=jnp.f...]
  transfers between devices with their start and end apart: 6 -> 19, of which waited for: 5 -> 6; matrix products, arithmetic and copies ran while one was open for 0% -> 2% of each run, Pallas kernels for 0% -> 0%
where the time goes in v1:
time: 289 us; the launch traced here: 287 us
  Pallas kernels  209 us (72%)
  starting transfers between devices  41.3 us (14%)
  waiting for transfers between devices  23.5 us (8%)
  local copies, waits for them, and re-layouts  11.1 us (4%)
    pallas_call x1, Pallas kernels, cross(): pl.pallas_call(functools.partial(cross_kernel, n_seg, rk, count_a), grid=...  166 us
    ppermute x19, starting transfers between devices, moved(): return lax.ppermute(x, ('chan', 'freq'), pairs)  41.3 us
    pallas_call x1, Pallas kernels, spectra(): pl.pallas_call(functools.partial(spectra_kernel, count_a, n_freq), out_sh...  40 us
    ppermute x19, waiting for transfers between devices, moved(): return lax.ppermute(x, ('chan', 'freq'), pairs)  23.5 us
    unnamed x24, local copies, waits for them, and re-layouts  7.19 us
  transfers between devices with their start and end apart: 19, of which 6 were waited for; matrix products, arithmetic and copies ran while one was open for 2% of the time, Pallas kernels for 0%

profile of v1, /device:TPU:9, one launch (start us, length us, event | category | flops | bytes accessed | tf_op | source)
XLA Modules:
  0.0 286.8 jit_solution(6631914896086096833)
XLA Ops:
  0.0 0.7 collective-permute-start
  0.7 0.8 fusion.7
  1.5 3.1 %collective-permute-start.1 = (bf16[64,256]{1,0:T(8,128)(2,1)S(1)}, bf16[64,256]{1,0:T(8,128)(2,1)S(1)}, u32[]{:S(2)}, u32[]{:S(2)}) collective-permute-start(bf16[64,256]{1,0:T(8,128)(2,1)S(1)} %get-tuple-element.20), channel_id=1, source_target_pairs={{0,1},{1,2},{2,3},{4,5},{5,6},{6,7},{8,9},{9,10},{10,11},{12,13},{... | collective-permute-start | bytes 98312 | tf_op jit(solution)/shard_map/ppermute | solution.py:442
  4.6 3.3 %collective-permute-start.2 = (bf16[64,256]{1,0:T(8,128)(2,1)S(1)}, bf16[64,256]{1,0:T(8,128)(2,1)S(1)}, u32[]{:S(2)}, u32[]{:S(2)}) collective-permute-start(bf16[64,256]{1,0:T(8,128)(2,1)S(1)} %get-tuple-element.20), channel_id=1, source_target_pairs={{0,5},{1,6},{2,7},{4,1},{5,2},{6,3},{8,13},{9,14},{10,15},{12,9},{... | collective-permute-start | bytes 98312 | tf_op jit(solution)/shard_map/ppermute | solution.py:442
  7.9 1.3 collective-permute-start.3
  9.2 1.3 collective-permute-start.4
  10.5 0.8 fusion.6.quality
  11.3 0.1 pad_add_fusion.meta
  11.3 0.0 collective-permute-done.1.lo_own
  11.3 0.0 collective-permute-done.2.lo_other
  11.3 1.2 collective-permute-done.3.hi_own
  12.5 2.6 collective-permute-done.4.hi_other
  15.1 0.0 collective-permute-done.other
  15.1 1.2 copy-done
  16.3 0.9 copy-done.3
  17.3 0.9 copy-done.4
  18.2 0.8 copy-done.6
  19.1 0.8 copy-done.7
  19.9 0.8 copy-done.9
  20.7 40.0 %spectra.1 = (bf16[960,128]{1,0:T(8,128)(2,1)S(1)}, bf16[960,128]{1,0:T(8,128)(2,1)S(1)}, bf16[960,128]{1,0:T(8,128)(2,1)S(1)}, bf16[960,128]{1,0:T(8,128)(2,1)S(1)}) custom-call(s32[2]{0:T(128)S(1)} %pad_add_fusion.meta, bf16[64,7680]{1,0:T(8,128)(2,1)S(1)} %copy-done, bf16[64,7680]{1,0:T(8,128)(2,1)S(1)} %collective-permute-done.other, ...), custom_call_target="tpu_custom_call" | custom-call | flops 6000000000 | bytes 4000000 | tf_op jit(solution)/shard_map/spectra/pallas_call | solution.py:176
  60.7 2.6 collective-permute-start.6
  63.3 1.2 collective-permute-start.7
  64.4 0.1 collective-permute-start.5
  64.5 2.1 collective-permute-start.12
  66.6 3.2 %collective-permute-start.8 = (bf16[960,128]{1,0:T(8,128)(2,1)S(1)}, bf16[960,128]{1,0:T(8,128)(2,1)S(1)}, u32[]{:S(2)}, u32[]{:S(2)}) collective-permute-start(bf16[960,128]{1,0:T(8,128)(2,1)S(1)} %get-tuple-element.11.rest_2_), channel_id=1, source_target_pairs={{0,8},{1,9},{2,10},{3,11},{4,12},{5,13},{6,14},{7,15},{8,16},{9,17... | collective-permute-start | bytes 737288 | tf_op jit(solution)/shard_map/ppermute | solution.py:442
  69.8 4.7 %collective-permute-done.6.rest_4_ = bf16[960,128]{1,0:T(8,128)(2,1)S(1)} collective-permute-done((bf16[960,128]{1,0:T(8,128)(2,1)S(1)}, bf16[960,128]{1,0:T(8,128)(2,1)S(1)}, u32[]{:S(2)}, u32[]{:S(2)}) %collective-permute-start.6) | collective-permute-done | bytes 245792 | tf_op jit(solution)/shard_map/ppermute | solution.py:442
  74.5 3.2 %collective-permute-start.10 = (bf16[960,128]{1,0:T(8,128)(2,1)S(1)}, bf16[960,128]{1,0:T(8,128)(2,1)S(1)}, u32[]{:S(2)}, u32[]{:S(2)}) collective-permute-start(bf16[960,128]{1,0:T(8,128)(2,1)S(1)} %collective-permute-done.6.rest_4_), channel_id=1, source_target_pairs={{0,8},{1,9},{2,10},{3,11},{4,12},{5,13},{6,14},{7,15},{8,16},{9,17... | collective-permute-start | bytes 737288 | tf_op jit(solution)/shard_map/ppermute | solution.py:442
  77.7 0.0 collective-permute-done.7.rest_5_
  77.7 2.1 collective-permute-start.14
  79.8 0.0 collective-permute-done.5.rest_3_
  79.8 3.2 %collective-permute-start.11 = (bf16[960,128]{1,0:T(8,128)(2,1)S(1)}, bf16[960,128]{1,0:T(8,128)(2,1)S(1)}, u32[]{:S(2)}, u32[]{:S(2)}) collective-permute-start(bf16[960,128]{1,0:T(8,128)(2,1)S(1)} %collective-permute-done.7.rest_5_), channel_id=1, source_target_pairs={{0,8},{1,9},{2,10},{3,11},{4,12},{5,13},{6,14},{7,15},{8,16},{9,17... | collective-permute-start | bytes 737288 | tf_op jit(solution)/shard_map/ppermute | solution.py:442
  83.0 0.0 collective-permute-done.12.rest_10_
  83.1 2.1 collective-permute-start.13
  85.2 0.0 collective-permute-done.8.rest_6_
  85.2 1.9 collective-permute-start.15
  87.1 0.0 collective-permute-done.10.rest_8_
  87.1 3.4 %collective-permute-start.9 = (bf16[960,128]{1,0:T(8,128)(2,1)S(1)}, bf16[960,128]{1,0:T(8,128)(2,1)S(1)}, u32[]{:S(2)}, u32[]{:S(2)}) collective-permute-start(bf16[960,128]{1,0:T(8,128)(2,1)S(1)} %collective-permute-done.5.rest_3_), channel_id=1, source_target_pairs={{0,8},{1,9},{2,10},{3,11},{4,12},{5,13},{6,14},{7,15},{8,16},{9,17... | collective-permute-start | bytes 737288 | tf_op jit(solution)/shard_map/ppermute | solution.py:442
  90.5 0.1 fusion.4
  90.6 0.1 copy.15.reach_own
  90.7 0.1 copy.16.reach_prev
  90.8 0.0 collective-permute-done.11.rest_9_
  90.9 0.0 collective-permute-done.13.rest_11_
  90.9 0.0 collective-permute-done.14.rest_12_
  90.9 5.0 %collective-permute-done.15.rest_13_ = bf16[960,128]{1,0:T(8,128)(2,1)S(1)} collective-permute-done((bf16[960,128]{1,0:T(8,128)(2,1)S(1)}, bf16[960,128]{1,0:T(8,128)(2,1)S(1)}, u32[]{:S(2)}, u32[]{:S(2)}) %collective-permute-start.15) | collective-permute-done | bytes 245792 | tf_op jit(solution)/shard_map/ppermute | solution.py:442
  95.9 0.0 collective-permute-done.9.rest_7_
  95.9 0.7 copy-done.1
  96.6 0.0 copy-done.8
  96.6 0.9 copy-done.2
  97.6 166.3 %cross.1 = (f32[2,2,2,480,128]{4,3,2,1,0:T(8,128)S(1)}, bf16[1920,128]{1,0:T(8,128)(2,1)S(1)}) custom-call(s32[128,1]{1,0:T(8,128)S(1)} %copy.15.reach_own, s32[128,1]{1,0:T(8,128)S(1)} %copy.16.reach_prev, bf16[128,128]{1,0:T(8,128)(2,1)S(1)} %copy-done.8, bf16[16,16,128]{2,1,0:T(8,128)(2,1)S(1)} %copy-done.5, ...), custom_call_target="tpu_custom_call" | custom-call | flops 30000001024 | bytes 6000000 | tf_op jit(solution)/shard_map/cross/pallas_call | solution.py:326
  263.9 0.0 copy-start.10
  263.9 0.1 dynamic-slice_bitcast_fusion
  264.1 2.7 collective-permute-start.16
  266.8 0.1 pad_dynamic-slice_fusion
  266.9 0.7 reshape.32
  267.6 0.9 pad.14
  268.5 0.8 reshape.33
  269.4 0.1 dynamic_slice.36
  269.5 2.1 collective-permute-start.17
  271.6 1.9 collective-permute-start.18
  273.5 0.9 fusion.2
  274.5 4.0 %collective-permute-done.17.far_a = bf16[960,128]{1,0:T(8,128)(2,1)S(1)} collective-permute-done((bf16[960,128]{1,0:T(8,128)(2,1)S(1)}, bf16[960,128]{1,0:T(8,128)(2,1)S(1)}, u32[]{:S(2)}, u32[]{:S(2)}) %collective-permute-start.17) | collective-permute-done | bytes 245792 | tf_op jit(solution)/shard_map/ppermute | solution.py:442
  278.4 5.9 %collective-permute-done.18.far_b = bf16[960,128]{1,0:T(8,128)(2,1)S(1)} collective-permute-done((bf16[960,128]{1,0:T(8,128)(2,1)S(1)}, bf16[960,128]{1,0:T(8,128)(2,1)S(1)}, u32[]{:S(2)}, u32[]{:S(2)}) %collective-permute-start.18) | collective-permute-done | bytes 245792 | tf_op jit(solution)/shard_map/ppermute | solution.py:442
  284.3 0.0 collective-permute-done.16.theirs
  284.3 2.5 finish.1
  (18 shorter events, 0.1 us)
Async XLA Ops:
  0.0 15.1 %collective-permute-start = (bf16[64,7680]{1,0:T(8,128)(2,1)}, bf16[64,7680]{1,0:T(8,128)(2,1)S(1)}, u32[]{:S(2)}, u32[]{:S(2)}) collective-permute-start(bf16[64,7680]{1,0:T(8,128)(2,1)} %own.1), channel_id=1, source_target_pairs={{0,4},{1,5},{2,6},{3,7},{4,0},{5,1},{6,2},{7,3},{8,12},{9,13},{10,... | collective-permute-start | bytes 2949128 | tf_op jit(solution)/shard_map/ppermute | solution.py:442
  1.5 9.9 %collective-permute-start.1 = (bf16[64,256]{1,0:T(8,128)(2,1)S(1)}, bf16[64,256]{1,0:T(8,128)(2,1)S(1)}, u32[]{:S(2)}, u32[]{:S(2)}) collective-permute-start(bf16[64,256]{1,0:T(8,128)(2,1)S(1)} %get-tuple-element.20), channel_id=1, source_target_pairs={{0,1},{1,2},{2,3},{4,5},{5,6},{6,7},{8,9},{9,10},{10,11},{12,13},{... | collective-permute-start | bytes 98312 | tf_op jit(solution)/shard_map/ppermute | solution.py:442
  4.6 6.8 %collective-permute-start.2 = (bf16[64,256]{1,0:T(8,128)(2,1)S(1)}, bf16[64,256]{1,0:T(8,128)(2,1)S(1)}, u32[]{:S(2)}, u32[]{:S(2)}) collective-permute-start(bf16[64,256]{1,0:T(8,128)(2,1)S(1)} %get-tuple-element.20), channel_id=1, source_target_pairs={{0,5},{1,6},{2,7},{4,1},{5,2},{6,3},{8,13},{9,14},{10,15},{12,9},{... | collective-permute-start | bytes 98312 | tf_op jit(solution)/shard_map/ppermute | solution.py:442
  7.9 4.7 %collective-permute-start.3 = (bf16[64,256]{1,0:T(8,128)(2,1)S(1)}, bf16[64,256]{1,0:T(8,128)(2,1)S(1)}, u32[]{:S(2)}, u32[]{:S(2)}) collective-permute-start(bf16[64,256]{1,0:T(8,128)(2,1)S(1)} %get-tuple-element.19), channel_id=1, source_target_pairs={{1,0},{2,1},{3,2},{5,4},{6,5},{7,6},{9,8},{10,9},{11,10},{13,12},{... | collective-permute-start | bytes 98312 | tf_op jit(solution)/shard_map/ppermute | solution.py:442
  9.2 6.0 %collective-permute-start.4 = (bf16[64,256]{1,0:T(8,128)(2,1)S(1)}, bf16[64,256]{1,0:T(8,128)(2,1)S(1)}, u32[]{:S(2)}, u32[]{:S(2)}) collective-permute-start(bf16[64,256]{1,0:T(8,128)(2,1)S(1)} %get-tuple-element.19), channel_id=1, source_target_pairs={{1,4},{2,5},{3,6},{5,0},{6,1},{7,2},{9,12},{10,13},{11,14},{13,8},... | collective-permute-start | bytes 98312 | tf_op jit(solution)/shard_map/ppermute | solution.py:442
  11.3 79.2 %copy-start.11 = (s32[512]{0:T(512)S(1)}, s32[512]{0:T(512)}, u32[]{:S(2)}) copy-start(s32[512]{0:T(512)} %param.12) | copy-start | bytes 6148
  15.1 1.2 copy-start
  16.3 0.9 copy-start.3
  17.3 0.9 copy-start.4
  18.2 0.8 copy-start.6
  19.1 0.8 copy-start.7
  19.9 0.8 copy-start.9
  20.7 75.9 %copy-start.5 = (bf16[16,16,128]{2,1,0:T(8,128)(2,1)S(1)}, bf16[16,16,128]{2,1,0:T(8,128)(2,1)}, u32[]{:S(2)}) copy-start(bf16[16,16,128]{2,1,0:T(8,128)(2,1)} %constant.84.clone.rest_1_) | copy-start | bytes 196612
  20.7 75.9 %copy-start.8 = (bf16[128,128]{1,0:T(8,128)(2,1)S(1)}, bf16[128,128]{1,0:T(8,128)(2,1)}, u32[]{:S(2)}) copy-start(bf16[128,128]{1,0:T(8,128)(2,1)} %constant.83.clone.rest_0_) | copy-start | bytes 98308
  60.7 13.8 %collective-permute-start.6 = (bf16[960,128]{1,0:T(8,128)(2,1)S(1)}, bf16[960,128]{1,0:T(8,128)(2,1)S(1)}, u32[]{:S(2)}, u32[]{:S(2)}) collective-permute-start(bf16[960,128]{1,0:T(8,128)(2,1)S(1)} %get-tuple-element.13), channel_id=1, source_target_pairs={{0,2},{1,3},{2,0},{3,1},{4,6},{5,7},{6,4},{7,5},{8,10},{9,11},{10,... | collective-permute-start | bytes 737288 | tf_op jit(solution)/shard_map/ppermute | solution.py:442
  63.3 14.5 %collective-permute-start.7 = (bf16[960,128]{1,0:T(8,128)(2,1)S(1)}, bf16[960,128]{1,0:T(8,128)(2,1)S(1)}, u32[]{:S(2)}, u32[]{:S(2)}) collective-permute-start(bf16[960,128]{1,0:T(8,128)(2,1)S(1)} %get-tuple-element.14), channel_id=1, source_target_pairs={{0,3},{1,2},{2,1},{3,0},{4,7},{5,6},{6,5},{7,4},{8,11},{9,10},{10,... | collective-permute-start | bytes 737288 | tf_op jit(solution)/shard_map/ppermute | solution.py:442
  64.4 15.4 %collective-permute-start.5 = (bf16[960,128]{1,0:T(8,128)(2,1)S(1)}, bf16[960,128]{1,0:T(8,128)(2,1)S(1)}, u32[]{:S(2)}, u32[]{:S(2)}) collective-permute-start(bf16[960,128]{1,0:T(8,128)(2,1)S(1)} %get-tuple-element.12), channel_id=1, source_target_pairs={{0,1},{1,0},{2,3},{3,2},{4,5},{5,4},{6,7},{7,6},{8,9},{9,8},{10,11... | collective-permute-start | bytes 737288 | tf_op jit(solution)/shard_map/ppermute | solution.py:442
  64.5 18.5 %collective-permute-start.12 = (bf16[960,128]{1,0:T(8,128)(2,1)S(1)}, bf16[960,128]{1,0:T(8,128)(2,1)S(1)}, u32[]{:S(2)}, u32[]{:S(2)}) collective-permute-start(bf16[960,128]{1,0:T(8,128)(2,1)S(1)} %get-tuple-element.11.rest_2_), channel_id=1, source_target_pairs={{8,0},{9,1},{10,2},{11,3},{12,4},{13,5},{14,6},{15,7},{16,8},{17,9... | collective-permute-start | bytes 737288 | tf_op jit(solution)/shard_map/ppermute | solution.py:442
  66.6 18.6 %collective-permute-start.8 = (bf16[960,128]{1,0:T(8,128)(2,1)S(1)}, bf16[960,128]{1,0:T(8,128)(2,1)S(1)}, u32[]{:S(2)}, u32[]{:S(2)}) collective-permute-start(bf16[960,128]{1,0:T(8,128)(2,1)S(1)} %get-tuple-element.11.rest_2_), channel_id=1, source_target_pairs={{0,8},{1,9},{2,10},{3,11},{4,12},{5,13},{6,14},{7,15},{8,16},{9,17... | collective-permute-start | bytes 737288 | tf_op jit(solution)/shard_map/ppermute | solution.py:442
  74.5 12.6 %collective-permute-start.10 = (bf16[960,128]{1,0:T(8,128)(2,1)S(1)}, bf16[960,128]{1,0:T(8,128)(2,1)S(1)}, u32[]{:S(2)}, u32[]{:S(2)}) collective-permute-start(bf16[960,128]{1,0:T(8,128)(2,1)S(1)} %collective-permute-done.6.rest_4_), channel_id=1, source_target_pairs={{0,8},{1,9},{2,10},{3,11},{4,12},{5,13},{6,14},{7,15},{8,16},{9,17... | collective-permute-start | bytes 737288 | tf_op jit(solution)/shard_map/ppermute | solution.py:442
  77.7 13.1 %collective-permute-start.14 = (bf16[960,128]{1,0:T(8,128)(2,1)S(1)}, bf16[960,128]{1,0:T(8,128)(2,1)S(1)}, u32[]{:S(2)}, u32[]{:S(2)}) collective-permute-start(bf16[960,128]{1,0:T(8,128)(2,1)S(1)} %collective-permute-done.6.rest_4_), channel_id=1, source_target_pairs={{8,0},{9,1},{10,2},{11,3},{12,4},{13,5},{14,6},{15,7},{16,8},{17,9... | collective-permute-start | bytes 737288 | tf_op jit(solution)/shard_map/ppermute | solution.py:442
  79.8 11.0 %collective-permute-start.11 = (bf16[960,128]{1,0:T(8,128)(2,1)S(1)}, bf16[960,128]{1,0:T(8,128)(2,1)S(1)}, u32[]{:S(2)}, u32[]{:S(2)}) collective-permute-start(bf16[960,128]{1,0:T(8,128)(2,1)S(1)} %collective-permute-done.7.rest_5_), channel_id=1, source_target_pairs={{0,8},{1,9},{2,10},{3,11},{4,12},{5,13},{6,14},{7,15},{8,16},{9,17... | collective-permute-start | bytes 737288 | tf_op jit(solution)/shard_map/ppermute | solution.py:442
  83.1 7.8 %collective-permute-start.13 = (bf16[960,128]{1,0:T(8,128)(2,1)S(1)}, bf16[960,128]{1,0:T(8,128)(2,1)S(1)}, u32[]{:S(2)}, u32[]{:S(2)}) collective-permute-start(bf16[960,128]{1,0:T(8,128)(2,1)S(1)} %collective-permute-done.5.rest_3_), channel_id=1, source_target_pairs={{8,0},{9,1},{10,2},{11,3},{12,4},{13,5},{14,6},{15,7},{16,8},{17,9... | collective-permute-start | bytes 737288 | tf_op jit(solution)/shard_map/ppermute | solution.py:442
  85.2 10.7 %collective-permute-start.15 = (bf16[960,128]{1,0:T(8,128)(2,1)S(1)}, bf16[960,128]{1,0:T(8,128)(2,1)S(1)}, u32[]{:S(2)}, u32[]{:S(2)}) collective-permute-start(bf16[960,128]{1,0:T(8,128)(2,1)S(1)} %collective-permute-done.7.rest_5_), channel_id=1, source_target_pairs={{8,0},{9,1},{10,2},{11,3},{12,4},{13,5},{14,6},{15,7},{16,8},{17,9... | collective-permute-start | bytes 737288 | tf_op jit(solution)/shard_map/ppermute | solution.py:442
  87.1 8.8 %collective-permute-start.9 = (bf16[960,128]{1,0:T(8,128)(2,1)S(1)}, bf16[960,128]{1,0:T(8,128)(2,1)S(1)}, u32[]{:S(2)}, u32[]{:S(2)}) collective-permute-start(bf16[960,128]{1,0:T(8,128)(2,1)S(1)} %collective-permute-done.5.rest_3_), channel_id=1, source_target_pairs={{0,8},{1,9},{2,10},{3,11},{4,12},{5,13},{6,14},{7,15},{8,16},{9,17... | collective-permute-start | bytes 737288 | tf_op jit(solution)/shard_map/ppermute | solution.py:442
  95.9 0.7 copy-start.1
  96.6 0.9 copy-start.2
  263.9 2.9 %copy-start.10 = (s32[512]{0:T(512)S(1)}, s32[512]{0:T(512)}, u32[]{:S(2)}) copy-start(s32[512]{0:T(512)} %param.11) | copy-start | bytes 6148
  264.1 20.2 %collective-permute-start.16 = (f32[2,2,480,128]{3,2,1,0:T(8,128)S(1)}, f32[2,2,480,128]{3,2,1,0:T(8,128)S(1)}, u32[]{:S(2)}, u32[]{:S(2)}) collective-permute-start(f32[2,2,480,128]{3,2,1,0:T(8,128)S(1)} %get-tuple-element.17), channel_id=1, source_target_pairs={{0,4},{1,5},{2,6},{3,7},{4,0},{5,1},{6,2},{7,3},{8,12},{9,13},{10,... | collective-permute-start | bytes 2949128 | tf_op jit(solution)/shard_map/ppermute | solution.py:442
  269.5 9.0 %collective-permute-start.17 = (bf16[960,128]{1,0:T(8,128)(2,1)S(1)}, bf16[960,128]{1,0:T(8,128)(2,1)S(1)}, u32[]{:S(2)}, u32[]{:S(2)}) collective-permute-start(bf16[960,128]{1,0:T(8,128)(2,1)S(1)} %bitcast.24), channel_id=1, source_target_pairs={{8,0},{9,1},{10,2},{11,3},{12,4},{13,5},{14,6},{15,7},{16,8},{17,9... | collective-permute-start | bytes 737288 | tf_op jit(solution)/shard_map/ppermute | solution.py:442
  271.6 12.7 %collective-permute-start.18 = (bf16[960,128]{1,0:T(8,128)(2,1)S(1)}, bf16[960,128]{1,0:T(8,128)(2,1)S(1)}, u32[]{:S(2)}, u32[]{:S(2)}) collective-permute-start(bf16[960,128]{1,0:T(8,128)(2,1)S(1)} %bitcast.23), channel_id=1, source_target_pairs={{8,4},{9,5},{10,6},{11,7},{12,0},{13,1},{14,2},{15,3},{16,12},{17,... | collective-permute-start | bytes 737288 | tf_op jit(solution)/shard_map/ppermute | solution.py:442

commit v2 on v1

--- a/solution.py
+++ b/solution.py
@@ -57,6 +57,14 @@
     second = np.stack([real, imag]).reshape(2, n_freq, 2, half, 2 * TBLK)
     second = second.transpose(1, 2, 0, 3, 4).reshape(n_freq, 2, 2 * half, 2 * TBLK)
     return first, twist, second.astype(ml_dtypes.bfloat16)
+
+
+def block_bins(n_freq):
+    return 16 if n_freq <= 4 else 8
+
+
+def whole(shape):
+    return pl.BlockSpec(shape, lambda t: (0,) * len(shape))
 
 
 def spectra_kernel(
@@ -104,7 +112,7 @@
             magnitude[j + n] = jnp.abs(part).astype(jnp.bfloat16)
         return carry
 
-    lax.fori_loop(0, count_a // 2 + 1, fir, 0)
+    lax.fori_loop(0, count_a // 2 + 1, fir, 0, unroll=True)
 
     def whiten(i, carry):
         j = 2 * i
@@ -116,7 +124,7 @@
             whitened[rows, :] = part
         return carry
 
-    lax.fori_loop(0, count_a // 2, whiten, 0)
+    lax.fori_loop(0, count_a // 2, whiten, 0, unroll=True)
     whitened[count_a * both : pad_a * both, :] = jnp.zeros(
         ((pad_a - count_a) * both, TBLK), jnp.float32
     )
@@ -135,10 +143,11 @@
             tw_im[rows, :] = im * twist[0] - re * twist[1]
         return carry
 
-    lax.fori_loop(0, both // 2, sections, 0)
+    lax.fori_loop(0, both // 2, sections, 0, unroll=True)
 
     rk = second.shape[2]
-    group = max(1, 16 // rk)
+    half = rk // 2
+    group = block_bins(n_freq) // half
     scale = quality[...] * (1.0 / math.sqrt(count_a * TBLK))
     turn = jnp.concatenate([second[band ^ d, core] for d in range(n_freq)], axis=0)
 
@@ -157,12 +166,12 @@
             results.append(result * scale)
         rows = pl.ds(pl.multiple_of(i * group * rk, 16), group * rk)
         for d in range(n_freq):
-            parts = [r[d * rk : (d + 1) * rk] for r in results]
-            block = parts[0] if group == 1 else jnp.concatenate(parts, axis=0)
+            starts = [d * rk + p * half for p in range(2)]
+            block = jnp.concatenate([r[s : s + half] for s in starts for r in results], axis=0)
             outs[d][rows, :] = block.astype(jnp.bfloat16)
         return carry
 
-    lax.fori_loop(0, count_a // group, bins, 0)
+    lax.fori_loop(0, count_a // group, bins, 0, unroll=True)
 
 
 def spectra(meta, own, other, halos, quality, n_freq):
@@ -172,12 +181,14 @@
     rk = second.shape[2]
     pad_a = first.shape[1]
     both = 2 * ch
-    vmem = pl.BlockSpec(memory_space=pltpu.VMEM)
+    tables = (stencil_table(False), stencil_table(True), first, twist, second)
+    operands = (own, other, *halos, *(jnp.asarray(t) for t in tables), quality)
     return pl.pallas_call(
         functools.partial(spectra_kernel, count_a, n_freq),
+        grid=(1,),
         out_shape=[jax.ShapeDtypeStruct((count_a * rk, both), jnp.bfloat16)] * n_freq,
-        in_specs=[pl.BlockSpec(memory_space=pltpu.SMEM)] + [vmem] * 12,
-        out_specs=[vmem] * n_freq,
+        in_specs=[pl.BlockSpec(memory_space=pltpu.SMEM)] + [whole(x.shape) for x in operands],
+        out_specs=[whole((count_a * rk, both))] * n_freq,
         scratch_shapes=[
             pltpu.VMEM((count_a + 4, both, TBLK), jnp.bfloat16),
             pltpu.VMEM((count_a + 2, both, TBLK), jnp.float32),
@@ -186,51 +197,52 @@
             pltpu.VMEM((both * pad_a, TBLK), jnp.float32),
             pltpu.VMEM((both * pad_a, TBLK), jnp.float32),
         ],
-        compiler_params=pltpu.CompilerParams(vmem_limit_bytes=48 * MIB),
+        compiler_params=pltpu.CompilerParams(vmem_limit_bytes=62 * MIB),
         cost_estimate=pl.CostEstimate(
             flops=6 * 10**9, bytes_accessed=4 * 10**6, transcendentals=0
         ),
         name="spectra",
-    )(
-        meta,
-        own,
-        other,
-        *halos,
-        jnp.asarray(stencil_table(False)),
-        jnp.asarray(stencil_table(True)),
-        jnp.asarray(first),
-        jnp.asarray(twist),
-        jnp.asarray(second),
-        quality,
-    )
-
-
-def cross_kernel(n_seg, rk, count_a, reach_own, reach_prev, *rest):
-    turn_ref, pick_ref = rest[0], rest[1]
-    own_refs = rest[2 : 2 + n_seg]
-    prev_refs = rest[2 + n_seg : 2 + 2 * n_seg]
-    next_refs = rest[2 + 2 * n_seg : 2 + 3 * n_seg]
-    near_ref, far_ref, w_near, w_far, sums = rest[2 + 3 * n_seg :]
+    )(meta, *operands)
+
+
+def cross_kernel(n_seg, half, count_a, reach_own, reach_prev, *rest):
+    turn_ref, pick_ref, cut_ref = rest[:3]
+    own_refs = rest[3 : 3 + n_seg]
+    prev_refs = rest[3 + n_seg : 3 + 2 * n_seg]
+    next_refs = rest[3 + 2 * n_seg : 3 + 3 * n_seg]
+    near_ref, far_ref, w_near, w_far, edge, sum_one, sum_two, sum_far = rest[3 + 3 * n_seg :]
     step = pl.program_id(0)
     both = own_refs[0].shape[1]
     depth = turn_ref.shape[0]
-    half = rk // 2
     nb = pick_ref.shape[0]
     nk1 = nb // half
     slabs = both // 8
-    per_group = slabs // 2
+    rb = 2 * nb
+    block = pl.ds(pl.multiple_of(step * rb, rb), rb)
 
     @pl.when(step == 0)
     def _():
-        row = lax.broadcasted_iota(jnp.int32, (both, both), 0)
-        col = lax.broadcasted_iota(jnp.int32, (both, both), 1)
-        near = (col >= row) & (both + col - row < reach_own[...])
-        far = (col < row) & (2 * both + col - row < reach_prev[...])
-        w_near[...] = jnp.where(near, 1.0, 0.0)
-        w_far[...] = jnp.where(far, 1.0, 0.0)
+        row = lax.broadcasted_iota(jnp.int32, (16, both), 0) % 8
+        col = lax.broadcasted_iota(jnp.int32, (16, both), 1)
+        offset = both + col - row
+        for a in range(slabs):
+            mine = reach_own[a * 8 : a * 8 + 8, :]
+            lent = reach_prev[a * 8 : a * 8 + 8, :]
+            mine = jnp.concatenate([mine, mine], axis=0)
+            lent = jnp.concatenate([lent, lent], axis=0)
+            inner = col < both - 8 * a
+            w_near[a] = jnp.where(inner & ((col < row) | (offset < mine)), 1.0, 0.0)
+            w_far[a] = jnp.where(~inner & (offset < lent), 1.0, 0.0)
+        row = lax.broadcasted_iota(jnp.int32, (both, 2 * both), 0)
+        col = lax.broadcasted_iota(jnp.int32, (both, 2 * both), 1)
+        same = (row // (both // 2)) == (col // both)
+        for d in range(1, 8):
+            hit = same & (col % both == both - d) & (row % 8 >= d)
+            hit = hit & (2 * both - d < reach_prev[...])
+            edge[(d - 1) * both : d * both, :] = jnp.where(hit, 1.0, 0.0).astype(jnp.bfloat16)
 
     def stacked(refs):
-        return jnp.concatenate([r[...] for r in refs], axis=0)
+        return jnp.concatenate([r[block, :] for r in refs], axis=0)
 
     def left_rows(block):
         re = block.astype(jnp.float32).T.astype(jnp.bfloat16)
@@ -241,66 +253,85 @@
 
     own = stacked(own_refs)
     nxt = stacked(next_refs)
-    right = jnp.concatenate([own, nxt], axis=1)
-    left_own = left_rows(own)
-    left_prev = left_rows(stacked(prev_refs))
-    row = lax.broadcasted_iota(jnp.int32, (8, both), 0)
-    col = lax.broadcasted_iota(jnp.int32, (8, both), 1)
-    lead = col - row
-
-    def bin_step(i, carry):
-        pick = pick_ref[i][None]
-        for g in range(2):
-            here = slice(g * per_group, (g + 1) * per_group)
-            rows = (left_own[here] * pick).reshape(per_group * 16, depth)
-            near = jnp.dot(rows, right, preferred_element_type=jnp.float32)
-            rows = (left_prev[here] * pick).reshape(per_group * 16, depth)
-            far = jnp.dot(rows, nxt, preferred_element_type=jnp.float32)
-            for p in range(2):
-                acc = [None] * 3
-                for n in range(per_group):
-                    a = g * per_group + n
-                    at = n * 16 + p * 8
-                    local = near[at : at + 8, :both]
-                    beyond = near[at : at + 8, both:]
-                    distant = far[at : at + 8]
-                    wn = w_near[a * 8 : a * 8 + 8, :]
-                    wf = w_far[a * 8 : a * 8 + 8, :]
-                    terms = (
-                        jnp.where(lead >= 8 * a, local, beyond),
-                        beyond * wn,
-                        distant * wf,
-                    )
-                    shift = (both - 8 * a) % both
-                    for r, term in enumerate(terms):
-                        if shift:
-                            term = pltpu.roll(term, shift, 1)
-                        acc[r] = term if acc[r] is None else acc[r] + term
-                for r in range(3):
-                    sums[(r * 2 + g) * 2 + p, pl.ds(pl.multiple_of(i * 8, 8), 8), :] = acc[r]
-        return carry
-
-    lax.fori_loop(0, nb, bin_step, 0)
-
-    def diagonal(r, g, p):
-        total = None
-        for b in range(8):
-            part = sums[(r * 2 + g) * 2 + p, pl.ds(b, nb, stride=8), :]
-            if b:
-                part = pltpu.roll(part, both - b, 1)
-            total = part if total is None else total + part
-        return total
-
+    prev = stacked(prev_refs)
+    left = jnp.concatenate([left_rows(own), left_rows(prev)], axis=2)
+    pick = pick_ref[...]
+
+    zero = jnp.zeros_like(own)
+    for a in range(slabs):
+        g, first = divmod(a, slabs // 2)
+        if a == 0:
+            right = jnp.concatenate(
+                [jnp.concatenate([own, nxt], axis=1), jnp.concatenate([zero, zero], axis=1)],
+                axis=0,
+            )
+        else:
+            moved_own = pltpu.roll(own, both - 8 * a, 1).reshape(depth // 16, 16, both)
+            moved_next = pltpu.roll(nxt, both - 8 * a, 1).reshape(depth // 16, 16, both)
+            cut = cut_ref[a][None]
+            inner = moved_next * cut
+            outer = moved_next - inner
+            local = (moved_own * cut + outer).reshape(depth, both)
+            inner = inner.reshape(depth, both)
+            outer = outer.reshape(depth, both)
+            right = jnp.concatenate(
+                [
+                    jnp.concatenate([local, inner], axis=1),
+                    jnp.concatenate([zero, outer], axis=1),
+                ],
+                axis=0,
+            )
+        rows = (left[a][None] * pick).reshape(nb * 16, 2 * depth)
+        result = jnp.dot(rows, right, preferred_element_type=jnp.float32)
+        one = result[:, :both]
+        two = result[:, both:].reshape(nb, 16, both)
+        near = (two * w_near[a][None]).reshape(nb * 16, both)
+        far = (two * w_far[a][None]).reshape(nb * 16, both)
+        if first == 0:
+            sum_one[g], sum_two[g], sum_far[g] = one, near, far
+        else:
+            sum_one[g] += one
+            sum_two[g] += near
+            sum_far[g] += far
+
+    def split(ref):
+        x = ref[block, :].astype(jnp.float32)
+        return x[:nb], x[nb:]
+
+    lefts = [split(r) for r in prev_refs]
+    rights = [split(r) for r in next_refs]
+    pieces = []
+    for d in range(1, 8):
+        re = im = None
+        for (xr, xi), (yr, yi) in zip(lefts, rights):
+            yr, yi = pltpu.roll(yr, d, 1), pltpu.roll(yi, d, 1)
+            r, i = xr * yr + xi * yi, xi * yr - xr * yi
+            re, im = (r, i) if re is None else (re + r, im + i)
+        pieces.append(jnp.concatenate([re, im], axis=0).astype(jnp.bfloat16))
+    margin = jnp.dot(
+        jnp.concatenate(pieces, axis=1), edge[...], preferred_element_type=jnp.float32
+    )
+
+    lane = lax.broadcasted_iota(jnp.int32, (nb, both), 1)
     far_parts = []
     for g in range(2):
         for p in range(2):
-            for r in range(2):
-                value = diagonal(r, g, p)
+            low = high = far = None
+            for b in range(8):
+                rows = pl.ds(p * 8 + b, nb, stride=16)
+                one, two, three = sum_one[g, rows, :], sum_two[g, rows, :], sum_far[g, rows, :]
+                if b == 0:
+                    low, high, far = one, two, three
+                    continue
+                low += pltpu.roll(jnp.where(lane >= b, one, two), both - b, 1)
+                high += pltpu.roll(jnp.where(lane >= b, two, 0.0), both - b, 1)
+                far += pltpu.roll(three, both - b, 1)
+            for r, value in enumerate((low, high)):
                 for n in range(nk1):
                     near_ref[g, p, r, pl.ds(step * nk1 + n, half, stride=count_a), :] = value[
                         n * half : (n + 1) * half
                     ]
-            far_parts.append(diagonal(2, g, p))
+            far_parts.append(far + margin[p * nb : (p + 1) * nb, g * both : (g + 1) * both])
     far_ref[...] = jnp.concatenate(far_parts, axis=0).astype(jnp.bfloat16)
 
 
@@ -308,60 +339,51 @@
     n_seg = len(own)
     rows, both = own[0].shape
     half = rk // 2
-    rb = 32 if n_seg <= 4 else 16
+    nb = block_bins(n_seg)
+    rb = 2 * nb
     depth = n_seg * rb
-    nb = rb // 2
     steps = rows // rb
+    slabs = both // 8
     lane = np.arange(depth)
-    within = lane % rb
-    part = within // half % 2
-    bin_of = within // rk * half + within % half
+    part = lane % rb // nb
     turn = np.zeros((depth, depth))
-    turn[lane + np.where(part == 0, half, -half), lane] = np.where(part == 0, 1.0, -1.0)
-    pick = (bin_of[None, None, :] == np.arange(nb)[:, None, None]).astype(np.float32)
-    pick = np.broadcast_to(pick, (nb, 16, depth)).astype(ml_dtypes.bfloat16)
-    whole = lambda shape: pl.BlockSpec(shape, lambda t: (0,) * len(shape))
-    block = pl.BlockSpec((rb, both), lambda t: (t, 0))
+    turn[lane + np.where(part == 0, nb, -nb), lane] = np.where(part == 0, 1.0, -1.0)
+    lane = np.arange(2 * depth)
+    pick = (lane % nb == np.arange(nb)[:, None, None]).astype(np.float32)
+    pick = np.broadcast_to(pick, (nb, 16, 2 * depth))
+    cut = np.arange(both) < both - 8 * np.arange(slabs)[:, None, None]
+    cut = np.broadcast_to(cut, (slabs, 16, both))
+    tables = [jnp.asarray(x.astype(ml_dtypes.bfloat16)) for x in (turn, pick, cut)]
+    operands = (reach_own, reach_prev, *tables, *own, *prev, *nxt)
     far_rows = 4 * nb
     return pl.pallas_call(
-        functools.partial(cross_kernel, n_seg, rk, count_a),
+        functools.partial(cross_kernel, n_seg, half, count_a),
         grid=(steps,),
         out_shape=[
             jax.ShapeDtypeStruct((2, 2, 2, rows // 2, both), jnp.float32),
             jax.ShapeDtypeStruct((steps * far_rows, both), jnp.bfloat16),
         ],
-        in_specs=[
-            whole((both, 1)),
-            whole((both, 1)),
-            whole(turn.shape),
-            whole(pick.shape),
-        ]
-        + [block] * (3 * n_seg),
+        in_specs=[whole(x.shape) for x in operands],
         out_specs=[
             whole((2, 2, 2, rows // 2, both)),
             pl.BlockSpec((far_rows, both), lambda t: (t, 0)),
         ],
         scratch_shapes=[
-            pltpu.VMEM((both, both), jnp.float32),
-            pltpu.VMEM((both, both), jnp.float32),
-            pltpu.VMEM((12, nb * 8, both), jnp.float32),
+            pltpu.VMEM((slabs, 16, both), jnp.float32),
+            pltpu.VMEM((slabs, 16, both), jnp.float32),
+            pltpu.VMEM((7 * both, 2 * both), jnp.bfloat16),
+            pltpu.VMEM((2, nb * 16, both), jnp.float32),
+            pltpu.VMEM((2, nb * 16, both), jnp.float32),
+            pltpu.VMEM((2, nb * 16, both), jnp.float32),
         ],
         compiler_params=pltpu.CompilerParams(
-            dimension_semantics=("arbitrary",), vmem_limit_bytes=48 * MIB
+            dimension_semantics=("arbitrary",), vmem_limit_bytes=62 * MIB
         ),
         cost_estimate=pl.CostEstimate(
             flops=30 * 10**9, bytes_accessed=6 * 10**6, transcendentals=0
         ),
         name="cross",
-    )(
-        reach_own,
-        reach_prev,
-        jnp.asarray(turn.astype(ml_dtypes.bfloat16)),
-        jnp.asarray(pick),
-        *own,
-        *prev,
-        *nxt,
-    )
+    )(*operands)
 
 
 def finish_kernel(rk, count_a, nb, meta, mine, theirs, far_a, far_b, count, out_ref, total):
@@ -386,24 +408,25 @@
                     total[p, place, :] += value[n * half : (n + 1) * half]
             return carry
 
-        lax.fori_loop(0, bins // nb, add, 0)
+        lax.fori_loop(0, bins // nb, add, 0, unroll=True)
         for p in range(2):
             out_ref[p, rows, :both] = near[p, 0] * inverse[:, :both]
             out_ref[p, rows, both:] = total[p] * inverse[:, both:]
 
 
 def finish(meta, mine, theirs, far_a, far_b, count, count_a, rk, nb):
-    vmem = pl.BlockSpec(memory_space=pltpu.VMEM)
     bins = mine.shape[2]
+    operands = (mine, theirs, far_a, far_b, count)
     return pl.pallas_call(
         functools.partial(finish_kernel, rk, count_a, nb),
+        grid=(1,),
         out_shape=jax.ShapeDtypeStruct((2, 2 * bins, BAND), jnp.float32),
-        in_specs=[pl.BlockSpec(memory_space=pltpu.SMEM)] + [vmem] * 5,
-        out_specs=vmem,
+        in_specs=[pl.BlockSpec(memory_space=pltpu.SMEM)] + [whole(x.shape) for x in operands],
+        out_specs=whole((2, 2 * bins, BAND)),
         scratch_shapes=[pltpu.VMEM((2, bins, TBLK), jnp.float32)],
-        compiler_params=pltpu.CompilerParams(vmem_limit_bytes=48 * MIB),
+        compiler_params=pltpu.CompilerParams(vmem_limit_bytes=62 * MIB),
         name="finish",
-    )(meta, mine, theirs, far_a, far_b, count)
+    )(meta, *operands)
 
 
 def skew_rows(matrix, keep):
@@ -468,7 +491,7 @@
     nxt = [moved(x, lambda c, f: (c - 2, f)) for x in own]
     prev = [moved(x, lambda c, f: (c + 2, f)) for x in own]
     near, far = cross(own, prev, nxt, reach_own, reach_prev, count_a, rk)
-    nb = (32 if n_freq <= 4 else 16) // 2
+    nb = block_bins(n_freq)
     steps = far.shape[0] // (4 * nb)
     far = far.reshape(steps, 2, 2 * nb, both)
     pick = lambda x, axis, at: lax.dynamic_index_in_dim(x, at, axis, keepdims=False)

time: 289 us -> 139 us (0.48)
  Pallas kernels: 209 us -> 62 us
    pallas_call x3, Pallas kernels: 209 us -> 62 us  [the longest x1 45.4 us: cross(): pl.pallas_call(functools.partial(cross_kernel, n_seg, half, count_a), gri...]
    unnamed x24 -> x42, local copies, waits for them, and re-layouts: 7.19 us -> 3.3 us
  transfers between devices with their start and end apart: 19 -> 19, of which waited for: 6 -> 5; matrix products, arithmetic and copies ran while one was open for 2% -> 4% of each run, Pallas kernels for 0% -> 0%
where the time goes in v2:
time: 139 us; the launch traced here: 137 us
  Pallas kernels  62 us (45%)
  starting transfers between devices  41.4 us (30%)
  waiting for transfers between devices  21.4 us (15%)
  local copies, waits for them, and re-layouts  8.81 us (6%)
  other arithmetic  2.66 us (2%)
    pallas_call x1, Pallas kernels, cross(): pl.pallas_call(functools.partial(cross_kernel, n_seg, half, count_a), gri...  45.4 us
    ppermute x19, starting transfers between devices, moved(): return lax.ppermute(x, ('chan', 'freq'), pairs)  41.4 us
    ppermute x19, waiting for transfers between devices, moved(): return lax.ppermute(x, ('chan', 'freq'), pairs)  21.4 us
    pallas_call x1, Pallas kernels, spectra(): pl.pallas_call(functools.partial(spectra_kernel, count_a, n_freq), grid=(...  13.4 us
    unnamed x42, local copies, waits for them, and re-layouts  3.3 us
    pallas_call x1, Pallas kernels, finish(): pl.pallas_call(functools.partial(finish_kernel, rk, count_a, nb), grid=(1...  3.2 us
  transfers between devices with their start and end apart: 19, of which 5 were waited for; matrix products, arithmetic and copies ran while one was open for 4% of the time, Pallas kernels for 0%

profile of v2, /device:TPU:9, one launch (start us, length us, event | category | flops | bytes accessed | tf_op | source)
XLA Modules:
  0.0 136.7 jit_solution(8269132800129166101)
XLA Ops:
  0.0 0.7 collective-permute-start
  0.7 0.8 fusion.7
  1.5 3.1 %collective-permute-start.1 = (bf16[64,256]{1,0:T(8,128)(2,1)S(1)}, bf16[64,256]{1,0:T(8,128)(2,1)S(1)}, u32[]{:S(2)}, u32[]{:S(2)}) collective-permute-start(bf16[64,256]{1,0:T(8,128)(2,1)S(1)} %get-tuple-element.20), channel_id=1, source_target_pairs={{0,1},{1,2},{2,3},{4,5},{5,6},{6,7},{8,9},{9,10},{10,11},{12,13},{... | collective-permute-start | bytes 98312 | tf_op jit(solution)/shard_map/ppermute | solution.py:465
  4.6 3.3 %collective-permute-start.2 = (bf16[64,256]{1,0:T(8,128)(2,1)S(1)}, bf16[64,256]{1,0:T(8,128)(2,1)S(1)}, u32[]{:S(2)}, u32[]{:S(2)}) collective-permute-start(bf16[64,256]{1,0:T(8,128)(2,1)S(1)} %get-tuple-element.20), channel_id=1, source_target_pairs={{0,5},{1,6},{2,7},{4,1},{5,2},{6,3},{8,13},{9,14},{10,15},{12,9},{... | collective-permute-start | bytes 98312 | tf_op jit(solution)/shard_map/ppermute | solution.py:465
  7.9 1.3 collective-permute-start.3
  9.2 1.3 collective-permute-start.4
  10.5 1.3 fusion.6.quality
  11.8 0.6 pad_add_fusion.meta
  12.5 0.0 collective-permute-done.1.lo_own
  12.5 0.0 collective-permute-done.2.lo_other
  12.5 0.0 copy-start.18
  12.5 0.0 collective-permute-done.3.hi_own
  12.5 2.6 %collective-permute-done.4.hi_other = bf16[64,256]{1,0:T(8,128)(2,1)S(1)} collective-permute-done((bf16[64,256]{1,0:T(8,128)(2,1)S(1)}, bf16[64,256]{1,0:T(8,128)(2,1)S(1)}, u32[]{:S(2)}, u32[]{:S(2)}) %collective-permute-start.4) | collective-permute-done | bytes 32800 | tf_op jit(solution)/shard_map/ppermute | solution.py:465
  15.1 0.0 collective-permute-done.other
  15.1 0.0 copy-done.17
  15.2 0.6 copy-done.20
  15.7 0.9 copy-done.6
  16.7 13.4 %spectra.1 = (bf16[960,128]{1,0:T(8,128)(2,1)}, bf16[960,128]{1,0:T(8,128)(2,1)}, bf16[960,128]{1,0:T(8,128)(2,1)}, bf16[960,128]{1,0:T(8,128)(2,1)}) custom-call(s32[2]{0:T(128)} %pad_add_fusion.meta, bf16[64,7680]{1,0:T(8,128)(2,1)} %own.1, bf16[64,7680]{1,0:T(8,128)(2,1)} %copy-done.6, bf16[64,256]{1,0:T(8,128)(2,1)} %copy-done.17, ...), custom_call_target="tpu_custom_call" | custom-call | flops 6000000000 | bytes 4000000 | tf_op jit(solution)/shard_map/spectra/pallas_call | solution.py:186
  30.1 2.5 %collective-permute-start.6 = (bf16[960,128]{1,0:T(8,128)(2,1)}, bf16[960,128]{1,0:T(8,128)(2,1)S(1)}, u32[]{:S(2)}, u32[]{:S(2)}) collective-permute-start(bf16[960,128]{1,0:T(8,128)(2,1)} %get-tuple-element.13), channel_id=1, source_target_pairs={{0,2},{1,3},{2,0},{3,1},{4,6},{5,7},{6,4},{7,5},{8,10},{9,11},{10,... | collective-permute-start | bytes 737288 | tf_op jit(solution)/shard_map/ppermute | solution.py:465
  32.7 1.1 collective-permute-start.7
  33.8 0.1 collective-permute-start.5
  33.9 2.1 %collective-permute-start.12 = (bf16[960,128]{1,0:T(8,128)(2,1)}, bf16[960,128]{1,0:T(8,128)(2,1)S(1)}, u32[]{:S(2)}, u32[]{:S(2)}) collective-permute-start(bf16[960,128]{1,0:T(8,128)(2,1)} %get-tuple-element.11.rest_3_), channel_id=1, source_target_pairs={{8,0},{9,1},{10,2},{11,3},{12,4},{13,5},{14,6},{15,7},{16,8},{17,9... | collective-permute-start | bytes 737288 | tf_op jit(solution)/shard_map/ppermute | solution.py:465
  36.0 3.2 %collective-permute-start.8 = (bf16[960,128]{1,0:T(8,128)(2,1)}, bf16[960,128]{1,0:T(8,128)(2,1)S(1)}, u32[]{:S(2)}, u32[]{:S(2)}) collective-permute-start(bf16[960,128]{1,0:T(8,128)(2,1)} %get-tuple-element.11.rest_3_), channel_id=1, source_target_pairs={{0,8},{1,9},{2,10},{3,11},{4,12},{5,13},{6,14},{7,15},{8,16},{9,17... | collective-permute-start | bytes 737288 | tf_op jit(solution)/shard_map/ppermute | solution.py:465
  39.2 5.0 %collective-permute-done.6.rest_5_ = bf16[960,128]{1,0:T(8,128)(2,1)S(1)} collective-permute-done((bf16[960,128]{1,0:T(8,128)(2,1)}, bf16[960,128]{1,0:T(8,128)(2,1)S(1)}, u32[]{:S(2)}, u32[]{:S(2)}) %collective-permute-start.6) | collective-permute-done | bytes 245792 | tf_op jit(solution)/shard_map/ppermute | solution.py:465
  44.2 3.2 %collective-permute-start.10 = (bf16[960,128]{1,0:T(8,128)(2,1)S(1)}, bf16[960,128]{1,0:T(8,128)(2,1)S(1)}, u32[]{:S(2)}, u32[]{:S(2)}) collective-permute-start(bf16[960,128]{1,0:T(8,128)(2,1)S(1)} %collective-permute-done.6.rest_5_), channel_id=1, source_target_pairs={{0,8},{1,9},{2,10},{3,11},{4,12},{5,13},{6,14},{7,15},{8,16},{9,17... | collective-permute-start | bytes 737288 | tf_op jit(solution)/shard_map/ppermute | solution.py:465
  47.4 0.0 collective-permute-done.7.rest_6_
  47.4 0.0 copy-start.8
  47.4 2.1 %collective-permute-start.14 = (bf16[960,128]{1,0:T(8,128)(2,1)S(1)}, bf16[960,128]{1,0:T(8,128)(2,1)S(1)}, u32[]{:S(2)}, u32[]{:S(2)}) collective-permute-start(bf16[960,128]{1,0:T(8,128)(2,1)S(1)} %collective-permute-done.6.rest_5_), channel_id=1, source_target_pairs={{8,0},{9,1},{10,2},{11,3},{12,4},{13,5},{14,6},{15,7},{16,8},{17,9... | collective-permute-start | bytes 737288 | tf_op jit(solution)/shard_map/ppermute | solution.py:465
  49.5 0.0 collective-permute-done.5.rest_4_
  49.5 3.2 %collective-permute-start.11 = (bf16[960,128]{1,0:T(8,128)(2,1)S(1)}, bf16[960,128]{1,0:T(8,128)(2,1)S(1)}, u32[]{:S(2)}, u32[]{:S(2)}) collective-permute-start(bf16[960,128]{1,0:T(8,128)(2,1)S(1)} %collective-permute-done.7.rest_6_), channel_id=1, source_target_pairs={{0,8},{1,9},{2,10},{3,11},{4,12},{5,13},{6,14},{7,15},{8,16},{9,17... | collective-permute-start | bytes 737288 | tf_op jit(solution)/shard_map/ppermute | solution.py:465
  52.7 0.0 collective-permute-done.12.rest_11_
  52.7 2.1 %collective-permute-start.13 = (bf16[960,128]{1,0:T(8,128)(2,1)S(1)}, bf16[960,128]{1,0:T(8,128)(2,1)S(1)}, u32[]{:S(2)}, u32[]{:S(2)}) collective-permute-start(bf16[960,128]{1,0:T(8,128)(2,1)S(1)} %collective-permute-done.5.rest_4_), channel_id=1, source_target_pairs={{8,0},{9,1},{10,2},{11,3},{12,4},{13,5},{14,6},{15,7},{16,8},{17,9... | collective-permute-start | bytes 737288 | tf_op jit(solution)/shard_map/ppermute | solution.py:465
  54.8 0.0 collective-permute-done.8.rest_7_
  54.8 1.9 %collective-permute-start.15 = (bf16[960,128]{1,0:T(8,128)(2,1)S(1)}, bf16[960,128]{1,0:T(8,128)(2,1)S(1)}, u32[]{:S(2)}, u32[]{:S(2)}) collective-permute-start(bf16[960,128]{1,0:T(8,128)(2,1)S(1)} %collective-permute-done.7.rest_6_), channel_id=1, source_target_pairs={{8,0},{9,1},{10,2},{11,3},{12,4},{13,5},{14,6},{15,7},{16,8},{17,9... | collective-permute-start | bytes 737288 | tf_op jit(solution)/shard_map/ppermute | solution.py:465
  56.8 0.0 collective-permute-done.10.rest_9_
  56.8 3.5 %collective-permute-start.9 = (bf16[960,128]{1,0:T(8,128)(2,1)S(1)}, bf16[960,128]{1,0:T(8,128)(2,1)}, u32[]{:S(2)}, u32[]{:S(2)}) collective-permute-start(bf16[960,128]{1,0:T(8,128)(2,1)S(1)} %collective-permute-done.5.rest_4_), channel_id=1, source_target_pairs={{0,8},{1,9},{2,10},{3,11},{4,12},{5,13},{6,14},{7,15},{8,16},{9,17... | collective-permute-start | bytes 737288 | tf_op jit(solution)/shard_map/ppermute | solution.py:465
  60.4 0.1 fusion.4
  60.5 0.7 copy.16.reach_own
  61.2 0.7 copy.17.reach_prev
  61.9 0.0 collective-permute-done.11.rest_10_
  62.0 0.0 collective-permute-done.13.rest_12_
  62.0 0.0 collective-permute-done.14.rest_13_
  62.0 3.7 %collective-permute-done.15.rest_14_ = bf16[960,128]{1,0:T(8,128)(2,1)S(1)} collective-permute-done((bf16[960,128]{1,0:T(8,128)(2,1)S(1)}, bf16[960,128]{1,0:T(8,128)(2,1)S(1)}, u32[]{:S(2)}, u32[]{:S(2)}) %collective-permute-start.15) | collective-permute-done | bytes 245792 | tf_op jit(solution)/shard_map/ppermute | solution.py:465
  65.7 0.0 copy-done.15
  65.7 0.7 copy-done.16
  66.4 0.0 collective-permute-done.9.rest_8_
  66.5 45.4 %cross.1 = (f32[2,2,2,480,128]{4,3,2,1,0:T(8,128)}, bf16[1920,128]{1,0:T(8,128)(2,1)}) custom-call(s32[128,1]{1,0:T(8,128)} %copy.16.reach_own, s32[128,1]{1,0:T(8,128)} %copy.17.reach_prev, bf16[128,128]{1,0:T(8,128)(2,1)} %constant.85.clone.rest_0_, bf16[16,16,256]{2,1,0:T(8,128)(2,1)} %constant.86.clone.rest_1_, ...), custom_call_target="tpu_custom_call" | custom-call | flops 30000001024 | bytes 6000000 | tf_op jit(solution)/shard_map/cross/pallas_call | solution.py:359
  111.9 0.0 copy-start.1
  111.9 2.7 %dynamic-slice_bitcast_fusion = (f32[2,2,480,128]{3,2,1,0:T(8,128)S(1)}, f32[2,2,480,128]{3,2,1,0:T(8,128)}) fusion(f32[2,2,2,480,128]{4,3,2,1,0:T(8,128)} %get-tuple-element.15, s32[]{:T(128)S(6)} %select_n.42, s32[]{:T(128)S(6)} %select_n.41), kind=kLoop, calls=%fused_computation | loop fusion | bytes 3932168 | tf_op jit(solution)/shard_map/jit(dynamic_index_in_dim)/squeeze | solution.py:497
  114.6 2.6 %collective-permute-start.16 = (f32[2,2,480,128]{3,2,1,0:T(8,128)S(1)}, f32[2,2,480,128]{3,2,1,0:T(8,128)S(1)}, u32[]{:S(2)}, u32[]{:S(2)}) collective-permute-start(f32[2,2,480,128]{3,2,1,0:T(8,128)S(1)} %get-tuple-element.17), channel_id=1, source_target_pairs={{0,4},{1,5},{2,6},{3,7},{4,0},{5,1},{6,2},{7,3},{8,12},{9,13},{10,... | collective-permute-start | bytes 2949128 | tf_op jit(solution)/shard_map/ppermute | solution.py:465
  117.1 0.1 pad_dynamic-slice_fusion
  117.2 0.1 reshape.32
  117.3 0.2 reshape.33
  117.5 0.1 dynamic_slice.36
  117.6 2.2 %collective-permute-start.17 = (bf16[960,128]{1,0:T(8,128)(2,1)S(1)}, bf16[960,128]{1,0:T(8,128)(2,1)S(1)}, u32[]{:S(2)}, u32[]{:S(2)}) collective-permute-start(bf16[960,128]{1,0:T(8,128)(2,1)S(1)} %bitcast.23), channel_id=1, source_target_pairs={{8,0},{9,1},{10,2},{11,3},{12,4},{13,5},{14,6},{15,7},{16,8},{17,9... | collective-permute-start | bytes 737288 | tf_op jit(solution)/shard_map/ppermute | solution.py:465
  119.8 1.9 %collective-permute-start.18 = (bf16[960,128]{1,0:T(8,128)(2,1)S(1)}, bf16[960,128]{1,0:T(8,128)(2,1)S(1)}, u32[]{:S(2)}, u32[]{:S(2)}) collective-permute-start(bf16[960,128]{1,0:T(8,128)(2,1)S(1)} %bitcast.22), channel_id=1, source_target_pairs={{8,4},{9,5},{10,6},{11,7},{12,0},{13,1},{14,2},{15,3},{16,12},{17,... | collective-permute-start | bytes 737288 | tf_op jit(solution)/shard_map/ppermute | solution.py:465
  121.8 0.1 fusion.2
  121.9 0.6 broadcast_maximum_fusion
  122.5 4.7 %collective-permute-done.17.far_a = bf16[960,128]{1,0:T(8,128)(2,1)S(1)} collective-permute-done((bf16[960,128]{1,0:T(8,128)(2,1)S(1)}, bf16[960,128]{1,0:T(8,128)(2,1)S(1)}, u32[]{:S(2)}, u32[]{:S(2)}) %collective-permute-start.17) | collective-permute-done | bytes 245792 | tf_op jit(solution)/shard_map/ppermute | solution.py:465
  127.1 5.4 %collective-permute-done.18.far_b = bf16[960,128]{1,0:T(8,128)(2,1)S(1)} collective-permute-done((bf16[960,128]{1,0:T(8,128)(2,1)S(1)}, bf16[960,128]{1,0:T(8,128)(2,1)S(1)}, u32[]{:S(2)}, u32[]{:S(2)}) %collective-permute-start.18) | collective-permute-done | bytes 245792 | tf_op jit(solution)/shard_map/ppermute | solution.py:465
  132.5 0.0 collective-permute-done.16.theirs
  132.5 0.7 copy-done.3
  133.2 0.3 copy-done
  133.5 3.2 %finish.1 = f32[2,960,256]{2,1,0:T(8,128)} custom-call(s32[2]{0:T(128)} %pad_add_fusion.meta, f32[2,2,480,128]{3,2,1,0:T(8,128)} %get-tuple-element.18.mine, f32[2,2,480,128]{3,2,1,0:T(8,128)} %copy-done, bf16[960,128]{1,0:T(8,128)(2,1)} %copy-done.2, bf16[960,128]{1,0:T(8,128)(2,1)} %copy-done.3, f32[1,256]{1,0:T(1,128)} %bitcast.24), custom_call_target="tpu_custom_call" | custom-call | tf_op jit(solution)/shard_map/finish/pallas_call | solution.py:420
  (36 shorter events, 0.1 us)
Async XLA Ops:
  0.0 15.1 %collective-permute-start = (bf16[64,7680]{1,0:T(8,128)(2,1)}, bf16[64,7680]{1,0:T(8,128)(2,1)S(1)}, u32[]{:S(2)}, u32[]{:S(2)}) collective-permute-start(bf16[64,7680]{1,0:T(8,128)(2,1)} %own.1), channel_id=1, source_target_pairs={{0,4},{1,5},{2,6},{3,7},{4,0},{5,1},{6,2},{7,3},{8,12},{9,13},{10,... | collective-permute-start | bytes 2949128 | tf_op jit(solution)/shard_map/ppermute | solution.py:465
  1.5 11.0 %collective-permute-start.1 = (bf16[64,256]{1,0:T(8,128)(2,1)S(1)}, bf16[64,256]{1,0:T(8,128)(2,1)S(1)}, u32[]{:S(2)}, u32[]{:S(2)}) collective-permute-start(bf16[64,256]{1,0:T(8,128)(2,1)S(1)} %get-tuple-element.20), channel_id=1, source_target_pairs={{0,1},{1,2},{2,3},{4,5},{5,6},{6,7},{8,9},{9,10},{10,11},{12,13},{... | collective-permute-start | bytes 98312 | tf_op jit(solution)/shard_map/ppermute | solution.py:465
  4.6 7.9 %collective-permute-start.2 = (bf16[64,256]{1,0:T(8,128)(2,1)S(1)}, bf16[64,256]{1,0:T(8,128)(2,1)S(1)}, u32[]{:S(2)}, u32[]{:S(2)}) collective-permute-start(bf16[64,256]{1,0:T(8,128)(2,1)S(1)} %get-tuple-element.20), channel_id=1, source_target_pairs={{0,5},{1,6},{2,7},{4,1},{5,2},{6,3},{8,13},{9,14},{10,15},{12,9},{... | collective-permute-start | bytes 98312 | tf_op jit(solution)/shard_map/ppermute | solution.py:465
  7.9 4.7 %collective-permute-start.3 = (bf16[64,256]{1,0:T(8,128)(2,1)S(1)}, bf16[64,256]{1,0:T(8,128)(2,1)S(1)}, u32[]{:S(2)}, u32[]{:S(2)}) collective-permute-start(bf16[64,256]{1,0:T(8,128)(2,1)S(1)} %get-tuple-element.19), channel_id=1, source_target_pairs={{1,0},{2,1},{3,2},{5,4},{6,5},{7,6},{9,8},{10,9},{11,10},{13,12},{... | collective-permute-start | bytes 98312 | tf_op jit(solution)/shard_map/ppermute | solution.py:465
  9.2 6.0 %collective-permute-start.4 = (bf16[64,256]{1,0:T(8,128)(2,1)S(1)}, bf16[64,256]{1,0:T(8,128)(2,1)S(1)}, u32[]{:S(2)}, u32[]{:S(2)}) collective-permute-start(bf16[64,256]{1,0:T(8,128)(2,1)S(1)} %get-tuple-element.19), channel_id=1, source_target_pairs={{1,4},{2,5},{3,6},{5,0},{6,1},{7,2},{9,12},{10,13},{11,14},{13,8},... | collective-permute-start | bytes 98312 | tf_op jit(solution)/shard_map/ppermute | solution.py:465
  12.5 47.9 %copy-start.5 = (s32[512]{0:T(512)S(1)}, s32[512]{0:T(512)}, u32[]{:S(2)}) copy-start(s32[512]{0:T(512)} %param.13) | copy-start | bytes 6148
  12.5 2.7 %copy-start.17 = (bf16[64,256]{1,0:T(8,128)(2,1)}, bf16[64,256]{1,0:T(8,128)(2,1)S(1)}, u32[]{:S(2)}) copy-start(bf16[64,256]{1,0:T(8,128)(2,1)S(1)} %collective-permute-done.1.lo_own) | copy-start | bytes 98308
  12.5 2.7 %copy-start.18 = (bf16[64,256]{1,0:T(8,128)(2,1)}, bf16[64,256]{1,0:T(8,128)(2,1)S(1)}, u32[]{:S(2)}) copy-start(bf16[64,256]{1,0:T(8,128)(2,1)S(1)} %collective-permute-done.2.lo_other) | copy-start | bytes 98308
  12.5 2.6 %copy-start.19 = (bf16[64,256]{1,0:T(8,128)(2,1)}, bf16[64,256]{1,0:T(8,128)(2,1)S(1)}, u32[]{:S(2)}) copy-start(bf16[64,256]{1,0:T(8,128)(2,1)S(1)} %collective-permute-done.3.hi_own) | copy-start | bytes 98308
  15.1 0.6 copy-start.20
  15.7 0.9 copy-start.6
  30.1 14.0 %collective-permute-start.6 = (bf16[960,128]{1,0:T(8,128)(2,1)}, bf16[960,128]{1,0:T(8,128)(2,1)S(1)}, u32[]{:S(2)}, u32[]{:S(2)}) collective-permute-start(bf16[960,128]{1,0:T(8,128)(2,1)} %get-tuple-element.13), channel_id=1, source_target_pairs={{0,2},{1,3},{2,0},{3,1},{4,6},{5,7},{6,4},{7,5},{8,10},{9,11},{10,... | collective-permute-start | bytes 737288 | tf_op jit(solution)/shard_map/ppermute | solution.py:465
  32.7 14.7 %collective-permute-start.7 = (bf16[960,128]{1,0:T(8,128)(2,1)}, bf16[960,128]{1,0:T(8,128)(2,1)S(1)}, u32[]{:S(2)}, u32[]{:S(2)}) collective-permute-start(bf16[960,128]{1,0:T(8,128)(2,1)} %get-tuple-element.14), channel_id=1, source_target_pairs={{0,3},{1,2},{2,1},{3,0},{4,7},{5,6},{6,5},{7,4},{8,11},{9,10},{10,... | collective-permute-start | bytes 737288 | tf_op jit(solution)/shard_map/ppermute | solution.py:465
  33.8 15.7 %collective-permute-start.5 = (bf16[960,128]{1,0:T(8,128)(2,1)}, bf16[960,128]{1,0:T(8,128)(2,1)S(1)}, u32[]{:S(2)}, u32[]{:S(2)}) collective-permute-start(bf16[960,128]{1,0:T(8,128)(2,1)} %get-tuple-element.12), channel_id=1, source_target_pairs={{0,1},{1,0},{2,3},{3,2},{4,5},{5,4},{6,7},{7,6},{8,9},{9,8},{10,11... | collective-permute-start | bytes 737288 | tf_op jit(solution)/shard_map/ppermute | solution.py:465
  33.9 18.8 %collective-permute-start.12 = (bf16[960,128]{1,0:T(8,128)(2,1)}, bf16[960,128]{1,0:T(8,128)(2,1)S(1)}, u32[]{:S(2)}, u32[]{:S(2)}) collective-permute-start(bf16[960,128]{1,0:T(8,128)(2,1)} %get-tuple-element.11.rest_3_), channel_id=1, source_target_pairs={{8,0},{9,1},{10,2},{11,3},{12,4},{13,5},{14,6},{15,7},{16,8},{17,9... | collective-permute-start | bytes 737288 | tf_op jit(solution)/shard_map/ppermute | solution.py:465
  36.0 18.8 %collective-permute-start.8 = (bf16[960,128]{1,0:T(8,128)(2,1)}, bf16[960,128]{1,0:T(8,128)(2,1)S(1)}, u32[]{:S(2)}, u32[]{:S(2)}) collective-permute-start(bf16[960,128]{1,0:T(8,128)(2,1)} %get-tuple-element.11.rest_3_), channel_id=1, source_target_pairs={{0,8},{1,9},{2,10},{3,11},{4,12},{5,13},{6,14},{7,15},{8,16},{9,17... | collective-permute-start | bytes 737288 | tf_op jit(solution)/shard_map/ppermute | solution.py:465
  44.2 22.3 %copy-start.7 = (bf16[960,128]{1,0:T(8,128)(2,1)}, bf16[960,128]{1,0:T(8,128)(2,1)S(1)}, u32[]{:S(2)}) copy-start(bf16[960,128]{1,0:T(8,128)(2,1)S(1)} %collective-permute-done.6.rest_5_) | copy-start | bytes 737284
  44.2 12.6 %collective-permute-start.10 = (bf16[960,128]{1,0:T(8,128)(2,1)S(1)}, bf16[960,128]{1,0:T(8,128)(2,1)S(1)}, u32[]{:S(2)}, u32[]{:S(2)}) collective-permute-start(bf16[960,128]{1,0:T(8,128)(2,1)S(1)} %collective-permute-done.6.rest_5_), channel_id=1, source_target_pairs={{0,8},{1,9},{2,10},{3,11},{4,12},{5,13},{6,14},{7,15},{8,16},{9,17... | collective-permute-start | bytes 737288 | tf_op jit(solution)/shard_map/ppermute | solution.py:465
  47.4 19.1 %copy-start.8 = (bf16[960,128]{1,0:T(8,128)(2,1)}, bf16[960,128]{1,0:T(8,128)(2,1)S(1)}, u32[]{:S(2)}) copy-start(bf16[960,128]{1,0:T(8,128)(2,1)S(1)} %collective-permute-done.7.rest_6_) | copy-start | bytes 737284
  47.4 14.6 %collective-permute-start.14 = (bf16[960,128]{1,0:T(8,128)(2,1)S(1)}, bf16[960,128]{1,0:T(8,128)(2,1)S(1)}, u32[]{:S(2)}, u32[]{:S(2)}) collective-permute-start(bf16[960,128]{1,0:T(8,128)(2,1)S(1)} %collective-permute-done.6.rest_5_), channel_id=1, source_target_pairs={{8,0},{9,1},{10,2},{11,3},{12,4},{13,5},{14,6},{15,7},{16,8},{17,9... | collective-permute-start | bytes 737288 | tf_op jit(solution)/shard_map/ppermute | solution.py:465
  49.5 16.9 %copy-start.9 = (bf16[960,128]{1,0:T(8,128)(2,1)}, bf16[960,128]{1,0:T(8,128)(2,1)S(1)}, u32[]{:S(2)}) copy-start(bf16[960,128]{1,0:T(8,128)(2,1)S(1)} %collective-permute-done.5.rest_4_) | copy-start | bytes 737284
  49.5 12.5 %collective-permute-start.11 = (bf16[960,128]{1,0:T(8,128)(2,1)S(1)}, bf16[960,128]{1,0:T(8,128)(2,1)S(1)}, u32[]{:S(2)}, u32[]{:S(2)}) collective-permute-start(bf16[960,128]{1,0:T(8,128)(2,1)S(1)} %collective-permute-done.7.rest_6_), channel_id=1, source_target_pairs={{0,8},{1,9},{2,10},{3,11},{4,12},{5,13},{6,14},{7,15},{8,16},{9,17... | collective-permute-start | bytes 737288 | tf_op jit(solution)/shard_map/ppermute | solution.py:465
  52.7 13.7 %copy-start.10 = (bf16[960,128]{1,0:T(8,128)(2,1)}, bf16[960,128]{1,0:T(8,128)(2,1)S(1)}, u32[]{:S(2)}) copy-start(bf16[960,128]{1,0:T(8,128)(2,1)S(1)} %collective-permute-done.12.rest_11_) | copy-start | bytes 737284
  52.7 9.2 %collective-permute-start.13 = (bf16[960,128]{1,0:T(8,128)(2,1)S(1)}, bf16[960,128]{1,0:T(8,128)(2,1)S(1)}, u32[]{:S(2)}, u32[]{:S(2)}) collective-permute-start(bf16[960,128]{1,0:T(8,128)(2,1)S(1)} %collective-permute-done.5.rest_4_), channel_id=1, source_target_pairs={{8,0},{9,1},{10,2},{11,3},{12,4},{13,5},{14,6},{15,7},{16,8},{17,9... | collective-permute-start | bytes 737288 | tf_op jit(solution)/shard_map/ppermute | solution.py:465
  54.8 11.6 %copy-start.11 = (bf16[960,128]{1,0:T(8,128)(2,1)}, bf16[960,128]{1,0:T(8,128)(2,1)S(1)}, u32[]{:S(2)}) copy-start(bf16[960,128]{1,0:T(8,128)(2,1)S(1)} %collective-permute-done.8.rest_7_) | copy-start | bytes 737284
  54.8 10.8 %collective-permute-start.15 = (bf16[960,128]{1,0:T(8,128)(2,1)S(1)}, bf16[960,128]{1,0:T(8,128)(2,1)S(1)}, u32[]{:S(2)}, u32[]{:S(2)}) collective-permute-start(bf16[960,128]{1,0:T(8,128)(2,1)S(1)} %collective-permute-done.7.rest_6_), channel_id=1, source_target_pairs={{8,0},{9,1},{10,2},{11,3},{12,4},{13,5},{14,6},{15,7},{16,8},{17,9... | collective-permute-start | bytes 737288 | tf_op jit(solution)/shard_map/ppermute | solution.py:465
  56.8 9.7 %copy-start.12 = (bf16[960,128]{1,0:T(8,128)(2,1)}, bf16[960,128]{1,0:T(8,128)(2,1)S(1)}, u32[]{:S(2)}) copy-start(bf16[960,128]{1,0:T(8,128)(2,1)S(1)} %collective-permute-done.10.rest_9_) | copy-start | bytes 737284
  56.8 9.6 %collective-permute-start.9 = (bf16[960,128]{1,0:T(8,128)(2,1)S(1)}, bf16[960,128]{1,0:T(8,128)(2,1)}, u32[]{:S(2)}, u32[]{:S(2)}) collective-permute-start(bf16[960,128]{1,0:T(8,128)(2,1)S(1)} %collective-permute-done.5.rest_4_), channel_id=1, source_target_pairs={{0,8},{1,9},{2,10},{3,11},{4,12},{5,13},{6,14},{7,15},{8,16},{9,17... | collective-permute-start | bytes 737288 | tf_op jit(solution)/shard_map/ppermute | solution.py:465
  61.9 3.7 %copy-start.14 = (bf16[960,128]{1,0:T(8,128)(2,1)}, bf16[960,128]{1,0:T(8,128)(2,1)S(1)}, u32[]{:S(2)}) copy-start(bf16[960,128]{1,0:T(8,128)(2,1)S(1)} %collective-permute-done.11.rest_10_) | copy-start | bytes 737284
  62.0 3.7 %copy-start.15 = (bf16[960,128]{1,0:T(8,128)(2,1)}, bf16[960,128]{1,0:T(8,128)(2,1)S(1)}, u32[]{:S(2)}) copy-start(bf16[960,128]{1,0:T(8,128)(2,1)S(1)} %collective-permute-done.13.rest_12_) | copy-start | bytes 737284
  62.0 4.5 %copy-start.13 = (bf16[960,128]{1,0:T(8,128)(2,1)}, bf16[960,128]{1,0:T(8,128)(2,1)S(1)}, u32[]{:S(2)}) copy-start(bf16[960,128]{1,0:T(8,128)(2,1)S(1)} %collective-permute-done.14.rest_13_) | copy-start | bytes 737284
  65.7 0.7 copy-start.16
  111.9 5.2 %copy-start.4 = (s32[512]{0:T(512)S(1)}, s32[512]{0:T(512)}, u32[]{:S(2)}) copy-start(s32[512]{0:T(512)} %param.12) | copy-start | bytes 6148
  111.9 5.7 %copy-start.1 = (bf16[1920,128]{1,0:T(8,128)(2,1)S(1)}, bf16[1920,128]{1,0:T(8,128)(2,1)}, u32[]{:S(2)}) copy-start(bf16[1920,128]{1,0:T(8,128)(2,1)} %get-tuple-element.16) | copy-start | bytes 1474564
  114.6 17.9 %collective-permute-start.16 = (f32[2,2,480,128]{3,2,1,0:T(8,128)S(1)}, f32[2,2,480,128]{3,2,1,0:T(8,128)S(1)}, u32[]{:S(2)}, u32[]{:S(2)}) collective-permute-start(f32[2,2,480,128]{3,2,1,0:T(8,128)S(1)} %get-tuple-element.17), channel_id=1, source_target_pairs={{0,4},{1,5},{2,6},{3,7},{4,0},{5,1},{6,2},{7,3},{8,12},{9,13},{10,... | collective-permute-start | bytes 2949128 | tf_op jit(solution)/shard_map/ppermute | solution.py:465
  117.6 9.5 %collective-permute-start.17 = (bf16[960,128]{1,0:T(8,128)(2,1)S(1)}, bf16[960,128]{1,0:T(8,128)(2,1)S(1)}, u32[]{:S(2)}, u32[]{:S(2)}) collective-permute-start(bf16[960,128]{1,0:T(8,128)(2,1)S(1)} %bitcast.23), channel_id=1, source_target_pairs={{8,0},{9,1},{10,2},{11,3},{12,4},{13,5},{14,6},{15,7},{16,8},{17,9... | collective-permute-start | bytes 737288 | tf_op jit(solution)/shard_map/ppermute | solution.py:465
  119.8 12.7 %collective-permute-start.18 = (bf16[960,128]{1,0:T(8,128)(2,1)S(1)}, bf16[960,128]{1,0:T(8,128)(2,1)S(1)}, u32[]{:S(2)}, u32[]{:S(2)}) collective-permute-start(bf16[960,128]{1,0:T(8,128)(2,1)S(1)} %bitcast.22), channel_id=1, source_target_pairs={{8,4},{9,5},{10,6},{11,7},{12,0},{13,1},{14,2},{15,3},{16,12},{17,... | collective-permute-start | bytes 737288 | tf_op jit(solution)/shard_map/ppermute | solution.py:465
  127.1 5.4 %copy-start.2 = (bf16[960,128]{1,0:T(8,128)(2,1)}, bf16[960,128]{1,0:T(8,128)(2,1)S(1)}, u32[]{:S(2)}) copy-start(bf16[960,128]{1,0:T(8,128)(2,1)S(1)} %collective-permute-done.17.far_a) | copy-start | bytes 737284
  132.5 0.7 copy-start.3
  132.5 1.0 copy-start

commit v3 on v2

--- a/solution.py
+++ b/solution.py
@@ -70,6 +70,7 @@
 def spectra_kernel(
     count_a,
     n_freq,
+    chunks,
     meta,
     own,
     other,
@@ -85,8 +86,8 @@
     quality,
     *rest,
 ):
-    outs = rest[:n_freq]
-    padded, filtered, magnitude, whitened, tw_re, tw_im = rest[n_freq:]
+    outs = rest[: n_freq * len(chunks)]
+    padded, filtered, magnitude, whitened, tw_re, tw_im = rest[len(outs) :]
     core, band = meta[0], meta[1]
     ch = own.shape[0]
     both = 2 * ch
@@ -151,10 +152,10 @@
     scale = quality[...] * (1.0 / math.sqrt(count_a * TBLK))
     turn = jnp.concatenate([second[band ^ d, core] for d in range(n_freq)], axis=0)
 
-    def bins(i, carry):
+    def bins(k, start, i):
         results = []
         for n in range(group):
-            k1 = i * group + n
+            k1 = (start + i) * group + n
             re = tw_re[pl.ds(k1, both, stride=pad_a), :].astype(jnp.bfloat16)
             im = tw_im[pl.ds(k1, both, stride=pad_a), :].astype(jnp.bfloat16)
             result = lax.dot_general(
@@ -164,31 +165,36 @@
                 preferred_element_type=jnp.float32,
             )
             results.append(result * scale)
-        rows = pl.ds(pl.multiple_of(i * group * rk, 16), group * rk)
+        rows = pl.ds(i * group * rk, group * rk)
         for d in range(n_freq):
             starts = [d * rk + p * half for p in range(2)]
             block = jnp.concatenate([r[s : s + half] for s in starts for r in results], axis=0)
-            outs[d][rows, :] = block.astype(jnp.bfloat16)
-        return carry
-
-    lax.fori_loop(0, count_a // group, bins, 0, unroll=True)
-
-
-def spectra(meta, own, other, halos, quality, n_freq):
+            outs[k * n_freq + d][rows, :] = block.astype(jnp.bfloat16)
+
+    start = 0
+    for k, size in enumerate(chunks):
+        for i in range(size):
+            bins(k, start, i)
+        start += size
+
+
+def spectra(meta, own, other, halos, quality, n_freq, chunks):
     ch, length = own.shape
     count_a = length // TBLK
     first, twist, second = dft_tables(count_a, n_freq)
     rk = second.shape[2]
     pad_a = first.shape[1]
     both = 2 * ch
+    rows = 2 * block_bins(n_freq)
+    shapes = [(size * rows, both) for size in chunks for _ in range(n_freq)]
     tables = (stencil_table(False), stencil_table(True), first, twist, second)
     operands = (own, other, *halos, *(jnp.asarray(t) for t in tables), quality)
     return pl.pallas_call(
-        functools.partial(spectra_kernel, count_a, n_freq),
+        functools.partial(spectra_kernel, count_a, n_freq, chunks),
         grid=(1,),
-        out_shape=[jax.ShapeDtypeStruct((count_a * rk, both), jnp.bfloat16)] * n_freq,
+        out_shape=[jax.ShapeDtypeStruct(shape, jnp.bfloat16) for shape in shapes],
         in_specs=[pl.BlockSpec(memory_space=pltpu.SMEM)] + [whole(x.shape) for x in operands],
-        out_specs=[whole((count_a * rk, both))] * n_freq,
+        out_specs=[whole(shape) for shape in shapes],
         scratch_shapes=[
             pltpu.VMEM((count_a + 4, both, TBLK), jnp.bfloat16),
             pltpu.VMEM((count_a + 2, both, TBLK), jnp.float32),
@@ -205,29 +211,46 @@
     )(meta, *operands)
 
 
-def cross_kernel(n_seg, half, count_a, reach_own, reach_prev, *rest):
-    turn_ref, pick_ref, cut_ref = rest[:3]
-    own_refs = rest[3 : 3 + n_seg]
-    prev_refs = rest[3 + n_seg : 3 + 2 * n_seg]
-    next_refs = rest[3 + 2 * n_seg : 3 + 3 * n_seg]
-    near_ref, far_ref, w_near, w_far, edge, sum_one, sum_two, sum_far = rest[3 + 3 * n_seg :]
+def cross_kernel(
+    meta,
+    reach_own,
+    reach_prev,
+    turn_ref,
+    pick_ref,
+    cut_ref,
+    own_ref,
+    prev_ref,
+    next_ref,
+    mine_ref,
+    theirs_ref,
+    far_mine_ref,
+    far_theirs_ref,
+    w_near,
+    w_far,
+    edge,
+    sum_one,
+    sum_two,
+    sum_far,
+):
     step = pl.program_id(0)
-    both = own_refs[0].shape[1]
+    n_seg, rb, both = own_ref.shape
     depth = turn_ref.shape[0]
     nb = pick_ref.shape[0]
-    nk1 = nb // half
     slabs = both // 8
-    rb = 2 * nb
-    block = pl.ds(pl.multiple_of(step * rb, rb), rb)
+    first_core = meta[0] == 0
 
     @pl.when(step == 0)
     def _():
         row = lax.broadcasted_iota(jnp.int32, (16, both), 0) % 8
         col = lax.broadcasted_iota(jnp.int32, (16, both), 1)
-        offset = both + col - row
+        offset = (both + col - row).astype(jnp.float32)
+        columns = [
+            jnp.broadcast_to(r[...], (both, both)).T for r in (reach_own, reach_prev)
+        ]
+        wide = jnp.concatenate([columns[1], columns[1]], axis=1)
         for a in range(slabs):
-            mine = reach_own[a * 8 : a * 8 + 8, :]
-            lent = reach_prev[a * 8 : a * 8 + 8, :]
+            mine = columns[0][a * 8 : a * 8 + 8]
+            lent = columns[1][a * 8 : a * 8 + 8]
             mine = jnp.concatenate([mine, mine], axis=0)
             lent = jnp.concatenate([lent, lent], axis=0)
             inner = col < both - 8 * a
@@ -238,11 +261,8 @@
         same = (row // (both // 2)) == (col // both)
         for d in range(1, 8):
             hit = same & (col % both == both - d) & (row % 8 >= d)
-            hit = hit & (2 * both - d < reach_prev[...])
+            hit = hit & (2 * both - d < wide)
             edge[(d - 1) * both : d * both, :] = jnp.where(hit, 1.0, 0.0).astype(jnp.bfloat16)
-
-    def stacked(refs):
-        return jnp.concatenate([r[block, :] for r in refs], axis=0)
 
     def left_rows(block):
         re = block.astype(jnp.float32).T.astype(jnp.bfloat16)
@@ -251,9 +271,7 @@
         im = im.reshape(slabs, 8, depth)
         return jnp.stack([re, im], axis=1).reshape(slabs, 16, depth).astype(jnp.bfloat16)
 
-    own = stacked(own_refs)
-    nxt = stacked(next_refs)
-    prev = stacked(prev_refs)
+    own, nxt, prev = (r[...].reshape(depth, both) for r in (own_ref, next_ref, prev_ref))
     left = jnp.concatenate([left_rows(own), left_rows(prev)], axis=2)
     pick = pick_ref[...]
 
@@ -294,12 +312,11 @@
             sum_two[g] += near
             sum_far[g] += far
 
-    def split(ref):
-        x = ref[block, :].astype(jnp.float32)
+    def split(x):
         return x[:nb], x[nb:]
 
-    lefts = [split(r) for r in prev_refs]
-    rights = [split(r) for r in next_refs]
+    lefts = [split(prev_ref[s].astype(jnp.float32)) for s in range(n_seg)]
+    rights = [split(next_ref[s].astype(jnp.float32)) for s in range(n_seg)]
     pieces = []
     for d in range(1, 8):
         re = im = None
@@ -313,9 +330,9 @@
     )
 
     lane = lax.broadcasted_iota(jnp.int32, (nb, both), 1)
-    far_parts = []
-    for g in range(2):
-        for p in range(2):
+    for p in range(2):
+        values = []
+        for g in range(2):
             low = high = far = None
             for b in range(8):
                 rows = pl.ds(p * 8 + b, nb, stride=16)
@@ -326,19 +343,21 @@
                 low += pltpu.roll(jnp.where(lane >= b, one, two), both - b, 1)
                 high += pltpu.roll(jnp.where(lane >= b, two, 0.0), both - b, 1)
                 far += pltpu.roll(three, both - b, 1)
-            for r, value in enumerate((low, high)):
-                for n in range(nk1):
-                    near_ref[g, p, r, pl.ds(step * nk1 + n, half, stride=count_a), :] = value[
-                        n * half : (n + 1) * half
-                    ]
-            far_parts.append(far + margin[p * nb : (p + 1) * nb, g * both : (g + 1) * both])
-    far_ref[...] = jnp.concatenate(far_parts, axis=0).astype(jnp.bfloat16)
-
-
-def cross(own, prev, nxt, reach_own, reach_prev, count_a, rk):
-    n_seg = len(own)
-    rows, both = own[0].shape
-    half = rk // 2
+            far += margin[p * nb : (p + 1) * nb, g * both : (g + 1) * both]
+            values.append((low, high, far))
+        mine = [jnp.where(first_core, x, y) for x, y in zip(*values)]
+        theirs = [jnp.where(first_core, y, x) for x, y in zip(*values)]
+        for near_ref, far_ref, value in (
+            (mine_ref, far_mine_ref, mine),
+            (theirs_ref, far_theirs_ref, theirs),
+        ):
+            near_ref[p, 0, :nb] = value[0]
+            near_ref[p, 0, nb:] = value[1]
+            far_ref[p, 0] = value[2].astype(jnp.bfloat16)
+
+
+def cross(meta, own, prev, nxt, reach_own, reach_prev):
+    n_seg, rows, both = own.shape
     nb = block_bins(n_seg)
     rb = 2 * nb
     depth = n_seg * rb
@@ -354,20 +373,20 @@
     cut = np.arange(both) < both - 8 * np.arange(slabs)[:, None, None]
     cut = np.broadcast_to(cut, (slabs, 16, both))
     tables = [jnp.asarray(x.astype(ml_dtypes.bfloat16)) for x in (turn, pick, cut)]
-    operands = (reach_own, reach_prev, *tables, *own, *prev, *nxt)
-    far_rows = 4 * nb
+    fixed = (reach_own, reach_prev, *tables)
+    near = jax.ShapeDtypeStruct((2, steps, 2 * nb, both), jnp.float32)
+    far = jax.ShapeDtypeStruct((2, steps, nb, both), jnp.bfloat16)
+    near_spec = pl.BlockSpec((2, 1, 2 * nb, both), lambda t: (0, t, 0, 0))
+    far_spec = pl.BlockSpec((2, 1, nb, both), lambda t: (0, t, 0, 0))
+    block = pl.BlockSpec((n_seg, rb, both), lambda t: (0, t, 0))
     return pl.pallas_call(
-        functools.partial(cross_kernel, n_seg, half, count_a),
+        cross_kernel,
         grid=(steps,),
-        out_shape=[
-            jax.ShapeDtypeStruct((2, 2, 2, rows // 2, both), jnp.float32),
-            jax.ShapeDtypeStruct((steps * far_rows, both), jnp.bfloat16),
-        ],
-        in_specs=[whole(x.shape) for x in operands],
-        out_specs=[
-            whole((2, 2, 2, rows // 2, both)),
-            pl.BlockSpec((far_rows, both), lambda t: (t, 0)),
-        ],
+        out_shape=[near, near, far, far],
+        in_specs=[pl.BlockSpec(memory_space=pltpu.SMEM)]
+        + [whole(x.shape) for x in fixed]
+        + [block] * 3,
+        out_specs=[near_spec, near_spec, far_spec, far_spec],
         scratch_shapes=[
             pltpu.VMEM((slabs, 16, both), jnp.float32),
             pltpu.VMEM((slabs, 16, both), jnp.float32),
@@ -380,53 +399,54 @@
             dimension_semantics=("arbitrary",), vmem_limit_bytes=62 * MIB
         ),
         cost_estimate=pl.CostEstimate(
-            flops=30 * 10**9, bytes_accessed=6 * 10**6, transcendentals=0
+            flops=10**9 * steps, bytes_accessed=2 * 10**5 * steps, transcendentals=0
         ),
         name="cross",
-    )(*operands)
-
-
-def finish_kernel(rk, count_a, nb, meta, mine, theirs, far_a, far_b, count, out_ref, total):
+    )(meta, *fixed, own, prev, nxt)
+
+
+def finish_kernel(count_a, half, chunks, meta, count, *rest):
+    parts, out_ref, stage = rest[: 4 * chunks], rest[4 * chunks], rest[4 * chunks + 1]
     core = meta[0]
-    half = rk // 2
-    nk1 = nb // half
-    bins = mine.shape[2]
+    bins = out_ref.shape[1] // 2
     inverse = 1.0 / count[...]
-    both = far_a.shape[1]
-    for which, (near, far) in enumerate(((mine, far_a), (theirs, far_b))):
-        at = core if which == 0 else 1 - core
-        rows = pl.ds(pl.multiple_of(at * bins, bins), bins)
-        for p in range(2):
-            total[p] = near[p, 1]
-
-        def add(t, carry):
-            for p in range(2):
-                start = pl.multiple_of((t * 2 + p) * nb, nb)
-                value = far[pl.ds(start, nb), :].astype(jnp.float32)
-                for n in range(nk1):
-                    place = pl.ds(t * nk1 + n, half, stride=count_a)
-                    total[p, place, :] += value[n * half : (n + 1) * half]
-            return carry
-
-        lax.fori_loop(0, bins // nb, add, 0, unroll=True)
-        for p in range(2):
-            out_ref[p, rows, :both] = near[p, 0] * inverse[:, :both]
-            out_ref[p, rows, both:] = total[p] * inverse[:, both:]
-
-
-def finish(meta, mine, theirs, far_a, far_b, count, count_a, rk, nb):
-    bins = mine.shape[2]
-    operands = (mine, theirs, far_a, far_b, count)
+    k1 = 0
+    for chunk in range(chunks):
+        mine, theirs, far_mine, far_theirs = parts[4 * chunk : 4 * chunk + 4]
+        steps, nb, both = far_mine.shape[1:]
+        for t in range(steps):
+            for which, (near, far) in enumerate(((mine, far_mine), (theirs, far_theirs))):
+                base = (core if which == 0 else 1 - core) * bins
+                value = near[0, t]
+                low = value[:nb] * inverse[:, :both]
+                high = (value[nb:] + far[0, t].astype(jnp.float32)) * inverse[:, both:]
+                for r, x in enumerate((low, high)):
+                    for n in range(nb // half):
+                        place = pl.ds(base + k1 + n, half, stride=count_a)
+                        stage[r, place, :] = x[n * half : (n + 1) * half]
+            k1 += nb // half
+    for r in range(2):
+        both = stage.shape[2]
+        out_ref[0, :, r * both : (r + 1) * both] = stage[r]
+
+
+def finish(meta, count, parts, count_a, half):
+    bins = count_a * half
+
+    def half_of(shape):
+        return pl.BlockSpec((1,) + shape[1:], lambda p: (p,) + (0,) * (len(shape) - 1))
+
     return pl.pallas_call(
-        functools.partial(finish_kernel, rk, count_a, nb),
-        grid=(1,),
+        functools.partial(finish_kernel, count_a, half, len(parts) // 4),
+        grid=(2,),
         out_shape=jax.ShapeDtypeStruct((2, 2 * bins, BAND), jnp.float32),
-        in_specs=[pl.BlockSpec(memory_space=pltpu.SMEM)] + [whole(x.shape) for x in operands],
-        out_specs=whole((2, 2 * bins, BAND)),
-        scratch_shapes=[pltpu.VMEM((2, bins, TBLK), jnp.float32)],
+        in_specs=[pl.BlockSpec(memory_space=pltpu.SMEM), whole(count.shape)]
+        + [half_of(x.shape) for x in parts],
+        out_specs=half_of((2, 2 * bins, BAND)),
+        scratch_shapes=[pltpu.VMEM((2, 2 * bins, TBLK), jnp.float32)],
         compiler_params=pltpu.CompilerParams(vmem_limit_bytes=62 * MIB),
         name="finish",
-    )(meta, *operands)
+    )(meta, count, *parts)
 
 
 def skew_rows(matrix, keep):
@@ -476,31 +496,38 @@
     quality_pad = jnp.pad(quality, (0, BAND + both))
     reach_pad = jnp.pad(offset_reach, (both, 0))
     quality_both = lax.dynamic_slice_in_dim(quality_pad, chip * both, both, 0)
-    reach_own = lax.dynamic_slice_in_dim(reach_pad, (chip + 1) * both, both, 0)[:, None]
-    reach_prev = lax.dynamic_slice_in_dim(reach_pad, chip * both, both, 0)[:, None]
+    reach_pad = reach_pad.astype(jnp.float32)
+    reach_own = lax.dynamic_slice_in_dim(reach_pad, (chip + 1) * both, both, 0)[None, :]
+    reach_prev = lax.dynamic_slice_in_dim(reach_pad, chip * both, both, 0)[None, :]
     quality_ext = lax.dynamic_slice_in_dim(quality_pad, me * ch, ch + BAND, 0)
     count = pair_count(quality_ext, lax.dynamic_slice_in_dim(offset_reach, me * ch, ch, 0), BAND)
 
     meta = jnp.stack([core, band]).astype(jnp.int32)
-    parts = spectra(
-        meta, strain, other, halos, quality_both.astype(jnp.float32)[None, :], n_freq
+    half = rk // 2
+    steps = count_a * half // block_bins(n_freq)
+    chunks = (steps // 2, steps - steps // 2)
+    pieces = spectra(
+        meta, strain, other, halos, quality_both.astype(jnp.float32)[None, :], n_freq, chunks
     )
-    own = [parts[0]]
-    for d in range(1, n_freq):
-        own.append(moved(parts[d], lambda c, f, d=d: (c, f ^ d)))
-    nxt = [moved(x, lambda c, f: (c - 2, f)) for x in own]
-    prev = [moved(x, lambda c, f: (c + 2, f)) for x in own]
-    near, far = cross(own, prev, nxt, reach_own, reach_prev, count_a, rk)
-    nb = block_bins(n_freq)
-    steps = far.shape[0] // (4 * nb)
-    far = far.reshape(steps, 2, 2 * nb, both)
-    pick = lambda x, axis, at: lax.dynamic_index_in_dim(x, at, axis, keepdims=False)
-    theirs = moved(pick(near, 0, 1 - core), lambda c, f: (c ^ 1, f))
-    far_a = moved(pick(far, 1, core).reshape(-1, both), lambda c, f: (c - 2, f))
-    far_b = moved(pick(far, 1, 1 - core).reshape(-1, both), lambda c, f: ((c ^ 1) - 2, f))
-    mine = pick(near, 0, core)
-    out = finish(meta, mine, theirs, far_a, far_b, count[None, :], count_a, rk, nb)
-    return out[None]
+    blocks = []
+    for k in range(len(chunks)):
+        mine = pieces[k * n_freq : (k + 1) * n_freq]
+        own = [mine[0]]
+        for d in range(1, n_freq):
+            own.append(moved(mine[d], lambda c, f, d=d: (c, f ^ d)))
+        blocks.append(jnp.stack(own))
+    results = []
+    for own in blocks:
+        nxt = moved(own, lambda c, f: (c - 2, f))
+        prev = moved(own, lambda c, f: (c + 2, f))
+        mine, theirs, far_mine, far_theirs = cross(meta, own, prev, nxt, reach_own, reach_prev)
+        results += [
+            mine,
+            moved(theirs, lambda c, f: (c ^ 1, f)),
+            moved(far_mine, lambda c, f: (c - 2, f)),
+            moved(far_theirs, lambda c, f: ((c ^ 1) - 2, f)),
+        ]
+    return finish(meta, count[None, :], results, count_a, half)[None]
 
 
 def solution(mesh):

time: 139 us -> 131 us (0.942)
  waiting for transfers between devices: 21.4 us -> 14.2 us
  local copies, waits for them, and re-layouts: 8.81 us -> 5.37 us
  starting transfers between devices: 41.4 us -> 43.6 us
  other arithmetic: 2.66 us -> 4.61 us
    ppermute x19 -> x21, waiting for transfers between devices: 21.4 us -> 14.2 us  [moved(): return lax.ppermute(x, ('chan', 'freq'), pairs)]
    squeeze x1 -> x0, local copies, waits for them, and re-layouts: 2.66 us -> none  [on_device(): lax.dynamic_index_in_dim(x, at, axis, keepdims=False)]
    ppermute x19 -> x21, starting transfers between devices: 41.4 us -> 43.6 us  [moved(): return lax.ppermute(x, ('chan', 'freq'), pairs)]
    another operation x0 -> x2, other arithmetic: none -> 1.93 us  [on_device(): blocks.append(jnp.stack(own))]
    pallas_call x3 -> x4, Pallas kernels: 62 us -> 61.4 us  [the longest x2 45.3 us: cross(): pl.pallas_call(cross_kernel, grid=(steps,), out_shape=[near, near, far, f...]
    unnamed x42 -> x38, local copies, waits for them, and re-layouts: 3.3 us -> 3.47 us
  transfers between devices with their start and end apart: 19 -> 21, of which waited for: 5 -> 9; matrix products, arithmetic and copies ran while one was open for 4% -> 4% of each run, Pallas kernels for 0% -> 35%
where the time goes in v3:
time: 131 us; the launch traced here: 130 us
  Pallas kernels  61.4 us (47%)
  starting transfers between devices  43.6 us (33%)
  waiting for transfers between devices  14.2 us (11%)
  local copies, waits for them, and re-layouts  5.37 us (4%)
  other arithmetic  4.61 us (4%)
    pallas_call x2, Pallas kernels, cross(): pl.pallas_call(cross_kernel, grid=(steps,), out_shape=[near, near, far, f...  45.3 us
    ppermute x21, starting transfers between devices, moved(): return lax.ppermute(x, ('chan', 'freq'), pairs)  43.6 us
    ppermute x21, waiting for transfers between devices, moved(): return lax.ppermute(x, ('chan', 'freq'), pairs)  14.2 us
    pallas_call x1, Pallas kernels, spectra(): pl.pallas_call(functools.partial(spectra_kernel, count_a, n_freq, chunks)...  13.3 us
    unnamed x38, local copies, waits for them, and re-layouts  3.47 us
    pallas_call x1, Pallas kernels, finish(): pl.pallas_call(functools.partial(finish_kernel, count_a, half, len(parts)...  2.83 us
  transfers between devices with their start and end apart: 21, of which 9 were waited for; matrix products, arithmetic and copies ran while one was open for 4% of the time, Pallas kernels for 35%

profile of v3, /device:TPU:9, one launch (start us, length us, event | category | flops | bytes accessed | tf_op | source)
XLA Modules:
  0.0 129.7 jit_solution(8830893826436376821)
XLA Ops:
  0.0 0.7 collective-permute-start
  0.7 0.8 fusion.5
  1.5 1.3 collective-permute-start.4
  2.7 1.3 collective-permute-start.3
  4.0 4.9 %collective-permute-start.2 = (bf16[64,256]{1,0:T(8,128)(2,1)S(1)}, bf16[64,256]{1,0:T(8,128)(2,1)S(1)}, u32[]{:S(2)}, u32[]{:S(2)}) collective-permute-start(bf16[64,256]{1,0:T(8,128)(2,1)S(1)} %get-tuple-element.38), channel_id=1, source_target_pairs={{0,5},{1,6},{2,7},{4,1},{5,2},{6,3},{8,13},{9,14},{10,15},{12,9},{... | collective-permute-start | bytes 98312 | tf_op jit(solution)/shard_map/ppermute | solution.py:485
  8.9 4.5 %collective-permute-start.1 = (bf16[64,256]{1,0:T(8,128)(2,1)S(1)}, bf16[64,256]{1,0:T(8,128)(2,1)S(1)}, u32[]{:S(2)}, u32[]{:S(2)}) collective-permute-start(bf16[64,256]{1,0:T(8,128)(2,1)S(1)} %get-tuple-element.38), channel_id=1, source_target_pairs={{0,1},{1,2},{2,3},{4,5},{5,6},{6,7},{8,9},{9,10},{10,11},{12,13},{... | collective-permute-start | bytes 98312 | tf_op jit(solution)/shard_map/ppermute | solution.py:485
  13.5 0.7 pad_add_fusion.meta
  14.2 1.3 %fusion.4.quality = f32[1,128]{1,0:T(1,128)} fusion(s32[]{:T(128)S(6)} %select_n.32, s32[512]{0:T(512)} %param.15), kind=kLoop, calls=%fused_computation.11 | loop fusion | flops 128 | bytes 2564 | tf_op jit(solution)/shard_map/broadcast_in_dim | solution.py:510
  15.5 0.0 collective-permute-done.4.hi_other
  15.5 0.0 collective-permute-done.3.hi_own
  15.6 0.0 collective-permute-done.1.lo_own
  15.6 0.0 collective-permute-done.other
  15.6 0.5 copy-done.15
  16.1 0.0 copy-done.16
  16.2 0.0 copy-done.17
  16.2 0.0 copy-done.18
  16.2 0.9 copy-done.10
  17.1 13.3 %spectra.1 = (bf16[480,128]{1,0:T(8,128)(2,1)}, bf16[480,128]{1,0:T(8,128)(2,1)}, bf16[480,128]{1,0:T(8,128)(2,1)}, bf16[480,128]{1,0:T(8,128)(2,1)}, bf16[480,1...) custom-call(s32[2]{0:T(128)} %pad_add_fusion.meta, ...), custom_call_target="tpu_custom_call" | custom-call | flops 6000000000 | bytes 4000000 | tf_op jit(solution)/shard_map/spectra/pallas_call | solution.py:192
  30.4 1.2 collective-permute-start.13
  31.7 0.9 collective-permute-start.14
  32.6 1.1 collective-permute-start.15
  33.7 1.9 %collective-permute-done.13 = bf16[480,128]{1,0:T(8,128)(2,1)S(1)} collective-permute-done((bf16[480,128]{1,0:T(8,128)(2,1)}, bf16[480,128]{1,0:T(8,128)(2,1)S(1)}, u32[]{:S(2)}, u32[]{:S(2)}) %collective-permute-start.13) | collective-permute-done | bytes 122912 | tf_op jit(solution)/shard_map/ppermute | solution.py:485
  35.6 0.3 collective-permute-done.14
  36.0 3.4 %collective-permute-done.15 = bf16[480,128]{1,0:T(8,128)(2,1)S(1)} collective-permute-done((bf16[480,128]{1,0:T(8,128)(2,1)}, bf16[480,128]{1,0:T(8,128)(2,1)S(1)}, u32[]{:S(2)}, u32[]{:S(2)}) %collective-permute-start.15) | collective-permute-done | bytes 122912 | tf_op jit(solution)/shard_map/ppermute | solution.py:485
  39.4 1.0 pad_maximum_fusion.1.own_ref
  40.4 2.1 %collective-permute-start.17 = (bf16[4,480,128]{2,1,0:T(8,128)(2,1)S(1)}, bf16[4,480,128]{2,1,0:T(8,128)(2,1)S(1)}, u32[]{:S(2)}, u32[]{:S(2)}) collective-permute-start(bf16[4,480,128]{2,1,0:T(8,128)(2,1)S(1)} %pad_maximum_fusion.1.own_ref), channel_id=1, source_target_pairs={{8,0},{9,1},{10,2},{11,3},{12,4},{13,5},{14,6},{15,7},{16,8},{17,9... | collective-permute-start | bytes 1474568 | tf_op jit(solution)/shard_map/ppermute | solution.py:485
  42.4 3.2 %collective-permute-start.16 = (bf16[4,480,128]{2,1,0:T(8,128)(2,1)S(1)}, bf16[4,480,128]{2,1,0:T(8,128)(2,1)S(1)}, u32[]{:S(2)}, u32[]{:S(2)}) collective-permute-start(bf16[4,480,128]{2,1,0:T(8,128)(2,1)S(1)} %pad_maximum_fusion.1.own_ref), channel_id=1, source_target_pairs={{0,8},{1,9},{2,10},{3,11},{4,12},{5,13},{6,14},{7,15},{8,16},{9,17... | collective-permute-start | bytes 1474568 | tf_op jit(solution)/shard_map/ppermute | solution.py:485
  45.7 0.1 collective-permute-start.5
  45.7 0.9 collective-permute-start.6
  46.7 1.7 %collective-permute-start.7 = (bf16[480,128]{1,0:T(8,128)(2,1)}, bf16[480,128]{1,0:T(8,128)(2,1)S(1)}, u32[]{:S(2)}, u32[]{:S(2)}) collective-permute-start(bf16[480,128]{1,0:T(8,128)(2,1)} %get-tuple-element.24), channel_id=1, source_target_pairs={{0,3},{1,2},{2,1},{3,0},{4,7},{5,6},{6,5},{7,4},{8,11},{9,10},{10,... | collective-permute-start | bytes 368648 | tf_op jit(solution)/shard_map/ppermute | solution.py:485
  48.4 0.7 dynamic-slice_bitcast_fusion
  49.1 0.9 collective-permute-done.5
  50.0 0.1 collective-permute-done.6
  50.0 2.2 %collective-permute-done.7 = bf16[480,128]{1,0:T(8,128)(2,1)S(1)} collective-permute-done((bf16[480,128]{1,0:T(8,128)(2,1)}, bf16[480,128]{1,0:T(8,128)(2,1)S(1)}, u32[]{:S(2)}, u32[]{:S(2)}) %collective-permute-start.7) | collective-permute-done | bytes 122912 | tf_op jit(solution)/shard_map/ppermute | solution.py:485
  52.2 1.0 pad_maximum_fusion.own_ref
  53.2 0.0 copy-start.3
  53.2 2.3 %collective-permute-start.9 = (bf16[4,480,128]{2,1,0:T(8,128)(2,1)S(1)}, bf16[4,480,128]{2,1,0:T(8,128)(2,1)}, u32[]{:S(2)}, u32[]{:S(2)}) collective-permute-start(bf16[4,480,128]{2,1,0:T(8,128)(2,1)S(1)} %pad_maximum_fusion.own_ref), channel_id=1, source_target_pairs={{8,0},{9,1},{10,2},{11,3},{12,4},{13,5},{14,6},{15,7},{16,8},{17,9... | collective-permute-start | bytes 1474568 | tf_op jit(solution)/shard_map/ppermute | solution.py:485
  55.5 3.2 %collective-permute-start.8 = (bf16[4,480,128]{2,1,0:T(8,128)(2,1)S(1)}, bf16[4,480,128]{2,1,0:T(8,128)(2,1)}, u32[]{:S(2)}, u32[]{:S(2)}) collective-permute-start(bf16[4,480,128]{2,1,0:T(8,128)(2,1)S(1)} %pad_maximum_fusion.own_ref), channel_id=1, source_target_pairs={{0,8},{1,9},{2,10},{3,11},{4,12},{5,13},{6,14},{7,15},{8,16},{9,17... | collective-permute-start | bytes 1474568 | tf_op jit(solution)/shard_map/ppermute | solution.py:485
  58.7 0.0 collective-permute-done.17.next_ref
  58.7 0.8 copy-done.12
  59.5 0.1 copy-done.11
  59.6 22.6 %cross.3 = (f32[2,15,32,128]{3,2,1,0:T(8,128)}, f32[2,15,32,128]{3,2,1,0:T(8,128)}, bf16[2,15,16,128]{3,2,1,0:T(8,128)(2,1)}, bf16[2,15,16,128]{3,2,1,0:T(8,128)(2,1)}) custom-call(s32[2]{0:T(128)} %pad_add_fusion.meta, f32[1,128]{1,0:T(1,128)} %get-tuple-element.40.reach_own, f32[1,128]{1,0:T(1,128)} %get-tuple-element.39.reach_prev, ...), custom_call_target="tpu_custom_call" | custom-call | flops 15000000512 | bytes 3000000 | tf_op jit(solution)/shard_map/cross/pallas_call | solution.py:382
  82.3 0.0 copy-start.8
  82.3 4.4 %collective-permute-start.18 = (f32[2,15,32,128]{3,2,1,0:T(8,128)}, f32[2,15,32,128]{3,2,1,0:T(8,128)S(1)}, u32[]{:S(2)}, u32[]{:S(2)}) collective-permute-start(f32[2,15,32,128]{3,2,1,0:T(8,128)} %get-tuple-element.34), channel_id=1, source_target_pairs={{0,4},{1,5},{2,6},{3,7},{4,0},{5,1},{6,2},{7,3},{8,12},{9,13},{10,... | collective-permute-start | bytes 1474568 | tf_op jit(solution)/shard_map/ppermute | solution.py:485
  86.7 0.0 collective-permute-done.9.next_ref
  86.7 22.7 %cross.2 = (f32[2,15,32,128]{3,2,1,0:T(8,128)}, f32[2,15,32,128]{3,2,1,0:T(8,128)}, bf16[2,15,16,128]{3,2,1,0:T(8,128)(2,1)}, bf16[2,15,16,128]{3,2,1,0:T(8,128)(2,1)}) custom-call(s32[2]{0:T(128)} %pad_add_fusion.meta, f32[1,128]{1,0:T(1,128)} %get-tuple-element.40.reach_own, f32[1,128]{1,0:T(1,128)} %get-tuple-element.39.reach_prev, ...), custom_call_target="tpu_custom_call" | custom-call | flops 15000000512 | bytes 3000000 | tf_op jit(solution)/shard_map/cross/pallas_call | solution.py:382
  109.4 0.1 collective-permute-start.10
  109.5 2.9 %collective-permute-start.19 = (bf16[2,15,16,128]{3,2,1,0:T(8,128)(2,1)S(1)}, bf16[2,15,16,128]{3,2,1,0:T(8,128)(2,1)S(1)}, u32[]{:S(2)}, u32[]{:S(2)}) collective-permute-start(bf16[2,15,16,128]{3,2,1,0:T(8,128)(2,1)S(1)} %copy-done.14), channel_id=1, source_target_pairs={{8,0},{9,1},{10,2},{11,3},{12,4},{13,5},{14,6},{15,7},{16,8},{17,9... | collective-permute-start | bytes 368648 | tf_op jit(solution)/shard_map/ppermute | solution.py:485
  112.4 0.1 pad_dynamic-slice_fusion.1
  112.5 0.1 dynamic_slice.15
  112.5 0.1 reshape.18
  112.7 0.2 reshape.19
  112.9 0.1 fusion.2
  113.0 1.9 %collective-permute-start.20 = (bf16[2,15,16,128]{3,2,1,0:T(8,128)(2,1)S(1)}, bf16[2,15,16,128]{3,2,1,0:T(8,128)(2,1)S(1)}, u32[]{:S(2)}, u32[]{:S(2)}) collective-permute-start(bf16[2,15,16,128]{3,2,1,0:T(8,128)(2,1)S(1)} %copy-done.13), channel_id=1, source_target_pairs={{8,4},{9,5},{10,6},{11,7},{12,0},{13,1},{14,2},{15,3},{16,12},{17,... | collective-permute-start | bytes 368648 | tf_op jit(solution)/shard_map/ppermute | solution.py:485
  114.9 1.9 %collective-permute-start.11 = (bf16[2,15,16,128]{3,2,1,0:T(8,128)(2,1)}, bf16[2,15,16,128]{3,2,1,0:T(8,128)(2,1)S(1)}, u32[]{:S(2)}, u32[]{:S(2)}) collective-permute-start(bf16[2,15,16,128]{3,2,1,0:T(8,128)(2,1)} %get-tuple-element.27), channel_id=1, source_target_pairs={{8,0},{9,1},{10,2},{11,3},{12,4},{13,5},{14,6},{15,7},{16,8},{17,9... | collective-permute-start | bytes 368648 | tf_op jit(solution)/shard_map/ppermute | solution.py:485
  116.8 3.0 %collective-permute-start.12 = (bf16[2,15,16,128]{3,2,1,0:T(8,128)(2,1)}, bf16[2,15,16,128]{3,2,1,0:T(8,128)(2,1)S(1)}, u32[]{:S(2)}, u32[]{:S(2)}) collective-permute-start(bf16[2,15,16,128]{3,2,1,0:T(8,128)(2,1)} %get-tuple-element.28), channel_id=1, source_target_pairs={{8,4},{9,5},{10,6},{11,7},{12,0},{13,1},{14,2},{15,3},{16,12},{17,... | collective-permute-start | bytes 368648 | tf_op jit(solution)/shard_map/ppermute | solution.py:485
  119.9 0.6 broadcast_maximum_fusion
  120.5 0.2 collective-permute-done.20.rest_7_
  120.7 2.5 %collective-permute-done.11.rest_2_ = bf16[2,15,16,128]{3,2,1,0:T(8,128)(2,1)S(1)} collective-permute-done((bf16[2,15,16,128]{3,2,1,0:T(8,128)(2,1)}, bf16[2,15,16,128]{3,2,1,0:T(8,128)(2,1)S(1)}, u32[]{:S(2)}, u32[]{:S(2)}) %collective-permute-start.11) | collective-permute-done | bytes 122912 | tf_op jit(solution)/shard_map/ppermute | solution.py:485
  123.2 2.6 %collective-permute-done.12.rest_3_ = bf16[2,15,16,128]{3,2,1,0:T(8,128)(2,1)S(1)} collective-permute-done((bf16[2,15,16,128]{3,2,1,0:T(8,128)(2,1)}, bf16[2,15,16,128]{3,2,1,0:T(8,128)(2,1)S(1)}, u32[]{:S(2)}, u32[]{:S(2)}) %collective-permute-start.12) | collective-permute-done | bytes 122912 | tf_op jit(solution)/shard_map/ppermute | solution.py:485
  125.9 0.6 copy-done.7
  126.5 0.2 copy-done
  126.7 0.2 copy-done.2
  126.8 2.8 %finish.1 = f32[2,960,256]{2,1,0:T(8,128)} custom-call(s32[2]{0:T(128)} %pad_add_fusion.meta, f32[1,256]{1,0:T(1,128)} %bitcast.26, f32[2,15,32,128]{3,2,1,0:T(8,128)} %get-tuple-element.25.rest_0_, f32[2,15,32,128]{3,2,1,0:T(8,128)} %copy-done.2, bf16[2,15,16,128]{3,2,1,0:T(8,128)(2,1)} %copy-done.6, bf16[2,15,16,128]{3,2,1,0:T(8,128)(2,1)} %copy-done.7, ...), custom_call_target="tpu_custom_call" | custom-call | tf_op jit(solution)/shard_map/finish/pallas_call | solution.py:439
  (36 shorter events, 0.1 us)
Async XLA Ops:
  0.0 15.6 %collective-permute-start = (bf16[64,7680]{1,0:T(8,128)(2,1)}, bf16[64,7680]{1,0:T(8,128)(2,1)S(1)}, u32[]{:S(2)}, u32[]{:S(2)}) collective-permute-start(bf16[64,7680]{1,0:T(8,128)(2,1)} %own.1), channel_id=1, source_target_pairs={{0,4},{1,5},{2,6},{3,7},{4,0},{5,1},{6,2},{7,3},{8,12},{9,13},{10,... | collective-permute-start | bytes 2949128 | tf_op jit(solution)/shard_map/ppermute | solution.py:485
  1.5 14.1 %collective-permute-start.4 = (bf16[64,256]{1,0:T(8,128)(2,1)S(1)}, bf16[64,256]{1,0:T(8,128)(2,1)S(1)}, u32[]{:S(2)}, u32[]{:S(2)}) collective-permute-start(bf16[64,256]{1,0:T(8,128)(2,1)S(1)} %get-tuple-element.37), channel_id=1, source_target_pairs={{1,4},{2,5},{3,6},{5,0},{6,1},{7,2},{9,12},{10,13},{11,14},{13,8},... | collective-permute-start | bytes 98312 | tf_op jit(solution)/shard_map/ppermute | solution.py:485
  2.7 12.8 %collective-permute-start.3 = (bf16[64,256]{1,0:T(8,128)(2,1)S(1)}, bf16[64,256]{1,0:T(8,128)(2,1)S(1)}, u32[]{:S(2)}, u32[]{:S(2)}) collective-permute-start(bf16[64,256]{1,0:T(8,128)(2,1)S(1)} %get-tuple-element.37), channel_id=1, source_target_pairs={{1,0},{2,1},{3,2},{5,4},{6,5},{7,6},{9,8},{10,9},{11,10},{13,12},{... | collective-permute-start | bytes 98312 | tf_op jit(solution)/shard_map/ppermute | solution.py:485
  4.0 11.5 %collective-permute-start.2 = (bf16[64,256]{1,0:T(8,128)(2,1)S(1)}, bf16[64,256]{1,0:T(8,128)(2,1)S(1)}, u32[]{:S(2)}, u32[]{:S(2)}) collective-permute-start(bf16[64,256]{1,0:T(8,128)(2,1)S(1)} %get-tuple-element.38), channel_id=1, source_target_pairs={{0,5},{1,6},{2,7},{4,1},{5,2},{6,3},{8,13},{9,14},{10,15},{12,9},{... | collective-permute-start | bytes 98312 | tf_op jit(solution)/shard_map/ppermute | solution.py:485
  8.9 6.6 %collective-permute-start.1 = (bf16[64,256]{1,0:T(8,128)(2,1)S(1)}, bf16[64,256]{1,0:T(8,128)(2,1)S(1)}, u32[]{:S(2)}, u32[]{:S(2)}) collective-permute-start(bf16[64,256]{1,0:T(8,128)(2,1)S(1)} %get-tuple-element.38), channel_id=1, source_target_pairs={{0,1},{1,2},{2,3},{4,5},{5,6},{6,7},{8,9},{9,10},{10,11},{12,13},{... | collective-permute-start | bytes 98312 | tf_op jit(solution)/shard_map/ppermute | solution.py:485
  15.5 32.9 %copy-start.9 = (s32[512]{0:T(512)S(1)}, s32[512]{0:T(512)}, u32[]{:S(2)}) copy-start(s32[512]{0:T(512)} %param.16) | copy-start | bytes 6148
  15.5 0.6 copy-start.15
  15.5 0.6 copy-start.16
  15.5 0.6 copy-start.17
  15.6 0.6 copy-start.18
  16.2 0.9 copy-start.10
  30.4 5.2 %collective-permute-start.13 = (bf16[480,128]{1,0:T(8,128)(2,1)}, bf16[480,128]{1,0:T(8,128)(2,1)S(1)}, u32[]{:S(2)}, u32[]{:S(2)}) collective-permute-start(bf16[480,128]{1,0:T(8,128)(2,1)} %get-tuple-element.30), channel_id=1, source_target_pairs={{0,1},{1,0},{2,3},{3,2},{4,5},{5,4},{6,7},{7,6},{8,9},{9,8},{10,11... | collective-permute-start | bytes 368648 | tf_op jit(solution)/shard_map/ppermute | solution.py:485
  31.7 4.3 %collective-permute-start.14 = (bf16[480,128]{1,0:T(8,128)(2,1)}, bf16[480,128]{1,0:T(8,128)(2,1)S(1)}, u32[]{:S(2)}, u32[]{:S(2)}) collective-permute-start(bf16[480,128]{1,0:T(8,128)(2,1)} %get-tuple-element.31), channel_id=1, source_target_pairs={{0,2},{1,3},{2,0},{3,1},{4,6},{5,7},{6,4},{7,5},{8,10},{9,11},{10,... | collective-permute-start | bytes 368648 | tf_op jit(solution)/shard_map/ppermute | solution.py:485
  32.6 6.8 %collective-permute-start.15 = (bf16[480,128]{1,0:T(8,128)(2,1)}, bf16[480,128]{1,0:T(8,128)(2,1)S(1)}, u32[]{:S(2)}, u32[]{:S(2)}) collective-permute-start(bf16[480,128]{1,0:T(8,128)(2,1)} %get-tuple-element.32), channel_id=1, source_target_pairs={{0,3},{1,2},{2,1},{3,0},{4,7},{5,6},{6,5},{7,4},{8,11},{9,10},{10,... | collective-permute-start | bytes 368648 | tf_op jit(solution)/shard_map/ppermute | solution.py:485
  40.4 19.2 %copy-start.1 = (bf16[4,480,128]{2,1,0:T(8,128)(2,1)}, bf16[4,480,128]{2,1,0:T(8,128)(2,1)S(1)}, u32[]{:S(2)}) copy-start(bf16[4,480,128]{2,1,0:T(8,128)(2,1)S(1)} %pad_maximum_fusion.1.own_ref) | copy-start | bytes 1474564
  40.4 18.3 %collective-permute-start.17 = (bf16[4,480,128]{2,1,0:T(8,128)(2,1)S(1)}, bf16[4,480,128]{2,1,0:T(8,128)(2,1)S(1)}, u32[]{:S(2)}, u32[]{:S(2)}) collective-permute-start(bf16[4,480,128]{2,1,0:T(8,128)(2,1)S(1)} %pad_maximum_fusion.1.own_ref), channel_id=1, source_target_pairs={{8,0},{9,1},{10,2},{11,3},{12,4},{13,5},{14,6},{15,7},{16,8},{17,9... | collective-permute-start | bytes 1474568 | tf_op jit(solution)/shard_map/ppermute | solution.py:485
  42.4 16.2 %collective-permute-start.16 = (bf16[4,480,128]{2,1,0:T(8,128)(2,1)S(1)}, bf16[4,480,128]{2,1,0:T(8,128)(2,1)S(1)}, u32[]{:S(2)}, u32[]{:S(2)}) collective-permute-start(bf16[4,480,128]{2,1,0:T(8,128)(2,1)S(1)} %pad_maximum_fusion.1.own_ref), channel_id=1, source_target_pairs={{0,8},{1,9},{2,10},{3,11},{4,12},{5,13},{6,14},{7,15},{8,16},{9,17... | collective-permute-start | bytes 1474568 | tf_op jit(solution)/shard_map/ppermute | solution.py:485
  45.7 4.3 %collective-permute-start.5 = (bf16[480,128]{1,0:T(8,128)(2,1)}, bf16[480,128]{1,0:T(8,128)(2,1)S(1)}, u32[]{:S(2)}, u32[]{:S(2)}) collective-permute-start(bf16[480,128]{1,0:T(8,128)(2,1)} %get-tuple-element.22), channel_id=1, source_target_pairs={{0,1},{1,0},{2,3},{3,2},{4,5},{5,4},{6,7},{7,6},{8,9},{9,8},{10,11... | collective-permute-start | bytes 368648 | tf_op jit(solution)/shard_map/ppermute | solution.py:485
  45.7 4.3 %collective-permute-start.6 = (bf16[480,128]{1,0:T(8,128)(2,1)}, bf16[480,128]{1,0:T(8,128)(2,1)S(1)}, u32[]{:S(2)}, u32[]{:S(2)}) collective-permute-start(bf16[480,128]{1,0:T(8,128)(2,1)} %get-tuple-element.23), channel_id=1, source_target_pairs={{0,2},{1,3},{2,0},{3,1},{4,6},{5,7},{6,4},{7,5},{8,10},{9,11},{10,... | collective-permute-start | bytes 368648 | tf_op jit(solution)/shard_map/ppermute | solution.py:485
  46.7 5.5 %collective-permute-start.7 = (bf16[480,128]{1,0:T(8,128)(2,1)}, bf16[480,128]{1,0:T(8,128)(2,1)S(1)}, u32[]{:S(2)}, u32[]{:S(2)}) collective-permute-start(bf16[480,128]{1,0:T(8,128)(2,1)} %get-tuple-element.24), channel_id=1, source_target_pairs={{0,3},{1,2},{2,1},{3,0},{4,7},{5,6},{6,5},{7,4},{8,11},{9,10},{10,... | collective-permute-start | bytes 368648 | tf_op jit(solution)/shard_map/ppermute | solution.py:485
  53.2 29.1 %copy-start.3 = (bf16[4,480,128]{2,1,0:T(8,128)(2,1)}, bf16[4,480,128]{2,1,0:T(8,128)(2,1)S(1)}, u32[]{:S(2)}) copy-start(bf16[4,480,128]{2,1,0:T(8,128)(2,1)S(1)} %pad_maximum_fusion.own_ref) | copy-start | bytes 1474564
  53.2 33.5 %collective-permute-start.9 = (bf16[4,480,128]{2,1,0:T(8,128)(2,1)S(1)}, bf16[4,480,128]{2,1,0:T(8,128)(2,1)}, u32[]{:S(2)}, u32[]{:S(2)}) collective-permute-start(bf16[4,480,128]{2,1,0:T(8,128)(2,1)S(1)} %pad_maximum_fusion.own_ref), channel_id=1, source_target_pairs={{8,0},{9,1},{10,2},{11,3},{12,4},{13,5},{14,6},{15,7},{16,8},{17,9... | collective-permute-start | bytes 1474568 | tf_op jit(solution)/shard_map/ppermute | solution.py:485
  55.5 31.2 %collective-permute-start.8 = (bf16[4,480,128]{2,1,0:T(8,128)(2,1)S(1)}, bf16[4,480,128]{2,1,0:T(8,128)(2,1)}, u32[]{:S(2)}, u32[]{:S(2)}) collective-permute-start(bf16[4,480,128]{2,1,0:T(8,128)(2,1)S(1)} %pad_maximum_fusion.own_ref), channel_id=1, source_target_pairs={{0,8},{1,9},{2,10},{3,11},{4,12},{5,13},{6,14},{7,15},{8,16},{9,17... | collective-permute-start | bytes 1474568 | tf_op jit(solution)/shard_map/ppermute | solution.py:485
  58.7 1.0 copy-start.11
  58.7 0.8 copy-start.12
  82.3 27.2 %copy-start.14 = (bf16[2,15,16,128]{3,2,1,0:T(8,128)(2,1)S(1)}, bf16[2,15,16,128]{3,2,1,0:T(8,128)(2,1)}, u32[]{:S(2)}) copy-start(bf16[2,15,16,128]{3,2,1,0:T(8,128)(2,1)} %get-tuple-element.35) | copy-start | bytes 368644
  82.3 30.1 %copy-start.8 = (s32[512]{0:T(512)S(1)}, s32[512]{0:T(512)}, u32[]{:S(2)}) copy-start(s32[512]{0:T(512)} %param.15) | copy-start | bytes 6148
  82.3 30.7 %copy-start.13 = (bf16[2,15,16,128]{3,2,1,0:T(8,128)(2,1)S(1)}, bf16[2,15,16,128]{3,2,1,0:T(8,128)(2,1)}, u32[]{:S(2)}) copy-start(bf16[2,15,16,128]{3,2,1,0:T(8,128)(2,1)} %get-tuple-element.36) | copy-start | bytes 368644
  82.3 43.5 %collective-permute-start.18 = (f32[2,15,32,128]{3,2,1,0:T(8,128)}, f32[2,15,32,128]{3,2,1,0:T(8,128)S(1)}, u32[]{:S(2)}, u32[]{:S(2)}) collective-permute-start(f32[2,15,32,128]{3,2,1,0:T(8,128)} %get-tuple-element.34), channel_id=1, source_target_pairs={{0,4},{1,5},{2,6},{3,7},{4,0},{5,1},{6,2},{7,3},{8,12},{9,13},{10,... | collective-permute-start | bytes 1474568 | tf_op jit(solution)/shard_map/ppermute | solution.py:485
  109.4 16.4 %collective-permute-start.10 = (f32[2,15,32,128]{3,2,1,0:T(8,128)}, f32[2,15,32,128]{3,2,1,0:T(8,128)S(1)}, u32[]{:S(2)}, u32[]{:S(2)}) collective-permute-start(f32[2,15,32,128]{3,2,1,0:T(8,128)} %get-tuple-element.26), channel_id=1, source_target_pairs={{0,4},{1,5},{2,6},{3,7},{4,0},{5,1},{6,2},{7,3},{8,12},{9,13},{10,... | collective-permute-start | bytes 1474568 | tf_op jit(solution)/shard_map/ppermute | solution.py:485
  109.5 7.3 %collective-permute-start.19 = (bf16[2,15,16,128]{3,2,1,0:T(8,128)(2,1)S(1)}, bf16[2,15,16,128]{3,2,1,0:T(8,128)(2,1)S(1)}, u32[]{:S(2)}, u32[]{:S(2)}) collective-permute-start(bf16[2,15,16,128]{3,2,1,0:T(8,128)(2,1)S(1)} %copy-done.14), channel_id=1, source_target_pairs={{8,0},{9,1},{10,2},{11,3},{12,4},{13,5},{14,6},{15,7},{16,8},{17,9... | collective-permute-start | bytes 368648 | tf_op jit(solution)/shard_map/ppermute | solution.py:485
  113.0 7.7 %collective-permute-start.20 = (bf16[2,15,16,128]{3,2,1,0:T(8,128)(2,1)S(1)}, bf16[2,15,16,128]{3,2,1,0:T(8,128)(2,1)S(1)}, u32[]{:S(2)}, u32[]{:S(2)}) collective-permute-start(bf16[2,15,16,128]{3,2,1,0:T(8,128)(2,1)S(1)} %copy-done.13), channel_id=1, source_target_pairs={{8,4},{9,5},{10,6},{11,7},{12,0},{13,1},{14,2},{15,3},{16,12},{17,... | collective-permute-start | bytes 368648 | tf_op jit(solution)/shard_map/ppermute | solution.py:485
  114.9 8.3 %collective-permute-start.11 = (bf16[2,15,16,128]{3,2,1,0:T(8,128)(2,1)}, bf16[2,15,16,128]{3,2,1,0:T(8,128)(2,1)S(1)}, u32[]{:S(2)}, u32[]{:S(2)}) collective-permute-start(bf16[2,15,16,128]{3,2,1,0:T(8,128)(2,1)} %get-tuple-element.27), channel_id=1, source_target_pairs={{8,0},{9,1},{10,2},{11,3},{12,4},{13,5},{14,6},{15,7},{16,8},{17,9... | collective-permute-start | bytes 368648 | tf_op jit(solution)/shard_map/ppermute | solution.py:485
  116.8 9.0 %copy-start.4 = (bf16[2,15,16,128]{3,2,1,0:T(8,128)(2,1)}, bf16[2,15,16,128]{3,2,1,0:T(8,128)(2,1)S(1)}, u32[]{:S(2)}) copy-start(bf16[2,15,16,128]{3,2,1,0:T(8,128)(2,1)S(1)} %collective-permute-done.19.rest_6_) | copy-start | bytes 368644
  116.8 9.0 %collective-permute-start.12 = (bf16[2,15,16,128]{3,2,1,0:T(8,128)(2,1)}, bf16[2,15,16,128]{3,2,1,0:T(8,128)(2,1)S(1)}, u32[]{:S(2)}, u32[]{:S(2)}) collective-permute-start(bf16[2,15,16,128]{3,2,1,0:T(8,128)(2,1)} %get-tuple-element.28), channel_id=1, source_target_pairs={{8,4},{9,5},{10,6},{11,7},{12,0},{13,1},{14,2},{15,3},{16,12},{17,... | collective-permute-start | bytes 368648 | tf_op jit(solution)/shard_map/ppermute | solution.py:485
  120.7 5.2 %copy-start.5 = (bf16[2,15,16,128]{3,2,1,0:T(8,128)(2,1)}, bf16[2,15,16,128]{3,2,1,0:T(8,128)(2,1)S(1)}, u32[]{:S(2)}) copy-start(bf16[2,15,16,128]{3,2,1,0:T(8,128)(2,1)S(1)} %collective-permute-done.20.rest_7_) | copy-start | bytes 368644
  123.2 2.7 %copy-start.6 = (bf16[2,15,16,128]{3,2,1,0:T(8,128)(2,1)}, bf16[2,15,16,128]{3,2,1,0:T(8,128)(2,1)S(1)}, u32[]{:S(2)}) copy-start(bf16[2,15,16,128]{3,2,1,0:T(8,128)(2,1)S(1)} %collective-permute-done.11.rest_2_) | copy-start | bytes 368644
  125.8 0.6 copy-start.7
  125.8 0.8 copy-start
  125.8 1.0 copy-start.2

commit v4 on v3

--- a/solution.py
+++ b/solution.py
@@ -70,8 +70,6 @@
 def spectra_kernel(
     count_a,
     n_freq,
-    chunks,
-    meta,
     own,
     other,
     lo_own,
@@ -83,12 +81,11 @@
     first,
     twist,
     second,
-    quality,
     *rest,
 ):
-    outs = rest[: n_freq * len(chunks)]
+    outs = rest[:n_freq]
     padded, filtered, magnitude, whitened, tw_re, tw_im = rest[len(outs) :]
-    core, band = meta[0], meta[1]
+    core, band = lax.axis_index("chan") % 2, lax.axis_index("freq")
     ch = own.shape[0]
     both = 2 * ch
     pad_a = first.shape[1]
@@ -149,13 +146,13 @@
     rk = second.shape[2]
     half = rk // 2
     group = block_bins(n_freq) // half
-    scale = quality[...] * (1.0 / math.sqrt(count_a * TBLK))
+    scale = 1.0 / math.sqrt(count_a * TBLK)
     turn = jnp.concatenate([second[band ^ d, core] for d in range(n_freq)], axis=0)
 
-    def bins(k, start, i):
+    def bins(i):
         results = []
         for n in range(group):
-            k1 = (start + i) * group + n
+            k1 = i * group + n
             re = tw_re[pl.ds(k1, both, stride=pad_a), :].astype(jnp.bfloat16)
             im = tw_im[pl.ds(k1, both, stride=pad_a), :].astype(jnp.bfloat16)
             result = lax.dot_general(
@@ -169,31 +166,27 @@
         for d in range(n_freq):
             starts = [d * rk + p * half for p in range(2)]
             block = jnp.concatenate([r[s : s + half] for s in starts for r in results], axis=0)
-            outs[k * n_freq + d][rows, :] = block.astype(jnp.bfloat16)
-
-    start = 0
-    for k, size in enumerate(chunks):
-        for i in range(size):
-            bins(k, start, i)
-        start += size
-
-
-def spectra(meta, own, other, halos, quality, n_freq, chunks):
+            outs[d][rows, :] = block.astype(jnp.bfloat16)
+
+    for i in range(count_a // group):
+        bins(i)
+
+
+def spectra(own, other, halos, n_freq):
     ch, length = own.shape
     count_a = length // TBLK
     first, twist, second = dft_tables(count_a, n_freq)
     rk = second.shape[2]
     pad_a = first.shape[1]
     both = 2 * ch
-    rows = 2 * block_bins(n_freq)
-    shapes = [(size * rows, both) for size in chunks for _ in range(n_freq)]
+    shapes = [(count_a * rk, both)] * n_freq
     tables = (stencil_table(False), stencil_table(True), first, twist, second)
-    operands = (own, other, *halos, *(jnp.asarray(t) for t in tables), quality)
+    operands = (own, other, *halos, *(jnp.asarray(t) for t in tables))
     return pl.pallas_call(
-        functools.partial(spectra_kernel, count_a, n_freq, chunks),
+        functools.partial(spectra_kernel, count_a, n_freq),
         grid=(1,),
         out_shape=[jax.ShapeDtypeStruct(shape, jnp.bfloat16) for shape in shapes],
-        in_specs=[pl.BlockSpec(memory_space=pltpu.SMEM)] + [whole(x.shape) for x in operands],
+        in_specs=[whole(x.shape) for x in operands],
         out_specs=[whole(shape) for shape in shapes],
         scratch_shapes=[
             pltpu.VMEM((count_a + 4, both, TBLK), jnp.bfloat16),
@@ -208,11 +201,11 @@
             flops=6 * 10**9, bytes_accessed=4 * 10**6, transcendentals=0
         ),
         name="spectra",
-    )(meta, *operands)
+    )(*operands)
 
 
 def cross_kernel(
-    meta,
+    per,
     reach_own,
     reach_prev,
     turn_ref,
@@ -234,10 +227,11 @@
 ):
     step = pl.program_id(0)
     n_seg, rb, both = own_ref.shape
+    rb //= per
     depth = turn_ref.shape[0]
     nb = pick_ref.shape[0]
     slabs = both // 8
-    first_core = meta[0] == 0
+    first_core = lax.axis_index("chan") % 2 == 0
 
     @pl.when(step == 0)
     def _():
@@ -271,98 +265,112 @@
         im = im.reshape(slabs, 8, depth)
         return jnp.stack([re, im], axis=1).reshape(slabs, 16, depth).astype(jnp.bfloat16)
 
-    own, nxt, prev = (r[...].reshape(depth, both) for r in (own_ref, next_ref, prev_ref))
-    left = jnp.concatenate([left_rows(own), left_rows(prev)], axis=2)
-    pick = pick_ref[...]
-
-    zero = jnp.zeros_like(own)
-    for a in range(slabs):
-        g, first = divmod(a, slabs // 2)
-        if a == 0:
-            right = jnp.concatenate(
-                [jnp.concatenate([own, nxt], axis=1), jnp.concatenate([zero, zero], axis=1)],
-                axis=0,
-            )
-        else:
-            moved_own = pltpu.roll(own, both - 8 * a, 1).reshape(depth // 16, 16, both)
-            moved_next = pltpu.roll(nxt, both - 8 * a, 1).reshape(depth // 16, 16, both)
-            cut = cut_ref[a][None]
-            inner = moved_next * cut
-            outer = moved_next - inner
-            local = (moved_own * cut + outer).reshape(depth, both)
-            inner = inner.reshape(depth, both)
-            outer = outer.reshape(depth, both)
-            right = jnp.concatenate(
-                [
-                    jnp.concatenate([local, inner], axis=1),
-                    jnp.concatenate([zero, outer], axis=1),
-                ],
-                axis=0,
-            )
-        rows = (left[a][None] * pick).reshape(nb * 16, 2 * depth)
-        result = jnp.dot(rows, right, preferred_element_type=jnp.float32)
-        one = result[:, :both]
-        two = result[:, both:].reshape(nb, 16, both)
-        near = (two * w_near[a][None]).reshape(nb * 16, both)
-        far = (two * w_far[a][None]).reshape(nb * 16, both)
-        if first == 0:
-            sum_one[g], sum_two[g], sum_far[g] = one, near, far
-        else:
-            sum_one[g] += one
-            sum_two[g] += near
-            sum_far[g] += far
-
-    def split(x):
-        return x[:nb], x[nb:]
-
-    lefts = [split(prev_ref[s].astype(jnp.float32)) for s in range(n_seg)]
-    rights = [split(next_ref[s].astype(jnp.float32)) for s in range(n_seg)]
-    pieces = []
-    for d in range(1, 8):
-        re = im = None
-        for (xr, xi), (yr, yi) in zip(lefts, rights):
-            yr, yi = pltpu.roll(yr, d, 1), pltpu.roll(yi, d, 1)
-            r, i = xr * yr + xi * yi, xi * yr - xr * yi
-            re, im = (r, i) if re is None else (re + r, im + i)
-        pieces.append(jnp.concatenate([re, im], axis=0).astype(jnp.bfloat16))
-    margin = jnp.dot(
-        jnp.concatenate(pieces, axis=1), edge[...], preferred_element_type=jnp.float32
-    )
-
-    lane = lax.broadcasted_iota(jnp.int32, (nb, both), 1)
-    for p in range(2):
-        values = []
-        for g in range(2):
-            low = high = far = None
-            for b in range(8):
-                rows = pl.ds(p * 8 + b, nb, stride=16)
-                one, two, three = sum_one[g, rows, :], sum_two[g, rows, :], sum_far[g, rows, :]
-                if b == 0:
-                    low, high, far = one, two, three
-                    continue
-                low += pltpu.roll(jnp.where(lane >= b, one, two), both - b, 1)
-                high += pltpu.roll(jnp.where(lane >= b, two, 0.0), both - b, 1)
-                far += pltpu.roll(three, both - b, 1)
-            far += margin[p * nb : (p + 1) * nb, g * both : (g + 1) * both]
-            values.append((low, high, far))
-        mine = [jnp.where(first_core, x, y) for x, y in zip(*values)]
-        theirs = [jnp.where(first_core, y, x) for x, y in zip(*values)]
-        for near_ref, far_ref, value in (
-            (mine_ref, far_mine_ref, mine),
-            (theirs_ref, far_theirs_ref, theirs),
-        ):
-            near_ref[p, 0, :nb] = value[0]
-            near_ref[p, 0, nb:] = value[1]
-            far_ref[p, 0] = value[2].astype(jnp.bfloat16)
-
-
-def cross(meta, own, prev, nxt, reach_own, reach_prev):
+    def dots(j):
+        own, nxt, prev = (r[:, j * rb : (j + 1) * rb, :].reshape(depth, both) for r in (own_ref, next_ref, prev_ref))
+        left = jnp.concatenate([left_rows(own), left_rows(prev)], axis=2)
+        pick = pick_ref[...]
+
+        zero = jnp.zeros_like(own)
+        for a in range(slabs):
+            g, first = divmod(a, slabs // 2)
+            if a == 0:
+                right = jnp.concatenate(
+                    [jnp.concatenate([own, nxt], axis=1), jnp.concatenate([zero, zero], axis=1)],
+                    axis=0,
+                )
+            else:
+                moved_own = pltpu.roll(own, both - 8 * a, 1).reshape(depth // 16, 16, both)
+                moved_next = pltpu.roll(nxt, both - 8 * a, 1).reshape(depth // 16, 16, both)
+                cut = cut_ref[a][None]
+                inner = moved_next * cut
+                outer = moved_next - inner
+                local = (moved_own * cut + outer).reshape(depth, both)
+                inner = inner.reshape(depth, both)
+                outer = outer.reshape(depth, both)
+                right = jnp.concatenate(
+                    [
+                        jnp.concatenate([local, inner], axis=1),
+                        jnp.concatenate([zero, outer], axis=1),
+                    ],
+                    axis=0,
+                )
+            rows = (left[a][None] * pick).reshape(nb * 16, 2 * depth)
+            result = jnp.dot(rows, right, preferred_element_type=jnp.float32)
+            one = result[:, :both]
+            two = result[:, both:].reshape(nb, 16, both)
+            near = (two * w_near[a][None]).reshape(nb * 16, both)
+            far = (two * w_far[a][None]).reshape(nb * 16, both)
+            if first == 0:
+                sum_one[2 * j + g], sum_two[2 * j + g], sum_far[2 * j + g] = one, near, far
+            else:
+                sum_one[2 * j + g] += one
+                sum_two[2 * j + g] += near
+                sum_far[2 * j + g] += far
+
+
+    def margins(j):
+        def split(x):
+            return x[:nb], x[nb:]
+
+        lefts = [split(prev_ref[s, j * rb : (j + 1) * rb].astype(jnp.float32)) for s in range(n_seg)]
+        rights = [split(next_ref[s, j * rb : (j + 1) * rb].astype(jnp.float32)) for s in range(n_seg)]
+        pieces = []
+        for d in range(1, 8):
+            re = im = None
+            for (xr, xi), (yr, yi) in zip(lefts, rights):
+                yr, yi = pltpu.roll(yr, d, 1), pltpu.roll(yi, d, 1)
+                r, i = xr * yr + xi * yi, xi * yr - xr * yi
+                re, im = (r, i) if re is None else (re + r, im + i)
+            pieces.append(jnp.concatenate([re, im], axis=0).astype(jnp.bfloat16))
+        margin = jnp.dot(
+            jnp.concatenate(pieces, axis=1), edge[...], preferred_element_type=jnp.float32
+        )
+
+
+        return margin
+
+    def diag(j, margin):
+        lane = lax.broadcasted_iota(jnp.int32, (nb, both), 1)
+        for p in range(2):
+            values = []
+            for g in range(2):
+                low = high = far = None
+                for b in range(8):
+                    rows = pl.ds(p * 8 + b, nb, stride=16)
+                    one, two, three = sum_one[2 * j + g, rows, :], sum_two[2 * j + g, rows, :], sum_far[2 * j + g, rows, :]
+                    if b == 0:
+                        low, high, far = one, two, three
+                        continue
+                    low += pltpu.roll(jnp.where(lane >= b, one, two), both - b, 1)
+                    high += pltpu.roll(jnp.where(lane >= b, two, 0.0), both - b, 1)
+                    far += pltpu.roll(three, both - b, 1)
+                far += margin[p * nb : (p + 1) * nb, g * both : (g + 1) * both]
+                values.append((low, high, far))
+            mine = [jnp.where(first_core, x, y) for x, y in zip(*values)]
+            theirs = [jnp.where(first_core, y, x) for x, y in zip(*values)]
+            for near_ref, far_ref, value in (
+                (mine_ref, far_mine_ref, mine),
+                (theirs_ref, far_theirs_ref, theirs),
+            ):
+                near_ref[p, j, :nb] = value[0]
+                near_ref[p, j, nb:] = value[1]
+                far_ref[p, j] = value[2].astype(far_ref.dtype)
+
+    for j in range(per):
+        dots(j)
+    margin = [margins(j) for j in range(per)]
+    for j in range(per):
+        diag(j, margin[j])
+
+
+def cross(own, prev, nxt, reach_own, reach_prev, far_type):
     n_seg, rows, both = own.shape
     nb = block_bins(n_seg)
     rb = 2 * nb
     depth = n_seg * rb
     steps = rows // rb
     slabs = both // 8
+    per = 2 if steps % 2 == 0 else 1
     lane = np.arange(depth)
     part = lane % rb // nb
     turn = np.zeros((depth, depth))
@@ -375,39 +383,37 @@
     tables = [jnp.asarray(x.astype(ml_dtypes.bfloat16)) for x in (turn, pick, cut)]
     fixed = (reach_own, reach_prev, *tables)
     near = jax.ShapeDtypeStruct((2, steps, 2 * nb, both), jnp.float32)
-    far = jax.ShapeDtypeStruct((2, steps, nb, both), jnp.bfloat16)
-    near_spec = pl.BlockSpec((2, 1, 2 * nb, both), lambda t: (0, t, 0, 0))
-    far_spec = pl.BlockSpec((2, 1, nb, both), lambda t: (0, t, 0, 0))
-    block = pl.BlockSpec((n_seg, rb, both), lambda t: (0, t, 0))
+    far = jax.ShapeDtypeStruct((2, steps, nb, both), far_type)
+    near_spec = pl.BlockSpec((2, per, 2 * nb, both), lambda t: (0, t, 0, 0))
+    far_spec = pl.BlockSpec((2, per, nb, both), lambda t: (0, t, 0, 0))
+    block = pl.BlockSpec((n_seg, per * rb, both), lambda t: (0, t, 0))
     return pl.pallas_call(
-        cross_kernel,
-        grid=(steps,),
+        functools.partial(cross_kernel, per),
+        grid=(steps // per,),
         out_shape=[near, near, far, far],
-        in_specs=[pl.BlockSpec(memory_space=pltpu.SMEM)]
-        + [whole(x.shape) for x in fixed]
-        + [block] * 3,
+        in_specs=[whole(x.shape) for x in fixed] + [block] * 3,
         out_specs=[near_spec, near_spec, far_spec, far_spec],
         scratch_shapes=[
             pltpu.VMEM((slabs, 16, both), jnp.float32),
             pltpu.VMEM((slabs, 16, both), jnp.float32),
             pltpu.VMEM((7 * both, 2 * both), jnp.bfloat16),
-            pltpu.VMEM((2, nb * 16, both), jnp.float32),
-            pltpu.VMEM((2, nb * 16, both), jnp.float32),
-            pltpu.VMEM((2, nb * 16, both), jnp.float32),
+            pltpu.VMEM((2 * per, nb * 16, both), jnp.float32),
+            pltpu.VMEM((2 * per, nb * 16, both), jnp.float32),
+            pltpu.VMEM((2 * per, nb * 16, both), jnp.float32),
         ],
         compiler_params=pltpu.CompilerParams(
-            dimension_semantics=("arbitrary",), vmem_limit_bytes=62 * MIB
+            dimension_semantics=("arbitrary",), vmem_limit_bytes=24 * MIB
         ),
         cost_estimate=pl.CostEstimate(
             flops=10**9 * steps, bytes_accessed=2 * 10**5 * steps, transcendentals=0
         ),
         name="cross",
-    )(meta, *fixed, own, prev, nxt)
-
-
-def finish_kernel(count_a, half, chunks, meta, count, *rest):
+    )(*fixed, own, prev, nxt)
+
+
+def finish_kernel(count_a, half, chunks, count, *rest):
     parts, out_ref, stage = rest[: 4 * chunks], rest[4 * chunks], rest[4 * chunks + 1]
-    core = meta[0]
+    core = lax.axis_index("chan") % 2
     bins = out_ref.shape[1] // 2
     inverse = 1.0 / count[...]
     k1 = 0
@@ -430,7 +436,7 @@
         out_ref[0, :, r * both : (r + 1) * both] = stage[r]
 
 
-def finish(meta, count, parts, count_a, half):
+def finish(count, parts, count_a, half):
     bins = count_a * half
 
     def half_of(shape):
@@ -440,13 +446,12 @@
         functools.partial(finish_kernel, count_a, half, len(parts) // 4),
         grid=(2,),
         out_shape=jax.ShapeDtypeStruct((2, 2 * bins, BAND), jnp.float32),
-        in_specs=[pl.BlockSpec(memory_space=pltpu.SMEM), whole(count.shape)]
-        + [half_of(x.shape) for x in parts],
+        in_specs=[whole(count.shape)] + [half_of(x.shape) for x in parts],
         out_specs=half_of((2, 2 * bins, BAND)),
         scratch_shapes=[pltpu.VMEM((2, 2 * bins, TBLK), jnp.float32)],
-        compiler_params=pltpu.CompilerParams(vmem_limit_bytes=62 * MIB),
+        compiler_params=pltpu.CompilerParams(vmem_limit_bytes=24 * MIB),
         name="finish",
-    )(meta, count, *parts)
+    )(count, *parts)
 
 
 def skew_rows(matrix, keep):
@@ -472,8 +477,8 @@
     n_chan, n_freq = lax.axis_size("chan"), lax.axis_size("freq")
     count_a = length // TBLK
     rk = TBLK // 2 // n_freq
-    me, band = lax.axis_index("chan"), lax.axis_index("freq")
-    core, chip = me % 2, me // 2
+    me = lax.axis_index("chan")
+    chip = me // 2
 
     def moved(x, target):
         pairs = []
@@ -502,32 +507,44 @@
     quality_ext = lax.dynamic_slice_in_dim(quality_pad, me * ch, ch + BAND, 0)
     count = pair_count(quality_ext, lax.dynamic_slice_in_dim(offset_reach, me * ch, ch, 0), BAND)
 
-    meta = jnp.stack([core, band]).astype(jnp.int32)
     half = rk // 2
-    steps = count_a * half // block_bins(n_freq)
-    chunks = (steps // 2, steps - steps // 2)
-    pieces = spectra(
-        meta, strain, other, halos, quality_both.astype(jnp.float32)[None, :], n_freq, chunks
-    )
+    nb = block_bins(n_freq)
+    steps = count_a * half // nb
+    first = steps * 7 // 15
+    chunks = (first, steps - first)
+    parts = spectra(strain, other, halos, n_freq)
+    pieces = [parts[0]]
+    for d in range(1, n_freq):
+        pieces.append(moved(parts[d], lambda c, f, d=d: (c, f ^ d)))
+    usable = quality_both.astype(jnp.bfloat16)[None, :]
     blocks = []
-    for k in range(len(chunks)):
-        mine = pieces[k * n_freq : (k + 1) * n_freq]
-        own = [mine[0]]
-        for d in range(1, n_freq):
-            own.append(moved(mine[d], lambda c, f, d=d: (c, f ^ d)))
-        blocks.append(jnp.stack(own))
+    start = 0
+    for size in chunks:
+        rows = slice(start * 2 * nb, (start + size) * 2 * nb)
+        own = jnp.stack([x[rows] * usable for x in pieces])
+        blocks.append(
+            (own, moved(own, lambda c, f: (c + 2, f)), moved(own, lambda c, f: (c - 2, f)))
+        )
+        start += size
     results = []
-    for own in blocks:
-        nxt = moved(own, lambda c, f: (c - 2, f))
-        prev = moved(own, lambda c, f: (c + 2, f))
-        mine, theirs, far_mine, far_theirs = cross(meta, own, prev, nxt, reach_own, reach_prev)
+    for k, (own, prev, nxt) in enumerate(blocks):
+        far_type = jnp.bfloat16 if k == len(blocks) - 1 else jnp.float32
+        if k:
+            own, results[-4] = lax.optimization_barrier((own, results[-4]))
+        mine, theirs, far_mine, far_theirs = cross(
+            own, prev, nxt, reach_own, reach_prev, far_type
+        )
+        if k:
+            tied = lax.optimization_barrier((theirs, far_mine, far_theirs, *results[-3:]))
+            theirs, far_mine, far_theirs = tied[:3]
+            results[-3:] = tied[3:]
         results += [
             mine,
             moved(theirs, lambda c, f: (c ^ 1, f)),
             moved(far_mine, lambda c, f: (c - 2, f)),
             moved(far_theirs, lambda c, f: ((c ^ 1) - 2, f)),
         ]
-    return finish(meta, count[None, :], results, count_a, half)[None]
+    return finish(count[None, :], results, count_a, half)[None]
 
 
 def solution(mesh):

time: 131 us -> 119 us (0.908)
  Pallas kernels: 61.4 us -> 51.8 us
  waiting for transfers between devices: 14.2 us -> 21.6 us
  other arithmetic: 4.61 us -> 1.33 us
  starting transfers between devices: 43.6 us -> 40.4 us
  local copies, waits for them, and re-layouts: 5.37 us -> 2.89 us
    pallas_call x3, Pallas kernels: 58.6 us -> 50.3 us  [the longest x2 36.8 us: cross(): pl.pallas_call(functools.partial(cross_kernel, per), grid=(steps // per,)...]
    ppermute x21 -> x18, waiting for transfers between devices: 14.2 us -> 21.6 us  [moved(): return lax.ppermute(x, ('chan', 'freq'), pairs)]
    ppermute x21 -> x18, starting transfers between devices: 43.6 us -> 40.4 us  [moved(): return lax.ppermute(x, ('chan', 'freq'), pairs)]
    unnamed x38 -> x22, local copies, waits for them, and re-layouts: 3.47 us -> 1.56 us
    another operation x3 -> x4, other arithmetic: 2.6 us -> 1.14 us  [on_device(): own = jnp.stack([x[rows] * usable for x in pieces])]
    pallas_call x1, Pallas kernels: 2.83 us -> 1.44 us  [finish(): pl.pallas_call(functools.partial(finish_kernel, count_a, half, len(parts)...]
    broadcast_in_dim x1 -> x0, other arithmetic: 1.32 us -> none  [on_device(): quality_both.astype(jnp.float32)[None, :]]
  transfers between devices with their start and end apart: 21 -> 18, of which waited for: 9 -> 8; matrix products, arithmetic and copies ran while one was open for 4% -> 1% of each run, Pallas kernels for 35% -> 31%
where the time goes in v4:
time: 119 us; the launch traced here: 118 us
  Pallas kernels  51.8 us (44%)
  starting transfers between devices  40.4 us (34%)
  waiting for transfers between devices  21.6 us (18%)
  local copies, waits for them, and re-layouts  2.89 us (2%)
  other arithmetic  1.33 us (1%)
    ppermute x18, starting transfers between devices, moved(): return lax.ppermute(x, ('chan', 'freq'), pairs)  40.4 us
    pallas_call x2, Pallas kernels, cross(): pl.pallas_call(functools.partial(cross_kernel, per), grid=(steps // per,)...  36.8 us
    ppermute x18, waiting for transfers between devices, moved(): return lax.ppermute(x, ('chan', 'freq'), pairs)  21.6 us
    pallas_call x1, Pallas kernels, spectra(): pl.pallas_call(functools.partial(spectra_kernel, count_a, n_freq), grid=(...  13.6 us
  transfers between devices with their start and end apart: 18, of which 8 were waited for; matrix products, arithmetic and copies ran while one was open for 1% of the time, Pallas kernels for 31%

profile of v4, /device:TPU:9, one launch (start us, length us, event | category | flops | bytes accessed | tf_op | source)
XLA Modules:
  0.0 118.3 jit_solution(2840908497730800544)
XLA Ops:
  0.0 0.7 collective-permute-start
  0.7 0.8 fusion.10
  1.5 1.3 %collective-permute-start.4 = (bf16[64,256]{1,0:T(8,128)(2,1)S(1)}, bf16[64,256]{1,0:T(8,128)(2,1)S(1)}, u32[]{:S(2)}, u32[]{:S(2)}) collective-permute-start(bf16[64,256]{1,0:T(8,128)(2,1)S(1)} %get-tuple-element.45), channel_id=1, source_target_pairs={{1,4},{2,5},{3,6},{5,0},{6,1},{7,2},{9,12},{10,13},{11,14},{13,8},... | collective-permute-start | bytes 98312 | tf_op jit(solution)/shard_map/ppermute | solution.py:490
  2.7 1.3 %collective-permute-start.3 = (bf16[64,256]{1,0:T(8,128)(2,1)S(1)}, bf16[64,256]{1,0:T(8,128)(2,1)S(1)}, u32[]{:S(2)}, u32[]{:S(2)}) collective-permute-start(bf16[64,256]{1,0:T(8,128)(2,1)S(1)} %get-tuple-element.45), channel_id=1, source_target_pairs={{1,0},{2,1},{3,2},{5,4},{6,5},{7,6},{9,8},{10,9},{11,10},{13,12},{... | collective-permute-start | bytes 98312 | tf_op jit(solution)/shard_map/ppermute | solution.py:490
  4.0 0.0 copy-start.4
  4.1 0.0 copy-start.5
  4.1 4.9 %collective-permute-start.2 = (bf16[64,256]{1,0:T(8,128)(2,1)S(1)}, bf16[64,256]{1,0:T(8,128)(2,1)S(1)}, u32[]{:S(2)}, u32[]{:S(2)}) collective-permute-start(bf16[64,256]{1,0:T(8,128)(2,1)S(1)} %get-tuple-element.46), channel_id=1, source_target_pairs={{0,5},{1,6},{2,7},{4,1},{5,2},{6,3},{8,13},{9,14},{10,15},{12,9},{... | collective-permute-start | bytes 98312 | tf_op jit(solution)/shard_map/ppermute | solution.py:490
  9.0 4.5 %collective-permute-start.1 = (bf16[64,256]{1,0:T(8,128)(2,1)S(1)}, bf16[64,256]{1,0:T(8,128)(2,1)S(1)}, u32[]{:S(2)}, u32[]{:S(2)}) collective-permute-start(bf16[64,256]{1,0:T(8,128)(2,1)S(1)} %get-tuple-element.46), channel_id=1, source_target_pairs={{0,1},{1,2},{2,3},{4,5},{5,6},{6,7},{8,9},{9,10},{10,11},{12,13},{... | collective-permute-start | bytes 98312 | tf_op jit(solution)/shard_map/ppermute | solution.py:490
  13.5 0.0 collective-permute-done.4.hi_other
  13.5 0.0 copy-start.7
  13.5 0.0 collective-permute-done.3.hi_own
  13.6 0.0 copy-start.8
  13.6 0.0 collective-permute-done.2.lo_other
  13.6 0.0 copy-start.9
  13.6 0.9 collective-permute-done.1.lo_own
  14.5 0.0 collective-permute-done.other
  14.5 0.0 copy-done.7
  14.5 0.0 copy-done.8
  14.5 0.0 copy-done.9
  14.5 0.6 copy-done.10
  15.1 0.9 copy-done.6
  16.1 13.6 %spectra.1 = (bf16[960,128]{1,0:T(8,128)(2,1)}, bf16[960,128]{1,0:T(8,128)(2,1)}, bf16[960,128]{1,0:T(8,128)(2,1)}, bf16[960,128]{1,0:T(8,128)(2,1)}) custom-call(bf16[64,7680]{1,0:T(8,128)(2,1)} %own.1, bf16[64,7680]{1,0:T(8,128)(2,1)} %copy-done.6, bf16[64,256]{1,0:T(8,128)(2,1)} %copy-done.10, bf16[64,256]{1,0:T(8,128)(2,1)} %copy-done.9, ...), custom_call_target="tpu_custom_call" | custom-call | flops 6000000000 | bytes 4000000 | tf_op jit(solution)/shard_map/spectra/pallas_call | solution.py:185
  29.6 2.2 %collective-permute-start.5 = (bf16[960,128]{1,0:T(8,128)(2,1)}, bf16[960,128]{1,0:T(8,128)(2,1)S(1)}, u32[]{:S(2)}, u32[]{:S(2)}) collective-permute-start(bf16[960,128]{1,0:T(8,128)(2,1)} %get-tuple-element.26), channel_id=1, source_target_pairs={{0,1},{1,0},{2,3},{3,2},{4,5},{5,4},{6,7},{7,6},{8,9},{9,8},{10,11... | collective-permute-start | bytes 737288 | tf_op jit(solution)/shard_map/ppermute | solution.py:490
  31.8 1.0 collective-permute-start.6
  32.8 1.1 collective-permute-start.7
  33.9 0.0 copy-done.4
  33.9 0.1 fusion.9
  34.0 0.0 copy-done.5
  34.0 3.8 %collective-permute-done.5 = bf16[960,128]{1,0:T(8,128)(2,1)S(1)} collective-permute-done((bf16[960,128]{1,0:T(8,128)(2,1)}, bf16[960,128]{1,0:T(8,128)(2,1)S(1)}, u32[]{:S(2)}, u32[]{:S(2)}) %collective-permute-start.5) | collective-permute-done | bytes 245792 | tf_op jit(solution)/shard_map/ppermute | solution.py:490
  37.9 0.8 collective-permute-done.6
  38.7 6.2 %collective-permute-done.7 = bf16[960,128]{1,0:T(8,128)(2,1)S(1)} collective-permute-done((bf16[960,128]{1,0:T(8,128)(2,1)}, bf16[960,128]{1,0:T(8,128)(2,1)S(1)}, u32[]{:S(2)}, u32[]{:S(2)}) %collective-permute-start.7) | collective-permute-done | bytes 245792 | tf_op jit(solution)/shard_map/ppermute | solution.py:490
  44.9 1.0 multiply_bitcast_fusion.1
  45.9 0.1 pad_maximum_fusion.1.own_ref
  46.0 2.1 %collective-permute-start.9 = (bf16[4,448,128]{2,1,0:T(8,128)(2,1)S(1)}, bf16[4,448,128]{2,1,0:T(8,128)(2,1)S(1)}, u32[]{:S(2)}, u32[]{:S(2)}) collective-permute-start(bf16[4,448,128]{2,1,0:T(8,128)(2,1)S(1)} %pad_maximum_fusion.1.own_ref), channel_id=1, source_target_pairs={{8,0},{9,1},{10,2},{11,3},{12,4},{13,5},{14,6},{15,7},{16,8},{17,9... | collective-permute-start | bytes 1376264 | tf_op jit(solution)/shard_map/ppermute | solution.py:490
  48.0 3.2 %collective-permute-start.8 = (bf16[4,448,128]{2,1,0:T(8,128)(2,1)S(1)}, bf16[4,448,128]{2,1,0:T(8,128)(2,1)S(1)}, u32[]{:S(2)}, u32[]{:S(2)}) collective-permute-start(bf16[4,448,128]{2,1,0:T(8,128)(2,1)S(1)} %pad_maximum_fusion.1.own_ref), channel_id=1, source_target_pairs={{0,8},{1,9},{2,10},{3,11},{4,12},{5,13},{6,14},{7,15},{8,16},{9,17... | collective-permute-start | bytes 1376264 | tf_op jit(solution)/shard_map/ppermute | solution.py:490
  51.3 0.1 dynamic-slice_bitcast_fusion
  51.4 0.1 pad_maximum_fusion.own_ref
  51.5 2.1 %collective-permute-start.11 = (bf16[4,512,128]{2,1,0:T(8,128)(2,1)S(1)}, bf16[4,512,128]{2,1,0:T(8,128)(2,1)S(1)}, u32[]{:S(2)}, u32[]{:S(2)}) collective-permute-start(bf16[4,512,128]{2,1,0:T(8,128)(2,1)S(1)} %pad_maximum_fusion.own_ref), channel_id=1, source_target_pairs={{8,0},{9,1},{10,2},{11,3},{12,4},{13,5},{14,6},{15,7},{16,8},{17,9... | collective-permute-start | bytes 1572872 | tf_op jit(solution)/shard_map/ppermute | solution.py:490
  53.6 3.4 %collective-permute-start.10 = (bf16[4,512,128]{2,1,0:T(8,128)(2,1)S(1)}, bf16[4,512,128]{2,1,0:T(8,128)(2,1)S(1)}, u32[]{:S(2)}, u32[]{:S(2)}) collective-permute-start(bf16[4,512,128]{2,1,0:T(8,128)(2,1)S(1)} %pad_maximum_fusion.own_ref), channel_id=1, source_target_pairs={{0,8},{1,9},{2,10},{3,11},{4,12},{5,13},{6,14},{7,15},{8,16},{9,17... | collective-permute-start | bytes 1572872 | tf_op jit(solution)/shard_map/ppermute | solution.py:490
  56.9 1.5 %collective-permute-done.9.next_ref = bf16[4,448,128]{2,1,0:T(8,128)(2,1)S(1)} collective-permute-done((bf16[4,448,128]{2,1,0:T(8,128)(2,1)S(1)}, bf16[4,448,128]{2,1,0:T(8,128)(2,1)S(1)}, u32[]{:S(2)}, u32[]{:S(2)}) %collective-permute-start.9) | collective-permute-done | bytes 458784 | tf_op jit(solution)/shard_map/ppermute | solution.py:490
  58.4 1.8 %collective-permute-done.8.prev_ref = bf16[4,448,128]{2,1,0:T(8,128)(2,1)S(1)} collective-permute-done((bf16[4,448,128]{2,1,0:T(8,128)(2,1)S(1)}, bf16[4,448,128]{2,1,0:T(8,128)(2,1)S(1)}, u32[]{:S(2)}, u32[]{:S(2)}) %collective-permute-start.8) | collective-permute-done | bytes 458784 | tf_op jit(solution)/shard_map/ppermute | solution.py:490
  60.3 0.0 copy-done.2
  60.3 17.2 %cross.2 = (f32[2,14,32,128]{3,2,1,0:T(8,128)S(1)}, f32[2,14,32,128]{3,2,1,0:T(8,128)S(1)}, f32[2,14,16,128]{3,2,1,0:T(8,128)S(1)}, f32[2,14,16,128]{3,2,1,0:T(8,128)S(1)}) custom-call(f32[1,128]{1,0:T(1,128)S(1)} %get-tuple-element.48.reach_own, f32[1,128]{1,0:T(1,128)S(1)} %get-tuple-element.47.reach_prev, bf16[128,128]{1,0:T(8,128)(2,1)S(1)} %copy-done.2, ...), custom_call_target="tpu_custom_call" | custom-call | flops 14000000000 | bytes 2800000 | tf_op jit(solution)/shard_map/cross/pallas_call | solution.py:390
  77.5 1.9 %collective-permute-start.13 = (f32[2,14,16,128]{3,2,1,0:T(8,128)S(1)}, f32[2,14,16,128]{3,2,1,0:T(8,128)S(1)}, u32[]{:S(2)}, u32[]{:S(2)}) collective-permute-start(f32[2,14,16,128]{3,2,1,0:T(8,128)S(1)} %get-tuple-element.36), channel_id=1, source_target_pairs={{8,0},{9,1},{10,2},{11,3},{12,4},{13,5},{14,6},{15,7},{16,8},{17,9... | collective-permute-start | bytes 688136 | tf_op jit(solution)/shard_map/ppermute | solution.py:490
  79.4 5.2 %collective-permute-start.14 = (f32[2,14,16,128]{3,2,1,0:T(8,128)S(1)}, f32[2,14,16,128]{3,2,1,0:T(8,128)S(1)}, u32[]{:S(2)}, u32[]{:S(2)}) collective-permute-start(f32[2,14,16,128]{3,2,1,0:T(8,128)S(1)} %get-tuple-element.37), channel_id=1, source_target_pairs={{8,4},{9,5},{10,6},{11,7},{12,0},{13,1},{14,2},{15,3},{16,12},{17,... | collective-permute-start | bytes 688136 | tf_op jit(solution)/shard_map/ppermute | solution.py:490
  84.6 1.6 %collective-permute-start.12 = (f32[2,14,32,128]{3,2,1,0:T(8,128)S(1)}, f32[2,14,32,128]{3,2,1,0:T(8,128)S(1)}, u32[]{:S(2)}, u32[]{:S(2)}) collective-permute-start(f32[2,14,32,128]{3,2,1,0:T(8,128)S(1)} %get-tuple-element.35), channel_id=1, source_target_pairs={{0,4},{1,5},{2,6},{3,7},{4,0},{5,1},{6,2},{7,3},{8,12},{9,13},{10,... | collective-permute-start | bytes 1376264 | tf_op jit(solution)/shard_map/ppermute | solution.py:490
  86.2 0.0 collective-permute-done.11.next_ref
  86.2 0.0 collective-permute-done.10.prev_ref
  86.2 19.6 %cross.3 = (f32[2,16,32,128]{3,2,1,0:T(8,128)S(1)}, f32[2,16,32,128]{3,2,1,0:T(8,128)S(1)}, bf16[2,16,16,128]{3,2,1,0:T(8,128)(2,1)S(1)}, bf16[2,16,16,128]{3,2,1,0:T(8,128)(2,1)S(1)}) custom-call(f32[1,128]{1,0:T(1,128)S(1)} %get-tuple-element.48.reach_own, f32[1,128]{1,0:T(1,128)S(1)} %get-tuple-element.47.reach_prev, bf16[128,128]{1,0:T(8,128)(2,1)S(1)} %copy-done.2, ...), custom_call_target="tpu_custom_call" | custom-call | flops 16000000000 | bytes 3200000 | tf_op jit(solution)/shard_map/cross/pallas_call | solution.py:390
  105.8 0.0 collective-permute-done.13.rest_2_
  105.8 0.0 collective-permute-done.14.rest_3_
  105.8 0.0 collective-permute-done.12.rest_1_
  105.8 0.1 collective-permute-start.15
  106.0 0.1 dynamic_slice.15
  106.0 0.1 pad_dynamic-slice_fusion.1
  106.1 0.1 reshape.19
  106.2 0.2 reshape.20
  106.4 0.1 fusion.8
  106.5 1.9 %collective-permute-start.16 = (bf16[2,16,16,128]{3,2,1,0:T(8,128)(2,1)S(1)}, bf16[2,16,16,128]{3,2,1,0:T(8,128)(2,1)S(1)}, u32[]{:S(2)}, u32[]{:S(2)}) collective-permute-start(bf16[2,16,16,128]{3,2,1,0:T(8,128)(2,1)S(1)} %get-tuple-element.43), channel_id=1, source_target_pairs={{8,0},{9,1},{10,2},{11,3},{12,4},{13,5},{14,6},{15,7},{16,8},{17,9... | collective-permute-start | bytes 393224 | tf_op jit(solution)/shard_map/ppermute | solution.py:490
  108.5 1.9 %collective-permute-start.17 = (bf16[2,16,16,128]{3,2,1,0:T(8,128)(2,1)S(1)}, bf16[2,16,16,128]{3,2,1,0:T(8,128)(2,1)S(1)}, u32[]{:S(2)}, u32[]{:S(2)}) collective-permute-start(bf16[2,16,16,128]{3,2,1,0:T(8,128)(2,1)S(1)} %get-tuple-element.44), channel_id=1, source_target_pairs={{8,4},{9,5},{10,6},{11,7},{12,0},{13,1},{14,2},{15,3},{16,12},{17,... | collective-permute-start | bytes 393224 | tf_op jit(solution)/shard_map/ppermute | solution.py:490
  110.4 3.4 %collective-permute-done.16.rest_6_ = bf16[2,16,16,128]{3,2,1,0:T(8,128)(2,1)S(1)} collective-permute-done((bf16[2,16,16,128]{3,2,1,0:T(8,128)(2,1)S(1)}, bf16[2,16,16,128]{3,2,1,0:T(8,128)(2,1)S(1)}, u32[]{:S(2)}, u32[]{:S(2)}) %collective-permute-start.16) | collective-permute-done | bytes 131104 | tf_op jit(solution)/shard_map/ppermute | solution.py:490
  113.8 3.0 %collective-permute-done.17.rest_7_ = bf16[2,16,16,128]{3,2,1,0:T(8,128)(2,1)S(1)} collective-permute-done((bf16[2,16,16,128]{3,2,1,0:T(8,128)(2,1)S(1)}, bf16[2,16,16,128]{3,2,1,0:T(8,128)(2,1)S(1)}, u32[]{:S(2)}, u32[]{:S(2)}) %collective-permute-start.17) | collective-permute-done | bytes 131104 | tf_op jit(solution)/shard_map/ppermute | solution.py:490
  116.8 0.0 collective-permute-done.15.rest_5_
  116.8 1.4 %finish.1 = f32[2,960,256]{2,1,0:T(8,128)} custom-call(f32[1,256]{1,0:T(1,128)S(1)} %bitcast.22, f32[2,14,32,128]{3,2,1,0:T(8,128)S(1)} %get-tuple-element.30.rest_0_, f32[2,14,32,128]{3,2,1,0:T(8,128)S(1)} %collective-permute-done.12.rest_1_, f32[2,14,16,128]{3,2,1,0:T(8,128)S(1)} %collective-permute-done.13.rest_2_, ...), custom_call_target="tpu_custom_call" | custom-call | tf_op jit(solution)/shard_map/finish/pallas_call | solution.py:445
  (15 shorter events, 0.1 us)
Async XLA Ops:
  0.0 14.5 %collective-permute-start = (bf16[64,7680]{1,0:T(8,128)(2,1)}, bf16[64,7680]{1,0:T(8,128)(2,1)S(1)}, u32[]{:S(2)}, u32[]{:S(2)}) collective-permute-start(bf16[64,7680]{1,0:T(8,128)(2,1)} %own.1), channel_id=1, source_target_pairs={{0,4},{1,5},{2,6},{3,7},{4,0},{5,1},{6,2},{7,3},{8,12},{9,13},{10,... | collective-permute-start | bytes 2949128 | tf_op jit(solution)/shard_map/ppermute | solution.py:490
  1.5 12.1 %collective-permute-start.4 = (bf16[64,256]{1,0:T(8,128)(2,1)S(1)}, bf16[64,256]{1,0:T(8,128)(2,1)S(1)}, u32[]{:S(2)}, u32[]{:S(2)}) collective-permute-start(bf16[64,256]{1,0:T(8,128)(2,1)S(1)} %get-tuple-element.45), channel_id=1, source_target_pairs={{1,4},{2,5},{3,6},{5,0},{6,1},{7,2},{9,12},{10,13},{11,14},{13,8},... | collective-permute-start | bytes 98312 | tf_op jit(solution)/shard_map/ppermute | solution.py:490
  2.7 10.8 %collective-permute-start.3 = (bf16[64,256]{1,0:T(8,128)(2,1)S(1)}, bf16[64,256]{1,0:T(8,128)(2,1)S(1)}, u32[]{:S(2)}, u32[]{:S(2)}) collective-permute-start(bf16[64,256]{1,0:T(8,128)(2,1)S(1)} %get-tuple-element.45), channel_id=1, source_target_pairs={{1,0},{2,1},{3,2},{5,4},{6,5},{7,6},{9,8},{10,9},{11,10},{13,12},{... | collective-permute-start | bytes 98312 | tf_op jit(solution)/shard_map/ppermute | solution.py:490
  4.0 29.9 %copy-start.4 = (s32[512]{0:T(512)S(1)}, s32[512]{0:T(512)}, u32[]{:S(2)}) copy-start(s32[512]{0:T(512)} %param.15) | copy-start | bytes 6148
  4.1 30.0 %copy-start.5 = (s32[512]{0:T(512)S(1)}, s32[512]{0:T(512)}, u32[]{:S(2)}) copy-start(s32[512]{0:T(512)} %param.16) | copy-start | bytes 6148
  4.1 9.5 %collective-permute-start.2 = (bf16[64,256]{1,0:T(8,128)(2,1)S(1)}, bf16[64,256]{1,0:T(8,128)(2,1)S(1)}, u32[]{:S(2)}, u32[]{:S(2)}) collective-permute-start(bf16[64,256]{1,0:T(8,128)(2,1)S(1)} %get-tuple-element.46), channel_id=1, source_target_pairs={{0,5},{1,6},{2,7},{4,1},{5,2},{6,3},{8,13},{9,14},{10,15},{12,9},{... | collective-permute-start | bytes 98312 | tf_op jit(solution)/shard_map/ppermute | solution.py:490
  9.0 5.6 %collective-permute-start.1 = (bf16[64,256]{1,0:T(8,128)(2,1)S(1)}, bf16[64,256]{1,0:T(8,128)(2,1)S(1)}, u32[]{:S(2)}, u32[]{:S(2)}) collective-permute-start(bf16[64,256]{1,0:T(8,128)(2,1)S(1)} %get-tuple-element.46), channel_id=1, source_target_pairs={{0,1},{1,2},{2,3},{4,5},{5,6},{6,7},{8,9},{9,10},{10,11},{12,13},{... | collective-permute-start | bytes 98312 | tf_op jit(solution)/shard_map/ppermute | solution.py:490
  13.5 1.0 copy-start.7
  13.6 1.0 copy-start.8
  13.6 1.0 copy-start.9
  14.5 0.6 copy-start.10
  15.1 0.9 copy-start.6
  29.6 21.7 %copy-start.3 = (bf16[960,128]{1,0:T(8,128)(2,1)S(1)}, bf16[960,128]{1,0:T(8,128)(2,1)}, u32[]{:S(2)}) copy-start(bf16[960,128]{1,0:T(8,128)(2,1)} %get-tuple-element.25) | copy-start | bytes 737284
  29.6 8.2 %collective-permute-start.5 = (bf16[960,128]{1,0:T(8,128)(2,1)}, bf16[960,128]{1,0:T(8,128)(2,1)S(1)}, u32[]{:S(2)}, u32[]{:S(2)}) collective-permute-start(bf16[960,128]{1,0:T(8,128)(2,1)} %get-tuple-element.26), channel_id=1, source_target_pairs={{0,1},{1,0},{2,3},{3,2},{4,5},{5,4},{6,7},{7,6},{8,9},{9,8},{10,11... | collective-permute-start | bytes 737288 | tf_op jit(solution)/shard_map/ppermute | solution.py:490
  31.8 6.8 %collective-permute-start.6 = (bf16[960,128]{1,0:T(8,128)(2,1)}, bf16[960,128]{1,0:T(8,128)(2,1)S(1)}, u32[]{:S(2)}, u32[]{:S(2)}) collective-permute-start(bf16[960,128]{1,0:T(8,128)(2,1)} %get-tuple-element.27), channel_id=1, source_target_pairs={{0,2},{1,3},{2,0},{3,1},{4,6},{5,7},{6,4},{7,5},{8,10},{9,11},{10,... | collective-permute-start | bytes 737288 | tf_op jit(solution)/shard_map/ppermute | solution.py:490
  32.8 12.1 %collective-permute-start.7 = (bf16[960,128]{1,0:T(8,128)(2,1)}, bf16[960,128]{1,0:T(8,128)(2,1)S(1)}, u32[]{:S(2)}, u32[]{:S(2)}) collective-permute-start(bf16[960,128]{1,0:T(8,128)(2,1)} %get-tuple-element.28), channel_id=1, source_target_pairs={{0,3},{1,2},{2,1},{3,0},{4,7},{5,6},{6,5},{7,4},{8,11},{9,10},{10,... | collective-permute-start | bytes 737288 | tf_op jit(solution)/shard_map/ppermute | solution.py:490
  44.9 15.3 %copy-start = (bf16[16,16,256]{2,1,0:T(8,128)(2,1)S(1)}, bf16[16,16,256]{2,1,0:T(8,128)(2,1)}, u32[]{:S(2)}) copy-start(bf16[16,16,256]{2,1,0:T(8,128)(2,1)} %constant.59.clone.pick_ref) | copy-start | bytes 393220
  44.9 15.3 %copy-start.1 = (bf16[16,16,128]{2,1,0:T(8,128)(2,1)S(1)}, bf16[16,16,128]{2,1,0:T(8,128)(2,1)}, u32[]{:S(2)}) copy-start(bf16[16,16,128]{2,1,0:T(8,128)(2,1)} %constant.60.clone.cut_ref) | copy-start | bytes 196612
  44.9 15.3 %copy-start.2 = (bf16[128,128]{1,0:T(8,128)(2,1)S(1)}, bf16[128,128]{1,0:T(8,128)(2,1)}, u32[]{:S(2)}) copy-start(bf16[128,128]{1,0:T(8,128)(2,1)} %constant.58.clone.turn_ref) | copy-start | bytes 98308
  46.0 12.5 %collective-permute-start.9 = (bf16[4,448,128]{2,1,0:T(8,128)(2,1)S(1)}, bf16[4,448,128]{2,1,0:T(8,128)(2,1)S(1)}, u32[]{:S(2)}, u32[]{:S(2)}) collective-permute-start(bf16[4,448,128]{2,1,0:T(8,128)(2,1)S(1)} %pad_maximum_fusion.1.own_ref), channel_id=1, source_target_pairs={{8,0},{9,1},{10,2},{11,3},{12,4},{13,5},{14,6},{15,7},{16,8},{17,9... | collective-permute-start | bytes 1376264 | tf_op jit(solution)/shard_map/ppermute | solution.py:490
  48.0 12.2 %collective-permute-start.8 = (bf16[4,448,128]{2,1,0:T(8,128)(2,1)S(1)}, bf16[4,448,128]{2,1,0:T(8,128)(2,1)S(1)}, u32[]{:S(2)}, u32[]{:S(2)}) collective-permute-start(bf16[4,448,128]{2,1,0:T(8,128)(2,1)S(1)} %pad_maximum_fusion.1.own_ref), channel_id=1, source_target_pairs={{0,8},{1,9},{2,10},{3,11},{4,12},{5,13},{6,14},{7,15},{8,16},{9,17... | collective-permute-start | bytes 1376264 | tf_op jit(solution)/shard_map/ppermute | solution.py:490
  51.5 34.8 %collective-permute-start.11 = (bf16[4,512,128]{2,1,0:T(8,128)(2,1)S(1)}, bf16[4,512,128]{2,1,0:T(8,128)(2,1)S(1)}, u32[]{:S(2)}, u32[]{:S(2)}) collective-permute-start(bf16[4,512,128]{2,1,0:T(8,128)(2,1)S(1)} %pad_maximum_fusion.own_ref), channel_id=1, source_target_pairs={{8,0},{9,1},{10,2},{11,3},{12,4},{13,5},{14,6},{15,7},{16,8},{17,9... | collective-permute-start | bytes 1572872 | tf_op jit(solution)/shard_map/ppermute | solution.py:490
  53.6 32.6 %collective-permute-start.10 = (bf16[4,512,128]{2,1,0:T(8,128)(2,1)S(1)}, bf16[4,512,128]{2,1,0:T(8,128)(2,1)S(1)}, u32[]{:S(2)}, u32[]{:S(2)}) collective-permute-start(bf16[4,512,128]{2,1,0:T(8,128)(2,1)S(1)} %pad_maximum_fusion.own_ref), channel_id=1, source_target_pairs={{0,8},{1,9},{2,10},{3,11},{4,12},{5,13},{6,14},{7,15},{8,16},{9,17... | collective-permute-start | bytes 1572872 | tf_op jit(solution)/shard_map/ppermute | solution.py:490
  77.5 28.4 %collective-permute-start.13 = (f32[2,14,16,128]{3,2,1,0:T(8,128)S(1)}, f32[2,14,16,128]{3,2,1,0:T(8,128)S(1)}, u32[]{:S(2)}, u32[]{:S(2)}) collective-permute-start(f32[2,14,16,128]{3,2,1,0:T(8,128)S(1)} %get-tuple-element.36), channel_id=1, source_target_pairs={{8,0},{9,1},{10,2},{11,3},{12,4},{13,5},{14,6},{15,7},{16,8},{17,9... | collective-permute-start | bytes 688136 | tf_op jit(solution)/shard_map/ppermute | solution.py:490
  79.4 26.4 %collective-permute-start.14 = (f32[2,14,16,128]{3,2,1,0:T(8,128)S(1)}, f32[2,14,16,128]{3,2,1,0:T(8,128)S(1)}, u32[]{:S(2)}, u32[]{:S(2)}) collective-permute-start(f32[2,14,16,128]{3,2,1,0:T(8,128)S(1)} %get-tuple-element.37), channel_id=1, source_target_pairs={{8,4},{9,5},{10,6},{11,7},{12,0},{13,1},{14,2},{15,3},{16,12},{17,... | collective-permute-start | bytes 688136 | tf_op jit(solution)/shard_map/ppermute | solution.py:490
  84.6 21.2 %collective-permute-start.12 = (f32[2,14,32,128]{3,2,1,0:T(8,128)S(1)}, f32[2,14,32,128]{3,2,1,0:T(8,128)S(1)}, u32[]{:S(2)}, u32[]{:S(2)}) collective-permute-start(f32[2,14,32,128]{3,2,1,0:T(8,128)S(1)} %get-tuple-element.35), channel_id=1, source_target_pairs={{0,4},{1,5},{2,6},{3,7},{4,0},{5,1},{6,2},{7,3},{8,12},{9,13},{10,... | collective-permute-start | bytes 1376264 | tf_op jit(solution)/shard_map/ppermute | solution.py:490
  105.8 11.0 %collective-permute-start.15 = (f32[2,16,32,128]{3,2,1,0:T(8,128)S(1)}, f32[2,16,32,128]{3,2,1,0:T(8,128)S(1)}, u32[]{:S(2)}, u32[]{:S(2)}) collective-permute-start(f32[2,16,32,128]{3,2,1,0:T(8,128)S(1)} %get-tuple-element.42), channel_id=1, source_target_pairs={{0,4},{1,5},{2,6},{3,7},{4,0},{5,1},{6,2},{7,3},{8,12},{9,13},{10,... | collective-permute-start | bytes 1572872 | tf_op jit(solution)/shard_map/ppermute | solution.py:490
  106.5 7.2 %collective-permute-start.16 = (bf16[2,16,16,128]{3,2,1,0:T(8,128)(2,1)S(1)}, bf16[2,16,16,128]{3,2,1,0:T(8,128)(2,1)S(1)}, u32[]{:S(2)}, u32[]{:S(2)}) collective-permute-start(bf16[2,16,16,128]{3,2,1,0:T(8,128)(2,1)S(1)} %get-tuple-element.43), channel_id=1, source_target_pairs={{8,0},{9,1},{10,2},{11,3},{12,4},{13,5},{14,6},{15,7},{16,8},{17,9... | collective-permute-start | bytes 393224 | tf_op jit(solution)/shard_map/ppermute | solution.py:490
  108.5 8.3 %collective-permute-start.17 = (bf16[2,16,16,128]{3,2,1,0:T(8,128)(2,1)S(1)}, bf16[2,16,16,128]{3,2,1,0:T(8,128)(2,1)S(1)}, u32[]{:S(2)}, u32[]{:S(2)}) collective-permute-start(bf16[2,16,16,128]{3,2,1,0:T(8,128)(2,1)S(1)} %get-tuple-element.44), channel_id=1, source_target_pairs={{8,4},{9,5},{10,6},{11,7},{12,0},{13,1},{14,2},{15,3},{16,12},{17,... | collective-permute-start | bytes 393224 | tf_op jit(solution)/shard_map/ppermute | solution.py:490

commit v5 on v4

--- a/solution.py
+++ b/solution.py
@@ -70,12 +70,13 @@
 def spectra_kernel(
     count_a,
     n_freq,
+    chunks,
     own,
     other,
-    lo_own,
-    lo_other,
-    hi_own,
-    hi_other,
+    near_own,
+    near_other,
+    off_own,
+    off_other,
     taps,
     box,
     first,
@@ -83,7 +84,7 @@
     second,
     *rest,
 ):
-    outs = rest[:n_freq]
+    outs = rest[: n_freq * len(chunks)]
     padded, filtered, magnitude, whitened, tw_re, tw_im = rest[len(outs) :]
     core, band = lax.axis_index("chan") % 2, lax.axis_index("freq")
     ch = own.shape[0]
@@ -91,7 +92,13 @@
     pad_a = first.shape[1]
     dot = functools.partial(jnp.dot, preferred_element_type=jnp.float32)
 
-    for which, (lo, mid, hi) in enumerate(((lo_own, own, hi_own), (lo_other, other, hi_other))):
+    even = band % 2 == 0
+    sides = ((own, near_own, off_own), (other, near_other, off_other))
+    for which, (mid, near, off) in enumerate(sides):
+        near, off = near[...], off[...]
+        lo, hi = jnp.where(even, off, near), jnp.where(even, near, off)
+        lo = jnp.where(band > 0, lo, jnp.zeros_like(lo))
+        hi = jnp.where(band < n_freq - 1, hi, jnp.zeros_like(hi))
         base = core if which == 0 else 1 - core
         rows = pl.ds(pl.multiple_of(base * ch, ch), ch)
         for j in range(2):
@@ -149,10 +156,10 @@
     scale = 1.0 / math.sqrt(count_a * TBLK)
     turn = jnp.concatenate([second[band ^ d, core] for d in range(n_freq)], axis=0)
 
-    def bins(i):
+    def bins(k, start, i):
         results = []
         for n in range(group):
-            k1 = i * group + n
+            k1 = (start + i) * group + n
             re = tw_re[pl.ds(k1, both, stride=pad_a), :].astype(jnp.bfloat16)
             im = tw_im[pl.ds(k1, both, stride=pad_a), :].astype(jnp.bfloat16)
             result = lax.dot_general(
@@ -166,24 +173,28 @@
         for d in range(n_freq):
             starts = [d * rk + p * half for p in range(2)]
             block = jnp.concatenate([r[s : s + half] for s in starts for r in results], axis=0)
-            outs[d][rows, :] = block.astype(jnp.bfloat16)
-
-    for i in range(count_a // group):
-        bins(i)
-
-
-def spectra(own, other, halos, n_freq):
+            outs[k * n_freq + d][rows, :] = block.astype(jnp.bfloat16)
+
+    start = 0
+    for k, size in enumerate(chunks):
+        for i in range(size):
+            bins(k, start, i)
+        start += size
+
+
+def spectra(own, other, halos, n_freq, chunks):
     ch, length = own.shape
     count_a = length // TBLK
     first, twist, second = dft_tables(count_a, n_freq)
     rk = second.shape[2]
     pad_a = first.shape[1]
     both = 2 * ch
-    shapes = [(count_a * rk, both)] * n_freq
+    rows = 2 * block_bins(n_freq)
+    shapes = [(size * rows, both) for size in chunks for _ in range(n_freq)]
     tables = (stencil_table(False), stencil_table(True), first, twist, second)
     operands = (own, other, *halos, *(jnp.asarray(t) for t in tables))
     return pl.pallas_call(
-        functools.partial(spectra_kernel, count_a, n_freq),
+        functools.partial(spectra_kernel, count_a, n_freq, chunks),
         grid=(1,),
         out_shape=[jax.ShapeDtypeStruct(shape, jnp.bfloat16) for shape in shapes],
         in_specs=[whole(x.shape) for x in operands],
@@ -212,8 +223,8 @@
     pick_ref,
     cut_ref,
     own_ref,
-    prev_ref,
-    next_ref,
+    near_chip_ref,
+    off_chip_ref,
     mine_ref,
     theirs_ref,
     far_mine_ref,
@@ -231,7 +242,19 @@
     depth = turn_ref.shape[0]
     nb = pick_ref.shape[0]
     slabs = both // 8
-    first_core = lax.axis_index("chan") % 2 == 0
+    me = lax.axis_index("chan")
+    first_core = me % 2 == 0
+    chip = me // 2
+    last_chip = lax.axis_size("chan") // 2 - 1
+
+    def beside(j):
+        rows = slice(j * rb, (j + 1) * rb)
+        near, off = near_chip_ref[:, rows, :], off_chip_ref[:, rows, :]
+        even = chip % 2 == 0
+        prev, nxt = jnp.where(even, off, near), jnp.where(even, near, off)
+        prev = jnp.where(chip > 0, prev, jnp.zeros_like(prev))
+        nxt = jnp.where(chip < last_chip, nxt, jnp.zeros_like(nxt))
+        return prev, nxt
 
     @pl.when(step == 0)
     def _():
@@ -266,7 +289,8 @@
         return jnp.stack([re, im], axis=1).reshape(slabs, 16, depth).astype(jnp.bfloat16)
 
     def dots(j):
-        own, nxt, prev = (r[:, j * rb : (j + 1) * rb, :].reshape(depth, both) for r in (own_ref, next_ref, prev_ref))
+        own = own_ref[:, j * rb : (j + 1) * rb, :].reshape(depth, both)
+        prev, nxt = (x.reshape(depth, both) for x in beside(j))
         left = jnp.concatenate([left_rows(own), left_rows(prev)], axis=2)
         pick = pick_ref[...]
 
@@ -312,8 +336,9 @@
         def split(x):
             return x[:nb], x[nb:]
 
-        lefts = [split(prev_ref[s, j * rb : (j + 1) * rb].astype(jnp.float32)) for s in range(n_seg)]
-        rights = [split(next_ref[s, j * rb : (j + 1) * rb].astype(jnp.float32)) for s in range(n_seg)]
+        prev, nxt = (x.astype(jnp.float32) for x in beside(j))
+        lefts = [split(prev[s]) for s in range(n_seg)]
+        rights = [split(nxt[s]) for s in range(n_seg)]
         pieces = []
         for d in range(1, 8):
             re = im = None
@@ -363,7 +388,7 @@
         diag(j, margin[j])
 
 
-def cross(own, prev, nxt, reach_own, reach_prev, far_type):
+def cross(own, near_chip, off_chip, reach_own, reach_prev, far_type):
     n_seg, rows, both = own.shape
     nb = block_bins(n_seg)
     rb = 2 * nb
@@ -408,7 +433,7 @@
             flops=10**9 * steps, bytes_accessed=2 * 10**5 * steps, transcendentals=0
         ),
         name="cross",
-    )(*fixed, own, prev, nxt)
+    )(*fixed, own, near_chip, off_chip)
 
 
 def finish_kernel(count_a, half, chunks, count, *rest):
@@ -489,13 +514,18 @@
                     pairs.append((c * n_freq + f, to[0] * n_freq + to[1]))
         return lax.ppermute(x, ("chan", "freq"), pairs)
 
+    def paired(at, count, off):
+        to = ((at + off) ^ 1) - off
+        return to if 0 <= to < count else at
+
     tail, head = strain[:, length - 2 * TBLK :], strain[:, : 2 * TBLK]
+    even = lax.axis_index("freq") % 2 == 0
+    ends = (jnp.where(even, tail, head), jnp.where(even, head, tail))
     other = moved(strain, lambda c, f: (c ^ 1, f))
     halos = [
-        moved(tail, lambda c, f: (c, f + 1)),
-        moved(tail, lambda c, f: (c ^ 1, f + 1)),
-        moved(head, lambda c, f: (c, f - 1)),
-        moved(head, lambda c, f: (c ^ 1, f - 1)),
+        moved(ends[off], lambda c, f, o=off, k=flip: (c ^ k, paired(f, n_freq, o)))
+        for off in range(2)
+        for flip in range(2)
     ]
 
     quality_pad = jnp.pad(quality, (0, BAND + both))
@@ -510,29 +540,30 @@
     half = rk // 2
     nb = block_bins(n_freq)
     steps = count_a * half // nb
-    first = steps * 7 // 15
+    first = steps // 3
     chunks = (first, steps - first)
-    parts = spectra(strain, other, halos, n_freq)
-    pieces = [parts[0]]
-    for d in range(1, n_freq):
-        pieces.append(moved(parts[d], lambda c, f, d=d: (c, f ^ d)))
+    parts = spectra(strain, other, halos, n_freq, chunks)
     usable = quality_both.astype(jnp.bfloat16)[None, :]
     blocks = []
-    start = 0
-    for size in chunks:
-        rows = slice(start * 2 * nb, (start + size) * 2 * nb)
-        own = jnp.stack([x[rows] * usable for x in pieces])
+    for k in range(len(chunks)):
+        pieces = list(parts[k * n_freq : (k + 1) * n_freq])
+        for d in range(1, n_freq):
+            pieces[d] = moved(pieces[d], lambda c, f, d=d: (c, f ^ d))
+        own = jnp.stack([x * usable for x in pieces])
         blocks.append(
-            (own, moved(own, lambda c, f: (c + 2, f)), moved(own, lambda c, f: (c - 2, f)))
+            [own]
+            + [
+                moved(own, lambda c, f, o=off: (2 * paired(c // 2, n_chan // 2, o) + c % 2, f))
+                for off in range(2)
+            ]
         )
-        start += size
     results = []
-    for k, (own, prev, nxt) in enumerate(blocks):
+    for k, (own, near_chip, off_chip) in enumerate(blocks):
         far_type = jnp.bfloat16 if k == len(blocks) - 1 else jnp.float32
         if k:
             own, results[-4] = lax.optimization_barrier((own, results[-4]))
         mine, theirs, far_mine, far_theirs = cross(
-            own, prev, nxt, reach_own, reach_prev, far_type
+            own, near_chip, off_chip, reach_own, reach_prev, far_type
         )
         if k:
             tied = lax.optimization_barrier((theirs, far_mine, far_theirs, *results[-3:]))

time: 119 us -> 105 us (0.88)
  waiting for transfers between devices: 21.6 us -> 10.9 us
  starting transfers between devices: 40.4 us -> 33.2 us
  other arithmetic: 1.33 us -> 3.72 us
    ppermute x18 -> x21, waiting for transfers between devices: 21.6 us -> 10.9 us  [moved(): return lax.ppermute(x, ('chan', 'freq'), pairs)]
    ppermute x18 -> x21, starting transfers between devices: 40.4 us -> 33.2 us  [moved(): return lax.ppermute(x, ('chan', 'freq'), pairs)]
  transfers between devices with their start and end apart: 18 -> 21, of which waited for: 8 -> 5; matrix products, arithmetic and copies ran while one was open for 1% -> 5% of each run, Pallas kernels for 31% -> 37%
where the time goes in v5:
time: 105 us; the launch traced here: 104 us
  Pallas kernels  52.7 us (50%)
  starting transfers between devices  33.2 us (32%)
  waiting for transfers between devices  10.9 us (10%)
  other arithmetic  3.72 us (4%)
  local copies, waits for them, and re-layouts  2.8 us (3%)
    pallas_call x2, Pallas kernels, cross(): pl.pallas_call(functools.partial(cross_kernel, per), grid=(steps // per,)...  37.9 us
    ppermute x21, starting transfers between devices, moved(): return lax.ppermute(x, ('chan', 'freq'), pairs)  33.2 us
    pallas_call x1, Pallas kernels, spectra(): pl.pallas_call(functools.partial(spectra_kernel, count_a, n_freq, chunks)...  13.4 us
    ppermute x21, waiting for transfers between devices, moved(): return lax.ppermute(x, ('chan', 'freq'), pairs)  10.9 us
  transfers between devices with their start and end apart: 21, of which 5 were waited for; matrix products, arithmetic and copies ran while one was open for 5% of the time, Pallas kernels for 37%

profile of v5, /device:TPU:9, one launch (start us, length us, event | category | flops | bytes accessed | tf_op | source)
XLA Modules:
  0.0 103.6 jit_solution(1270592907801779107)
XLA Ops:
  0.0 0.7 collective-permute-start
  0.7 0.8 broadcast_select_fusion
  1.5 1.3 %collective-permute-start.1 = (bf16[64,256]{1,0:T(8,128)(2,1)S(1)}, bf16[64,256]{1,0:T(8,128)(2,1)S(1)}, u32[]{:S(2)}, u32[]{:S(2)}) collective-permute-start(bf16[64,256]{1,0:T(8,128)(2,1)S(1)} %get-tuple-element.54), channel_id=1, source_target_pairs={{0,1},{1,0},{2,3},{3,2},{4,5},{5,4},{6,7},{7,6},{8,9},{9,8},{10,11... | collective-permute-start | bytes 98312 | tf_op jit(solution)/shard_map/ppermute | solution.py:515
  2.7 0.4 collective-permute-start.2
  3.2 0.7 collective-permute-start.3
  3.8 0.3 collective-permute-start.4
  4.1 0.7 pad_convert_fusion
  4.8 0.1 dynamic-slice_bitcast_fusion
  4.9 0.0 collective-permute-done.1.near_own
  4.9 1.2 %collective-permute-done.2.near_other = bf16[64,256]{1,0:T(8,128)(2,1)S(1)} collective-permute-done((bf16[64,256]{1,0:T(8,128)(2,1)S(1)}, bf16[64,256]{1,0:T(8,128)(2,1)S(1)}, u32[]{:S(2)}, u32[]{:S(2)}) %collective-permute-start.2) | collective-permute-done | bytes 32800 | tf_op jit(solution)/shard_map/ppermute | solution.py:515
  6.1 0.0 collective-permute-done.3.off_own
  6.1 0.0 collective-permute-done.4.off_other
  6.1 0.0 copy-start.8
  6.1 0.0 collective-permute-done.other
  6.1 0.0 copy-done.5
  6.1 0.6 copy-done.6
  6.7 0.0 copy-done.7
  6.7 0.0 copy-done.8
  6.7 0.9 copy-done.4
  7.7 13.4 %spectra.1 = (bf16[320,128]{1,0:T(8,128)(2,1)}, bf16[320,128]{1,0:T(8,128)(2,1)}, bf16[320,128]{1,0:T(8,128)(2,1)}, bf16[320,128]{1,0:T(8,128)(2,1)}, bf16[640,1...) custom-call(bf16[64,7680]{1,0:T(8,128)(2,1)} %own.1, ...), custom_call_target="tpu_custom_call" | custom-call | flops 6000000000 | bytes 4000000 | tf_op jit(solution)/shard_map/spectra/pallas_call | solution.py:196
  21.1 1.5 %collective-permute-start.10 = (bf16[320,128]{1,0:T(8,128)(2,1)}, bf16[320,128]{1,0:T(8,128)(2,1)S(1)}, u32[]{:S(2)}, u32[]{:S(2)}) collective-permute-start(bf16[320,128]{1,0:T(8,128)(2,1)} %get-tuple-element.36), channel_id=1, source_target_pairs={{0,3},{1,2},{2,1},{3,0},{4,7},{5,6},{6,5},{7,4},{8,11},{9,10},{10,... | collective-permute-start | bytes 245768 | tf_op jit(solution)/shard_map/ppermute | solution.py:515
  22.6 5.6 %collective-permute-start.8 = (bf16[320,128]{1,0:T(8,128)(2,1)}, bf16[320,128]{1,0:T(8,128)(2,1)S(1)}, u32[]{:S(2)}, u32[]{:S(2)}) collective-permute-start(bf16[320,128]{1,0:T(8,128)(2,1)} %get-tuple-element.34), channel_id=1, source_target_pairs={{0,1},{1,0},{2,3},{3,2},{4,5},{5,4},{6,7},{7,6},{8,9},{9,8},{10,11... | collective-permute-start | bytes 245768 | tf_op jit(solution)/shard_map/ppermute | solution.py:515
  28.2 0.0 collective-permute-start.9
  28.2 0.1 fusion.3
  28.3 1.5 %collective-permute-start.5 = (bf16[640,128]{1,0:T(8,128)(2,1)}, bf16[640,128]{1,0:T(8,128)(2,1)S(1)}, u32[]{:S(2)}, u32[]{:S(2)}) collective-permute-start(bf16[640,128]{1,0:T(8,128)(2,1)} %get-tuple-element.30), channel_id=1, source_target_pairs={{0,1},{1,0},{2,3},{3,2},{4,5},{5,4},{6,7},{7,6},{8,9},{9,8},{10,11... | collective-permute-start | bytes 491528 | tf_op jit(solution)/shard_map/ppermute | solution.py:515
  29.8 0.0 collective-permute-start.6
  29.8 0.0 collective-permute-done.10
  29.8 1.2 %collective-permute-start.7 = (bf16[640,128]{1,0:T(8,128)(2,1)}, bf16[640,128]{1,0:T(8,128)(2,1)S(1)}, u32[]{:S(2)}, u32[]{:S(2)}) collective-permute-start(bf16[640,128]{1,0:T(8,128)(2,1)} %get-tuple-element.32), channel_id=1, source_target_pairs={{0,3},{1,2},{2,1},{3,0},{4,7},{5,6},{6,5},{7,4},{8,11},{9,10},{10,... | collective-permute-start | bytes 491528 | tf_op jit(solution)/shard_map/ppermute | solution.py:515
  31.0 1.3 %collective-permute-done.8 = bf16[320,128]{1,0:T(8,128)(2,1)S(1)} collective-permute-done((bf16[320,128]{1,0:T(8,128)(2,1)}, bf16[320,128]{1,0:T(8,128)(2,1)S(1)}, u32[]{:S(2)}, u32[]{:S(2)}) %collective-permute-start.8) | collective-permute-done | bytes 81952 | tf_op jit(solution)/shard_map/ppermute | solution.py:515
  32.3 0.0 collective-permute-done.9
  32.3 1.0 multiply_bitcast_fusion.7
  33.4 0.3 collective-permute-start.11
  33.6 4.5 %collective-permute-start.12 = (bf16[4,320,128]{2,1,0:T(8,128)(2,1)S(1)}, bf16[4,320,128]{2,1,0:T(8,128)(2,1)S(1)}, u32[]{:S(2)}, u32[]{:S(2)}) collective-permute-start(bf16[4,320,128]{2,1,0:T(8,128)(2,1)S(1)} %pad_maximum_fusion.1.own_ref), channel_id=1, source_target_pairs={{0,0},{1,1},{2,2},{3,3},{4,4},{5,5},{6,6},{7,7},{8,16},{9,17},{10,... | collective-permute-start | bytes 983048 | tf_op jit(solution)/shard_map/ppermute | solution.py:515
  38.1 0.0 collective-permute-done.5
  38.1 0.0 collective-permute-done.6
  38.1 0.5 collective-permute-done.7
  38.6 1.0 multiply_bitcast_fusion.3
  39.6 0.1 pad_maximum_fusion.own_ref
  39.7 0.2 collective-permute-start.13
  39.9 4.4 %collective-permute-start.14 = (bf16[4,640,128]{2,1,0:T(8,128)(2,1)S(1)}, bf16[4,640,128]{2,1,0:T(8,128)(2,1)S(1)}, u32[]{:S(2)}, u32[]{:S(2)}) collective-permute-start(bf16[4,640,128]{2,1,0:T(8,128)(2,1)S(1)} %pad_maximum_fusion.own_ref), channel_id=1, source_target_pairs={{0,0},{1,1},{2,2},{3,3},{4,4},{5,5},{6,6},{7,7},{8,16},{9,17},{10,... | collective-permute-start | bytes 1966088 | tf_op jit(solution)/shard_map/ppermute | solution.py:515
  44.3 0.0 collective-permute-done.11.near_chip_ref
  44.3 0.0 collective-permute-done.12.off_chip_ref
  44.3 12.7 %cross.2 = (f32[2,10,32,128]{3,2,1,0:T(8,128)S(1)}, f32[2,10,32,128]{3,2,1,0:T(8,128)S(1)}, f32[2,10,16,128]{3,2,1,0:T(8,128)S(1)}, f32[2,10,16,128]{3,2,1,0:T(8,128)S(1)}) custom-call(f32[1,128]{1,0:T(1,128)S(1)} %get-tuple-element.56.reach_own, f32[1,128]{1,0:T(1,128)S(1)} %get-tuple-element.55.reach_prev, bf16[128,128]{1,0:T(8,128)(2,1)S(1)} %copy-done.2, ...), custom_call_target="tpu_custom_call" | custom-call | flops 10000000000 | bytes 2000000 | tf_op jit(solution)/shard_map/cross/pallas_call | solution.py:415
  57.0 3.0 %collective-permute-start.15 = (f32[2,10,32,128]{3,2,1,0:T(8,128)S(1)}, f32[2,10,32,128]{3,2,1,0:T(8,128)S(1)}, u32[]{:S(2)}, u32[]{:S(2)}) collective-permute-start(f32[2,10,32,128]{3,2,1,0:T(8,128)S(1)} %get-tuple-element.43), channel_id=1, source_target_pairs={{0,4},{1,5},{2,6},{3,7},{4,0},{5,1},{6,2},{7,3},{8,12},{9,13},{10,... | collective-permute-start | bytes 983048 | tf_op jit(solution)/shard_map/ppermute | solution.py:515
  59.9 1.9 %collective-permute-start.16 = (f32[2,10,16,128]{3,2,1,0:T(8,128)S(1)}, f32[2,10,16,128]{3,2,1,0:T(8,128)S(1)}, u32[]{:S(2)}, u32[]{:S(2)}) collective-permute-start(f32[2,10,16,128]{3,2,1,0:T(8,128)S(1)} %get-tuple-element.44), channel_id=1, source_target_pairs={{8,0},{9,1},{10,2},{11,3},{12,4},{13,5},{14,6},{15,7},{16,8},{17,9... | collective-permute-start | bytes 491528 | tf_op jit(solution)/shard_map/ppermute | solution.py:515
  61.9 1.9 %collective-permute-start.17 = (f32[2,10,16,128]{3,2,1,0:T(8,128)S(1)}, f32[2,10,16,128]{3,2,1,0:T(8,128)S(1)}, u32[]{:S(2)}, u32[]{:S(2)}) collective-permute-start(f32[2,10,16,128]{3,2,1,0:T(8,128)S(1)} %get-tuple-element.45), channel_id=1, source_target_pairs={{8,4},{9,5},{10,6},{11,7},{12,0},{13,1},{14,2},{15,3},{16,12},{17,... | collective-permute-start | bytes 491528 | tf_op jit(solution)/shard_map/ppermute | solution.py:515
  63.8 0.0 collective-permute-done.13.near_chip_ref
  63.8 0.0 collective-permute-done.14.off_chip_ref
  63.8 25.2 %cross.3 = (f32[2,20,32,128]{3,2,1,0:T(8,128)S(1)}, f32[2,20,32,128]{3,2,1,0:T(8,128)S(1)}, bf16[2,20,16,128]{3,2,1,0:T(8,128)(2,1)S(1)}, bf16[2,20,16,128]{3,2,1,0:T(8,128)(2,1)S(1)}) custom-call(f32[1,128]{1,0:T(1,128)S(1)} %get-tuple-element.56.reach_own, f32[1,128]{1,0:T(1,128)S(1)} %get-tuple-element.55.reach_prev, bf16[128,128]{1,0:T(8,128)(2,1)S(1)} %copy-done.2, ...), custom_call_target="tpu_custom_call" | custom-call | flops 20000000000 | bytes 4000000 | tf_op jit(solution)/shard_map/cross/pallas_call | solution.py:415
  89.0 0.0 collective-permute-done.16.rest_2_
  89.0 0.0 collective-permute-done.17.rest_3_
  89.1 0.0 collective-permute-done.15.rest_1_
  89.1 0.1 collective-permute-start.18
  89.2 0.1 pad_dynamic-slice_fusion.1
  89.3 0.1 reshape.19
  89.4 0.2 reshape.20
  89.6 0.8 dynamic_slice.15
  90.3 0.1 fusion.2
  90.4 1.9 %collective-permute-start.19 = (bf16[2,20,16,128]{3,2,1,0:T(8,128)(2,1)S(1)}, bf16[2,20,16,128]{3,2,1,0:T(8,128)(2,1)S(1)}, u32[]{:S(2)}, u32[]{:S(2)}) collective-permute-start(bf16[2,20,16,128]{3,2,1,0:T(8,128)(2,1)S(1)} %get-tuple-element.51), channel_id=1, source_target_pairs={{8,0},{9,1},{10,2},{11,3},{12,4},{13,5},{14,6},{15,7},{16,8},{17,9... | collective-permute-start | bytes 491528 | tf_op jit(solution)/shard_map/ppermute | solution.py:515
  92.4 1.9 %collective-permute-start.20 = (bf16[2,20,16,128]{3,2,1,0:T(8,128)(2,1)S(1)}, bf16[2,20,16,128]{3,2,1,0:T(8,128)(2,1)S(1)}, u32[]{:S(2)}, u32[]{:S(2)}) collective-permute-start(bf16[2,20,16,128]{3,2,1,0:T(8,128)(2,1)S(1)} %get-tuple-element.52), channel_id=1, source_target_pairs={{8,4},{9,5},{10,6},{11,7},{12,0},{13,1},{14,2},{15,3},{16,12},{17,... | collective-permute-start | bytes 491528 | tf_op jit(solution)/shard_map/ppermute | solution.py:515
  94.3 4.1 %collective-permute-done.19.rest_6_ = bf16[2,20,16,128]{3,2,1,0:T(8,128)(2,1)S(1)} collective-permute-done((bf16[2,20,16,128]{3,2,1,0:T(8,128)(2,1)S(1)}, bf16[2,20,16,128]{3,2,1,0:T(8,128)(2,1)S(1)}, u32[]{:S(2)}, u32[]{:S(2)}) %collective-permute-start.19) | collective-permute-done | bytes 163872 | tf_op jit(solution)/shard_map/ppermute | solution.py:515
  98.4 3.7 %collective-permute-done.20.rest_7_ = bf16[2,20,16,128]{3,2,1,0:T(8,128)(2,1)S(1)} collective-permute-done((bf16[2,20,16,128]{3,2,1,0:T(8,128)(2,1)S(1)}, bf16[2,20,16,128]{3,2,1,0:T(8,128)(2,1)S(1)}, u32[]{:S(2)}, u32[]{:S(2)}) %collective-permute-start.20) | collective-permute-done | bytes 163872 | tf_op jit(solution)/shard_map/ppermute | solution.py:515
  102.1 0.0 collective-permute-done.18.rest_5_
  102.1 1.4 %finish.1 = f32[2,960,256]{2,1,0:T(8,128)} custom-call(f32[1,256]{1,0:T(1,128)S(1)} %bitcast.22, f32[2,10,32,128]{3,2,1,0:T(8,128)S(1)} %get-tuple-element.38.rest_0_, f32[2,10,32,128]{3,2,1,0:T(8,128)S(1)} %collective-permute-done.15.rest_1_, f32[2,10,16,128]{3,2,1,0:T(8,128)S(1)} %collective-permute-done.16.rest_2_, ...), custom_call_target="tpu_custom_call" | custom-call | tf_op jit(solution)/shard_map/finish/pallas_call | solution.py:470
  (17 shorter events, 0.1 us)
Async XLA Ops:
  0.0 6.1 %collective-permute-start = (bf16[64,7680]{1,0:T(8,128)(2,1)}, bf16[64,7680]{1,0:T(8,128)(2,1)S(1)}, u32[]{:S(2)}, u32[]{:S(2)}) collective-permute-start(bf16[64,7680]{1,0:T(8,128)(2,1)} %own.1), channel_id=1, source_target_pairs={{0,4},{1,5},{2,6},{3,7},{4,0},{5,1},{6,2},{7,3},{8,12},{9,13},{10,... | collective-permute-start | bytes 2949128 | tf_op jit(solution)/shard_map/ppermute | solution.py:515
  1.5 3.4 %collective-permute-start.1 = (bf16[64,256]{1,0:T(8,128)(2,1)S(1)}, bf16[64,256]{1,0:T(8,128)(2,1)S(1)}, u32[]{:S(2)}, u32[]{:S(2)}) collective-permute-start(bf16[64,256]{1,0:T(8,128)(2,1)S(1)} %get-tuple-element.54), channel_id=1, source_target_pairs={{0,1},{1,0},{2,3},{3,2},{4,5},{5,4},{6,7},{7,6},{8,9},{9,8},{10,11... | collective-permute-start | bytes 98312 | tf_op jit(solution)/shard_map/ppermute | solution.py:515
  2.7 3.3 %collective-permute-start.2 = (bf16[64,256]{1,0:T(8,128)(2,1)S(1)}, bf16[64,256]{1,0:T(8,128)(2,1)S(1)}, u32[]{:S(2)}, u32[]{:S(2)}) collective-permute-start(bf16[64,256]{1,0:T(8,128)(2,1)S(1)} %get-tuple-element.54), channel_id=1, source_target_pairs={{0,5},{1,4},{2,7},{3,6},{4,1},{5,0},{6,3},{7,2},{8,13},{9,12},{10,... | collective-permute-start | bytes 98312 | tf_op jit(solution)/shard_map/ppermute | solution.py:515
  3.2 2.9 %collective-permute-start.3 = (bf16[64,256]{1,0:T(8,128)(2,1)S(1)}, bf16[64,256]{1,0:T(8,128)(2,1)S(1)}, u32[]{:S(2)}, u32[]{:S(2)}) collective-permute-start(bf16[64,256]{1,0:T(8,128)(2,1)S(1)} %get-tuple-element.53), channel_id=1, source_target_pairs={{0,0},{1,2},{2,1},{3,3},{4,4},{5,6},{6,5},{7,7},{8,8},{9,10},{10,9... | collective-permute-start | bytes 98312 | tf_op jit(solution)/shard_map/ppermute | solution.py:515
  3.8 2.3 %collective-permute-start.4 = (bf16[64,256]{1,0:T(8,128)(2,1)S(1)}, bf16[64,256]{1,0:T(8,128)(2,1)S(1)}, u32[]{:S(2)}, u32[]{:S(2)}) collective-permute-start(bf16[64,256]{1,0:T(8,128)(2,1)S(1)} %get-tuple-element.53), channel_id=1, source_target_pairs={{0,4},{1,6},{2,5},{3,7},{4,0},{5,2},{6,1},{7,3},{8,12},{9,14},{10,... | collective-permute-start | bytes 98312 | tf_op jit(solution)/shard_map/ppermute | solution.py:515
  4.9 23.3 %copy-start.3 = (s32[512]{0:T(512)S(1)}, s32[512]{0:T(512)}, u32[]{:S(2)}) copy-start(s32[512]{0:T(512)} %param.15) | copy-start | bytes 6148
  4.9 1.2 %copy-start.5 = (bf16[64,256]{1,0:T(8,128)(2,1)}, bf16[64,256]{1,0:T(8,128)(2,1)S(1)}, u32[]{:S(2)}) copy-start(bf16[64,256]{1,0:T(8,128)(2,1)S(1)} %collective-permute-done.1.near_own) | copy-start | bytes 98308
  6.1 0.6 copy-start.6
  6.1 0.6 copy-start.7
  6.1 0.6 copy-start.8
  6.7 0.9 copy-start.4
  21.1 8.7 %collective-permute-start.10 = (bf16[320,128]{1,0:T(8,128)(2,1)}, bf16[320,128]{1,0:T(8,128)(2,1)S(1)}, u32[]{:S(2)}, u32[]{:S(2)}) collective-permute-start(bf16[320,128]{1,0:T(8,128)(2,1)} %get-tuple-element.36), channel_id=1, source_target_pairs={{0,3},{1,2},{2,1},{3,0},{4,7},{5,6},{6,5},{7,4},{8,11},{9,10},{10,... | collective-permute-start | bytes 245768 | tf_op jit(solution)/shard_map/ppermute | solution.py:515
  22.6 9.8 %collective-permute-start.8 = (bf16[320,128]{1,0:T(8,128)(2,1)}, bf16[320,128]{1,0:T(8,128)(2,1)S(1)}, u32[]{:S(2)}, u32[]{:S(2)}) collective-permute-start(bf16[320,128]{1,0:T(8,128)(2,1)} %get-tuple-element.34), channel_id=1, source_target_pairs={{0,1},{1,0},{2,3},{3,2},{4,5},{5,4},{6,7},{7,6},{8,9},{9,8},{10,11... | collective-permute-start | bytes 245768 | tf_op jit(solution)/shard_map/ppermute | solution.py:515
  28.2 4.2 %collective-permute-start.9 = (bf16[320,128]{1,0:T(8,128)(2,1)}, bf16[320,128]{1,0:T(8,128)(2,1)S(1)}, u32[]{:S(2)}, u32[]{:S(2)}) collective-permute-start(bf16[320,128]{1,0:T(8,128)(2,1)} %get-tuple-element.35), channel_id=1, source_target_pairs={{0,2},{1,3},{2,0},{3,1},{4,6},{5,7},{6,4},{7,5},{8,10},{9,11},{10,... | collective-permute-start | bytes 245768 | tf_op jit(solution)/shard_map/ppermute | solution.py:515
  28.3 9.8 %collective-permute-start.5 = (bf16[640,128]{1,0:T(8,128)(2,1)}, bf16[640,128]{1,0:T(8,128)(2,1)S(1)}, u32[]{:S(2)}, u32[]{:S(2)}) collective-permute-start(bf16[640,128]{1,0:T(8,128)(2,1)} %get-tuple-element.30), channel_id=1, source_target_pairs={{0,1},{1,0},{2,3},{3,2},{4,5},{5,4},{6,7},{7,6},{8,9},{9,8},{10,11... | collective-permute-start | bytes 491528 | tf_op jit(solution)/shard_map/ppermute | solution.py:515
  29.8 8.4 %collective-permute-start.6 = (bf16[640,128]{1,0:T(8,128)(2,1)}, bf16[640,128]{1,0:T(8,128)(2,1)S(1)}, u32[]{:S(2)}, u32[]{:S(2)}) collective-permute-start(bf16[640,128]{1,0:T(8,128)(2,1)} %get-tuple-element.31), channel_id=1, source_target_pairs={{0,2},{1,3},{2,0},{3,1},{4,6},{5,7},{6,4},{7,5},{8,10},{9,11},{10,... | collective-permute-start | bytes 491528 | tf_op jit(solution)/shard_map/ppermute | solution.py:515
  29.8 8.8 %collective-permute-start.7 = (bf16[640,128]{1,0:T(8,128)(2,1)}, bf16[640,128]{1,0:T(8,128)(2,1)S(1)}, u32[]{:S(2)}, u32[]{:S(2)}) collective-permute-start(bf16[640,128]{1,0:T(8,128)(2,1)} %get-tuple-element.32), channel_id=1, source_target_pairs={{0,3},{1,2},{2,1},{3,0},{4,7},{5,6},{6,5},{7,4},{8,11},{9,10},{10,... | collective-permute-start | bytes 491528 | tf_op jit(solution)/shard_map/ppermute | solution.py:515
  32.3 12.0 %copy-start = (bf16[16,16,256]{2,1,0:T(8,128)(2,1)S(1)}, bf16[16,16,256]{2,1,0:T(8,128)(2,1)}, u32[]{:S(2)}) copy-start(bf16[16,16,256]{2,1,0:T(8,128)(2,1)} %constant.72.clone.pick_ref) | copy-start | bytes 393220
  32.3 12.0 %copy-start.1 = (bf16[16,16,128]{2,1,0:T(8,128)(2,1)S(1)}, bf16[16,16,128]{2,1,0:T(8,128)(2,1)}, u32[]{:S(2)}) copy-start(bf16[16,16,128]{2,1,0:T(8,128)(2,1)} %constant.73.clone.cut_ref) | copy-start | bytes 196612
  32.3 12.0 %copy-start.2 = (bf16[128,128]{1,0:T(8,128)(2,1)S(1)}, bf16[128,128]{1,0:T(8,128)(2,1)}, u32[]{:S(2)}) copy-start(bf16[128,128]{1,0:T(8,128)(2,1)} %constant.71.clone.turn_ref) | copy-start | bytes 98308
  33.4 10.9 %collective-permute-start.11 = (bf16[4,320,128]{2,1,0:T(8,128)(2,1)S(1)}, bf16[4,320,128]{2,1,0:T(8,128)(2,1)S(1)}, u32[]{:S(2)}, u32[]{:S(2)}) collective-permute-start(bf16[4,320,128]{2,1,0:T(8,128)(2,1)S(1)} %pad_maximum_fusion.1.own_ref), channel_id=1, source_target_pairs={{0,8},{1,9},{2,10},{3,11},{4,12},{5,13},{6,14},{7,15},{8,0},{9,1},... | collective-permute-start | bytes 983048 | tf_op jit(solution)/shard_map/ppermute | solution.py:515
  33.6 10.6 %collective-permute-start.12 = (bf16[4,320,128]{2,1,0:T(8,128)(2,1)S(1)}, bf16[4,320,128]{2,1,0:T(8,128)(2,1)S(1)}, u32[]{:S(2)}, u32[]{:S(2)}) collective-permute-start(bf16[4,320,128]{2,1,0:T(8,128)(2,1)S(1)} %pad_maximum_fusion.1.own_ref), channel_id=1, source_target_pairs={{0,0},{1,1},{2,2},{3,3},{4,4},{5,5},{6,6},{7,7},{8,16},{9,17},{10,... | collective-permute-start | bytes 983048 | tf_op jit(solution)/shard_map/ppermute | solution.py:515
  39.7 24.1 %collective-permute-start.13 = (bf16[4,640,128]{2,1,0:T(8,128)(2,1)S(1)}, bf16[4,640,128]{2,1,0:T(8,128)(2,1)S(1)}, u32[]{:S(2)}, u32[]{:S(2)}) collective-permute-start(bf16[4,640,128]{2,1,0:T(8,128)(2,1)S(1)} %pad_maximum_fusion.own_ref), channel_id=1, source_target_pairs={{0,8},{1,9},{2,10},{3,11},{4,12},{5,13},{6,14},{7,15},{8,0},{9,1},... | collective-permute-start | bytes 1966088 | tf_op jit(solution)/shard_map/ppermute | solution.py:515
  39.9 23.9 %collective-permute-start.14 = (bf16[4,640,128]{2,1,0:T(8,128)(2,1)S(1)}, bf16[4,640,128]{2,1,0:T(8,128)(2,1)S(1)}, u32[]{:S(2)}, u32[]{:S(2)}) collective-permute-start(bf16[4,640,128]{2,1,0:T(8,128)(2,1)S(1)} %pad_maximum_fusion.own_ref), channel_id=1, source_target_pairs={{0,0},{1,1},{2,2},{3,3},{4,4},{5,5},{6,6},{7,7},{8,16},{9,17},{10,... | collective-permute-start | bytes 1966088 | tf_op jit(solution)/shard_map/ppermute | solution.py:515
  57.0 32.1 %collective-permute-start.15 = (f32[2,10,32,128]{3,2,1,0:T(8,128)S(1)}, f32[2,10,32,128]{3,2,1,0:T(8,128)S(1)}, u32[]{:S(2)}, u32[]{:S(2)}) collective-permute-start(f32[2,10,32,128]{3,2,1,0:T(8,128)S(1)} %get-tuple-element.43), channel_id=1, source_target_pairs={{0,4},{1,5},{2,6},{3,7},{4,0},{5,1},{6,2},{7,3},{8,12},{9,13},{10,... | collective-permute-start | bytes 983048 | tf_op jit(solution)/shard_map/ppermute | solution.py:515
  59.9 29.1 %collective-permute-start.16 = (f32[2,10,16,128]{3,2,1,0:T(8,128)S(1)}, f32[2,10,16,128]{3,2,1,0:T(8,128)S(1)}, u32[]{:S(2)}, u32[]{:S(2)}) collective-permute-start(f32[2,10,16,128]{3,2,1,0:T(8,128)S(1)} %get-tuple-element.44), channel_id=1, source_target_pairs={{8,0},{9,1},{10,2},{11,3},{12,4},{13,5},{14,6},{15,7},{16,8},{17,9... | collective-permute-start | bytes 491528 | tf_op jit(solution)/shard_map/ppermute | solution.py:515
  61.9 27.2 %collective-permute-start.17 = (f32[2,10,16,128]{3,2,1,0:T(8,128)S(1)}, f32[2,10,16,128]{3,2,1,0:T(8,128)S(1)}, u32[]{:S(2)}, u32[]{:S(2)}) collective-permute-start(f32[2,10,16,128]{3,2,1,0:T(8,128)S(1)} %get-tuple-element.45), channel_id=1, source_target_pairs={{8,4},{9,5},{10,6},{11,7},{12,0},{13,1},{14,2},{15,3},{16,12},{17,... | collective-permute-start | bytes 491528 | tf_op jit(solution)/shard_map/ppermute | solution.py:515
  89.1 13.1 %collective-permute-start.18 = (f32[2,20,32,128]{3,2,1,0:T(8,128)S(1)}, f32[2,20,32,128]{3,2,1,0:T(8,128)S(1)}, u32[]{:S(2)}, u32[]{:S(2)}) collective-permute-start(f32[2,20,32,128]{3,2,1,0:T(8,128)S(1)} %get-tuple-element.50), channel_id=1, source_target_pairs={{0,4},{1,5},{2,6},{3,7},{4,0},{5,1},{6,2},{7,3},{8,12},{9,13},{10,... | collective-permute-start | bytes 1966088 | tf_op jit(solution)/shard_map/ppermute | solution.py:515
  90.4 8.0 %collective-permute-start.19 = (bf16[2,20,16,128]{3,2,1,0:T(8,128)(2,1)S(1)}, bf16[2,20,16,128]{3,2,1,0:T(8,128)(2,1)S(1)}, u32[]{:S(2)}, u32[]{:S(2)}) collective-permute-start(bf16[2,20,16,128]{3,2,1,0:T(8,128)(2,1)S(1)} %get-tuple-element.51), channel_id=1, source_target_pairs={{8,0},{9,1},{10,2},{11,3},{12,4},{13,5},{14,6},{15,7},{16,8},{17,9... | collective-permute-start | bytes 491528 | tf_op jit(solution)/shard_map/ppermute | solution.py:515
  92.4 9.8 %collective-permute-start.20 = (bf16[2,20,16,128]{3,2,1,0:T(8,128)(2,1)S(1)}, bf16[2,20,16,128]{3,2,1,0:T(8,128)(2,1)S(1)}, u32[]{:S(2)}, u32[]{:S(2)}) collective-permute-start(bf16[2,20,16,128]{3,2,1,0:T(8,128)(2,1)S(1)} %get-tuple-element.52), channel_id=1, source_target_pairs={{8,4},{9,5},{10,6},{11,7},{12,0},{13,1},{14,2},{15,3},{16,12},{17,... | collective-permute-start | bytes 491528 | tf_op jit(solution)/shard_map/ppermute | solution.py:515

commit v6 on v5

--- a/solution.py
+++ b/solution.py
@@ -395,7 +395,7 @@
     depth = n_seg * rb
     steps = rows // rb
     slabs = both // 8
-    per = 2 if steps % 2 == 0 else 1
+    per = max(n for n in (1, 2, 4) if steps % n == 0)
     lane = np.arange(depth)
     part = lane % rb // nb
     turn = np.zeros((depth, depth))
@@ -561,7 +561,7 @@
     for k, (own, near_chip, off_chip) in enumerate(blocks):
         far_type = jnp.bfloat16 if k == len(blocks) - 1 else jnp.float32
         if k:
-            own, results[-4] = lax.optimization_barrier((own, results[-4]))
+            own, results[-4], count = lax.optimization_barrier((own, results[-4], count))
         mine, theirs, far_mine, far_theirs = cross(
             own, near_chip, off_chip, reach_own, reach_prev, far_type
         )

time: 105 us -> 102 us (0.971)
  starting transfers between devices: 33.2 us -> 30.7 us
  Pallas kernels: 52.7 us -> 51.6 us
    ppermute x21, starting transfers between devices: 33.2 us -> 30.7 us  [moved(): return lax.ppermute(x, ('chan', 'freq'), pairs)]
    pallas_call x2, Pallas kernels: 37.9 us -> 36.7 us  [cross(): pl.pallas_call(functools.partial(cross_kernel, per), grid=(steps // per,)...]
  transfers between devices with their start and end apart: 21 -> 21, of which waited for: 5 -> 6; matrix products, arithmetic and copies ran while one was open for 5% -> 6% of each run, Pallas kernels for 37% -> 36%
where the time goes in v6:
time: 102 us; the launch traced here: 101 us
  Pallas kernels  51.6 us (51%)
  starting transfers between devices  30.7 us (30%)
  waiting for transfers between devices  11.7 us (11%)
  other arithmetic  3.72 us (4%)
  local copies, waits for them, and re-layouts  3.48 us (3%)
    pallas_call x2, Pallas kernels, cross(): pl.pallas_call(functools.partial(cross_kernel, per), grid=(steps // per,)...  36.7 us
    ppermute x21, starting transfers between devices, moved(): return lax.ppermute(x, ('chan', 'freq'), pairs)  30.7 us
    pallas_call x1, Pallas kernels, spectra(): pl.pallas_call(functools.partial(spectra_kernel, count_a, n_freq, chunks)...  13.4 us
    ppermute x21, waiting for transfers between devices, moved(): return lax.ppermute(x, ('chan', 'freq'), pairs)  11.7 us
    another operation x4, other arithmetic, on_device(): own = jnp.stack([x * usable for x in pieces])  2.06 us
  transfers between devices with their start and end apart: 21, of which 6 were waited for; matrix products, arithmetic and copies ran while one was open for 6% of the time, Pallas kernels for 36%

profile of v6, /device:TPU:9, one launch (start us, length us, event | category | flops | bytes accessed | tf_op | source)
XLA Modules:
  0.0 101.4 jit_solution(1281150736361669146)
XLA Ops:
  0.0 0.7 collective-permute-start
  0.7 0.8 broadcast_select_fusion
  1.5 0.1 collective-permute-start.4
  1.5 0.7 collective-permute-start.3
  2.2 5.4 %collective-permute-start.2 = (bf16[64,256]{1,0:T(8,128)(2,1)S(1)}, bf16[64,256]{1,0:T(8,128)(2,1)S(1)}, u32[]{:S(2)}, u32[]{:S(2)}) collective-permute-start(bf16[64,256]{1,0:T(8,128)(2,1)S(1)} %get-tuple-element.56), channel_id=1, source_target_pairs={{0,5},{1,4},{2,7},{3,6},{4,1},{5,0},{6,3},{7,2},{8,13},{9,12},{10,... | collective-permute-start | bytes 98312 | tf_op jit(solution)/shard_map/ppermute | solution.py:515
  7.6 0.0 collective-permute-start.1
  7.6 0.8 pad_dynamic-slice_fusion
  8.4 0.1 reshape.10
  8.5 0.2 reshape.11
  8.7 0.8 dynamic_slice.18
  9.5 0.7 pad_convert_fusion
  10.2 0.1 fusion.2
  10.3 0.1 dynamic-slice_bitcast_fusion
  10.4 0.0 collective-permute-done.4.off_other
  10.4 0.0 collective-permute-done.3.off_own
  10.4 0.0 collective-permute-done.2.near_other
  10.4 0.4 collective-permute-done.1.near_own
  10.8 0.0 collective-permute-done.other
  10.9 0.1 copy-done.5
  11.0 0.0 copy-done.7
  11.0 0.4 copy-done.8
  11.5 0.9 copy-done.4
  12.4 13.4 %spectra.1 = (bf16[320,128]{1,0:T(8,128)(2,1)}, bf16[320,128]{1,0:T(8,128)(2,1)}, bf16[320,128]{1,0:T(8,128)(2,1)}, bf16[320,128]{1,0:T(8,128)(2,1)}, bf16[640,1...) custom-call(bf16[64,7680]{1,0:T(8,128)(2,1)} %own.1, ...), custom_call_target="tpu_custom_call" | custom-call | flops 6000000000 | bytes 4000000 | tf_op jit(solution)/shard_map/spectra/pallas_call | solution.py:196
  25.8 1.0 %collective-permute-start.8 = (bf16[320,128]{1,0:T(8,128)(2,1)}, bf16[320,128]{1,0:T(8,128)(2,1)S(1)}, u32[]{:S(2)}, u32[]{:S(2)}) collective-permute-start(bf16[320,128]{1,0:T(8,128)(2,1)} %get-tuple-element.35), channel_id=1, source_target_pairs={{0,1},{1,0},{2,3},{3,2},{4,5},{5,4},{6,7},{7,6},{8,9},{9,8},{10,11... | collective-permute-start | bytes 245768 | tf_op jit(solution)/shard_map/ppermute | solution.py:515
  26.8 0.5 collective-permute-start.9
  27.3 1.2 %collective-permute-start.10 = (bf16[320,128]{1,0:T(8,128)(2,1)}, bf16[320,128]{1,0:T(8,128)(2,1)S(1)}, u32[]{:S(2)}, u32[]{:S(2)}) collective-permute-start(bf16[320,128]{1,0:T(8,128)(2,1)} %get-tuple-element.37), channel_id=1, source_target_pairs={{0,3},{1,2},{2,1},{3,0},{4,7},{5,6},{6,5},{7,4},{8,11},{9,10},{10,... | collective-permute-start | bytes 245768 | tf_op jit(solution)/shard_map/ppermute | solution.py:515
  28.5 0.1 fusion.3
  28.5 1.0 %collective-permute-start.5 = (bf16[640,128]{1,0:T(8,128)(2,1)}, bf16[640,128]{1,0:T(8,128)(2,1)S(1)}, u32[]{:S(2)}, u32[]{:S(2)}) collective-permute-start(bf16[640,128]{1,0:T(8,128)(2,1)} %get-tuple-element.31), channel_id=1, source_target_pairs={{0,1},{1,0},{2,3},{3,2},{4,5},{5,4},{6,7},{7,6},{8,9},{9,8},{10,11... | collective-permute-start | bytes 491528 | tf_op jit(solution)/shard_map/ppermute | solution.py:515
  29.6 0.5 collective-permute-start.6
  30.0 0.0 collective-permute-done.8
  30.0 1.2 %collective-permute-start.7 = (bf16[640,128]{1,0:T(8,128)(2,1)}, bf16[640,128]{1,0:T(8,128)(2,1)S(1)}, u32[]{:S(2)}, u32[]{:S(2)}) collective-permute-start(bf16[640,128]{1,0:T(8,128)(2,1)} %get-tuple-element.33), channel_id=1, source_target_pairs={{0,3},{1,2},{2,1},{3,0},{4,7},{5,6},{6,5},{7,4},{8,11},{9,10},{10,... | collective-permute-start | bytes 491528 | tf_op jit(solution)/shard_map/ppermute | solution.py:515
  31.2 0.0 collective-permute-done.9
  31.2 0.8 collective-permute-done.10
  31.9 1.0 multiply_bitcast_fusion.7
  33.0 3.2 %collective-permute-start.12 = (bf16[4,320,128]{2,1,0:T(8,128)(2,1)S(1)}, bf16[4,320,128]{2,1,0:T(8,128)(2,1)S(1)}, u32[]{:S(2)}, u32[]{:S(2)}) collective-permute-start(bf16[4,320,128]{2,1,0:T(8,128)(2,1)S(1)} %pad_maximum_fusion.1.own_ref), channel_id=1, source_target_pairs={{0,0},{1,1},{2,2},{3,3},{4,4},{5,5},{6,6},{7,7},{8,16},{9,17},{10,... | collective-permute-start | bytes 983048 | tf_op jit(solution)/shard_map/ppermute | solution.py:515
  36.2 0.1 collective-permute-start.11
  36.3 0.0 collective-permute-done.5
  36.3 0.1 collective-permute-done.6
  36.4 2.5 %collective-permute-done.7 = bf16[640,128]{1,0:T(8,128)(2,1)S(1)} collective-permute-done((bf16[640,128]{1,0:T(8,128)(2,1)}, bf16[640,128]{1,0:T(8,128)(2,1)S(1)}, u32[]{:S(2)}, u32[]{:S(2)}) %collective-permute-start.7) | collective-permute-done | bytes 163872 | tf_op jit(solution)/shard_map/ppermute | solution.py:515
  38.9 1.0 multiply_bitcast_fusion.3
  39.9 0.1 pad_maximum_fusion.own_ref
  40.0 3.2 %collective-permute-start.14 = (bf16[4,640,128]{2,1,0:T(8,128)(2,1)S(1)}, bf16[4,640,128]{2,1,0:T(8,128)(2,1)S(1)}, u32[]{:S(2)}, u32[]{:S(2)}) collective-permute-start(bf16[4,640,128]{2,1,0:T(8,128)(2,1)S(1)} %pad_maximum_fusion.own_ref), channel_id=1, source_target_pairs={{0,0},{1,1},{2,2},{3,3},{4,4},{5,5},{6,6},{7,7},{8,16},{9,17},{10,... | collective-permute-start | bytes 1966088 | tf_op jit(solution)/shard_map/ppermute | solution.py:515
  43.2 0.1 collective-permute-start.13
  43.3 0.0 collective-permute-done.12.off_chip_ref
  43.3 0.0 collective-permute-done.11.near_chip_ref
  43.3 0.0 copy-done
  43.3 0.0 copy-done.1
  43.3 12.7 %cross.2 = (f32[2,10,32,128]{3,2,1,0:T(8,128)S(1)}, f32[2,10,32,128]{3,2,1,0:T(8,128)S(1)}, f32[2,10,16,128]{3,2,1,0:T(8,128)S(1)}, f32[2,10,16,128]{3,2,1,0:T(8,128)S(1)}) custom-call(f32[1,128]{1,0:T(1,128)S(1)} %get-tuple-element.58.reach_own, f32[1,128]{1,0:T(1,128)S(1)} %get-tuple-element.57.reach_prev, bf16[128,128]{1,0:T(8,128)(2,1)S(1)} %copy-done.2, ...), custom_call_target="tpu_custom_call" | custom-call | flops 10000000000 | bytes 2000000 | tf_op jit(solution)/shard_map/cross/pallas_call | solution.py:415
  56.0 3.3 %collective-permute-start.16 = (f32[2,10,16,128]{3,2,1,0:T(8,128)S(1)}, f32[2,10,16,128]{3,2,1,0:T(8,128)S(1)}, u32[]{:S(2)}, u32[]{:S(2)}) collective-permute-start(f32[2,10,16,128]{3,2,1,0:T(8,128)S(1)} %get-tuple-element.46), channel_id=1, source_target_pairs={{8,0},{9,1},{10,2},{11,3},{12,4},{13,5},{14,6},{15,7},{16,8},{17,9... | collective-permute-start | bytes 491528 | tf_op jit(solution)/shard_map/ppermute | solution.py:515
  59.4 3.6 %collective-permute-start.17 = (f32[2,10,16,128]{3,2,1,0:T(8,128)S(1)}, f32[2,10,16,128]{3,2,1,0:T(8,128)S(1)}, u32[]{:S(2)}, u32[]{:S(2)}) collective-permute-start(f32[2,10,16,128]{3,2,1,0:T(8,128)S(1)} %get-tuple-element.47), channel_id=1, source_target_pairs={{8,4},{9,5},{10,6},{11,7},{12,0},{13,1},{14,2},{15,3},{16,12},{17,... | collective-permute-start | bytes 491528 | tf_op jit(solution)/shard_map/ppermute | solution.py:515
  63.0 1.1 %collective-permute-start.15 = (f32[2,10,32,128]{3,2,1,0:T(8,128)S(1)}, f32[2,10,32,128]{3,2,1,0:T(8,128)S(1)}, u32[]{:S(2)}, u32[]{:S(2)}) collective-permute-start(f32[2,10,32,128]{3,2,1,0:T(8,128)S(1)} %get-tuple-element.45), channel_id=1, source_target_pairs={{0,4},{1,5},{2,6},{3,7},{4,0},{5,1},{6,2},{7,3},{8,12},{9,13},{10,... | collective-permute-start | bytes 983048 | tf_op jit(solution)/shard_map/ppermute | solution.py:515
  64.1 0.0 collective-permute-done.14.off_chip_ref
  64.1 0.0 collective-permute-done.13.near_chip_ref
  64.1 24.1 %cross.3 = (f32[2,20,32,128]{3,2,1,0:T(8,128)S(1)}, f32[2,20,32,128]{3,2,1,0:T(8,128)S(1)}, bf16[2,20,16,128]{3,2,1,0:T(8,128)(2,1)S(1)}, bf16[2,20,16,128]{3,2,1,0:T(8,128)(2,1)S(1)}) custom-call(f32[1,128]{1,0:T(1,128)S(1)} %get-tuple-element.58.reach_own, f32[1,128]{1,0:T(1,128)S(1)} %get-tuple-element.57.reach_prev, bf16[128,128]{1,0:T(8,128)(2,1)S(1)} %copy-done.2, ...), custom_call_target="tpu_custom_call" | custom-call | flops 20000000000 | bytes 4000000 | tf_op jit(solution)/shard_map/cross/pallas_call | solution.py:415
  88.1 0.0 collective-permute-done.16.rest_2_
  88.1 0.0 collective-permute-done.17.rest_3_
  88.1 0.0 collective-permute-done.15.rest_1_
  88.2 0.1 collective-permute-start.18
  88.3 1.9 %collective-permute-start.19 = (bf16[2,20,16,128]{3,2,1,0:T(8,128)(2,1)S(1)}, bf16[2,20,16,128]{3,2,1,0:T(8,128)(2,1)S(1)}, u32[]{:S(2)}, u32[]{:S(2)}) collective-permute-start(bf16[2,20,16,128]{3,2,1,0:T(8,128)(2,1)S(1)} %get-tuple-element.53), channel_id=1, source_target_pairs={{8,0},{9,1},{10,2},{11,3},{12,4},{13,5},{14,6},{15,7},{16,8},{17,9... | collective-permute-start | bytes 491528 | tf_op jit(solution)/shard_map/ppermute | solution.py:515
  90.2 1.9 %collective-permute-start.20 = (bf16[2,20,16,128]{3,2,1,0:T(8,128)(2,1)S(1)}, bf16[2,20,16,128]{3,2,1,0:T(8,128)(2,1)S(1)}, u32[]{:S(2)}, u32[]{:S(2)}) collective-permute-start(bf16[2,20,16,128]{3,2,1,0:T(8,128)(2,1)S(1)} %get-tuple-element.54), channel_id=1, source_target_pairs={{8,4},{9,5},{10,6},{11,7},{12,0},{13,1},{14,2},{15,3},{16,12},{17,... | collective-permute-start | bytes 491528 | tf_op jit(solution)/shard_map/ppermute | solution.py:515
  92.1 4.0 %collective-permute-done.19.rest_6_ = bf16[2,20,16,128]{3,2,1,0:T(8,128)(2,1)S(1)} collective-permute-done((bf16[2,20,16,128]{3,2,1,0:T(8,128)(2,1)S(1)}, bf16[2,20,16,128]{3,2,1,0:T(8,128)(2,1)S(1)}, u32[]{:S(2)}, u32[]{:S(2)}) %collective-permute-start.19) | collective-permute-done | bytes 163872 | tf_op jit(solution)/shard_map/ppermute | solution.py:515
  96.2 3.8 %collective-permute-done.20.rest_7_ = bf16[2,20,16,128]{3,2,1,0:T(8,128)(2,1)S(1)} collective-permute-done((bf16[2,20,16,128]{3,2,1,0:T(8,128)(2,1)S(1)}, bf16[2,20,16,128]{3,2,1,0:T(8,128)(2,1)S(1)}, u32[]{:S(2)}, u32[]{:S(2)}) %collective-permute-start.20) | collective-permute-done | bytes 163872 | tf_op jit(solution)/shard_map/ppermute | solution.py:515
  99.9 0.0 collective-permute-done.18.rest_5_
  99.9 1.5 %finish.1 = f32[2,960,256]{2,1,0:T(8,128)} custom-call(f32[1,256]{1,0:T(1,128)S(1)} %bitcast.22, f32[2,10,32,128]{3,2,1,0:T(8,128)S(1)} %get-tuple-element.40.rest_0_, f32[2,10,32,128]{3,2,1,0:T(8,128)S(1)} %collective-permute-done.15.rest_1_, f32[2,10,16,128]{3,2,1,0:T(8,128)S(1)} %collective-permute-done.16.rest_2_, ...), custom_call_target="tpu_custom_call" | custom-call | tf_op jit(solution)/shard_map/finish/pallas_call | solution.py:470
  (17 shorter events, 0.1 us)
Async XLA Ops:
  0.0 10.9 %collective-permute-start = (bf16[64,7680]{1,0:T(8,128)(2,1)}, bf16[64,7680]{1,0:T(8,128)(2,1)S(1)}, u32[]{:S(2)}, u32[]{:S(2)}) collective-permute-start(bf16[64,7680]{1,0:T(8,128)(2,1)} %own.1), channel_id=1, source_target_pairs={{0,4},{1,5},{2,6},{3,7},{4,0},{5,1},{6,2},{7,3},{8,12},{9,13},{10,... | collective-permute-start | bytes 2949128 | tf_op jit(solution)/shard_map/ppermute | solution.py:515
  1.5 8.9 %collective-permute-start.4 = (bf16[64,256]{1,0:T(8,128)(2,1)S(1)}, bf16[64,256]{1,0:T(8,128)(2,1)S(1)}, u32[]{:S(2)}, u32[]{:S(2)}) collective-permute-start(bf16[64,256]{1,0:T(8,128)(2,1)S(1)} %get-tuple-element.55), channel_id=1, source_target_pairs={{0,4},{1,6},{2,5},{3,7},{4,0},{5,2},{6,1},{7,3},{8,12},{9,14},{10,... | collective-permute-start | bytes 98312 | tf_op jit(solution)/shard_map/ppermute | solution.py:515
  1.5 8.8 %collective-permute-start.3 = (bf16[64,256]{1,0:T(8,128)(2,1)S(1)}, bf16[64,256]{1,0:T(8,128)(2,1)S(1)}, u32[]{:S(2)}, u32[]{:S(2)}) collective-permute-start(bf16[64,256]{1,0:T(8,128)(2,1)S(1)} %get-tuple-element.55), channel_id=1, source_target_pairs={{0,0},{1,2},{2,1},{3,3},{4,4},{5,6},{6,5},{7,7},{8,8},{9,10},{10,9... | collective-permute-start | bytes 98312 | tf_op jit(solution)/shard_map/ppermute | solution.py:515
  2.2 8.2 %collective-permute-start.2 = (bf16[64,256]{1,0:T(8,128)(2,1)S(1)}, bf16[64,256]{1,0:T(8,128)(2,1)S(1)}, u32[]{:S(2)}, u32[]{:S(2)}) collective-permute-start(bf16[64,256]{1,0:T(8,128)(2,1)S(1)} %get-tuple-element.56), channel_id=1, source_target_pairs={{0,5},{1,4},{2,7},{3,6},{4,1},{5,0},{6,3},{7,2},{8,13},{9,12},{10,... | collective-permute-start | bytes 98312 | tf_op jit(solution)/shard_map/ppermute | solution.py:515
  7.6 3.2 %collective-permute-start.1 = (bf16[64,256]{1,0:T(8,128)(2,1)S(1)}, bf16[64,256]{1,0:T(8,128)(2,1)S(1)}, u32[]{:S(2)}, u32[]{:S(2)}) collective-permute-start(bf16[64,256]{1,0:T(8,128)(2,1)S(1)} %get-tuple-element.56), channel_id=1, source_target_pairs={{0,1},{1,0},{2,3},{3,2},{4,5},{5,4},{6,7},{7,6},{8,9},{9,8},{10,11... | collective-permute-start | bytes 98312 | tf_op jit(solution)/shard_map/ppermute | solution.py:515
  10.4 18.1 %copy-start.3 = (s32[512]{0:T(512)S(1)}, s32[512]{0:T(512)}, u32[]{:S(2)}) copy-start(s32[512]{0:T(512)} %param.15) | copy-start | bytes 6148
  10.4 0.6 copy-start.5
  10.4 0.6 copy-start.6
  10.4 0.6 copy-start.7
  10.8 0.6 copy-start.8
  11.5 0.9 copy-start.4
  25.8 4.2 %collective-permute-start.8 = (bf16[320,128]{1,0:T(8,128)(2,1)}, bf16[320,128]{1,0:T(8,128)(2,1)S(1)}, u32[]{:S(2)}, u32[]{:S(2)}) collective-permute-start(bf16[320,128]{1,0:T(8,128)(2,1)} %get-tuple-element.35), channel_id=1, source_target_pairs={{0,1},{1,0},{2,3},{3,2},{4,5},{5,4},{6,7},{7,6},{8,9},{9,8},{10,11... | collective-permute-start | bytes 245768 | tf_op jit(solution)/shard_map/ppermute | solution.py:515
  26.8 4.3 %collective-permute-start.9 = (bf16[320,128]{1,0:T(8,128)(2,1)}, bf16[320,128]{1,0:T(8,128)(2,1)S(1)}, u32[]{:S(2)}, u32[]{:S(2)}) collective-permute-start(bf16[320,128]{1,0:T(8,128)(2,1)} %get-tuple-element.36), channel_id=1, source_target_pairs={{0,2},{1,3},{2,0},{3,1},{4,6},{5,7},{6,4},{7,5},{8,10},{9,11},{10,... | collective-permute-start | bytes 245768 | tf_op jit(solution)/shard_map/ppermute | solution.py:515
  27.3 4.6 %collective-permute-start.10 = (bf16[320,128]{1,0:T(8,128)(2,1)}, bf16[320,128]{1,0:T(8,128)(2,1)S(1)}, u32[]{:S(2)}, u32[]{:S(2)}) collective-permute-start(bf16[320,128]{1,0:T(8,128)(2,1)} %get-tuple-element.37), channel_id=1, source_target_pairs={{0,3},{1,2},{2,1},{3,0},{4,7},{5,6},{6,5},{7,4},{8,11},{9,10},{10,... | collective-permute-start | bytes 245768 | tf_op jit(solution)/shard_map/ppermute | solution.py:515
  28.5 7.7 %collective-permute-start.5 = (bf16[640,128]{1,0:T(8,128)(2,1)}, bf16[640,128]{1,0:T(8,128)(2,1)S(1)}, u32[]{:S(2)}, u32[]{:S(2)}) collective-permute-start(bf16[640,128]{1,0:T(8,128)(2,1)} %get-tuple-element.31), channel_id=1, source_target_pairs={{0,1},{1,0},{2,3},{3,2},{4,5},{5,4},{6,7},{7,6},{8,9},{9,8},{10,11... | collective-permute-start | bytes 491528 | tf_op jit(solution)/shard_map/ppermute | solution.py:515
  29.6 6.8 %collective-permute-start.6 = (bf16[640,128]{1,0:T(8,128)(2,1)}, bf16[640,128]{1,0:T(8,128)(2,1)S(1)}, u32[]{:S(2)}, u32[]{:S(2)}) collective-permute-start(bf16[640,128]{1,0:T(8,128)(2,1)} %get-tuple-element.32), channel_id=1, source_target_pairs={{0,2},{1,3},{2,0},{3,1},{4,6},{5,7},{6,4},{7,5},{8,10},{9,11},{10,... | collective-permute-start | bytes 491528 | tf_op jit(solution)/shard_map/ppermute | solution.py:515
  30.0 8.9 %collective-permute-start.7 = (bf16[640,128]{1,0:T(8,128)(2,1)}, bf16[640,128]{1,0:T(8,128)(2,1)S(1)}, u32[]{:S(2)}, u32[]{:S(2)}) collective-permute-start(bf16[640,128]{1,0:T(8,128)(2,1)} %get-tuple-element.33), channel_id=1, source_target_pairs={{0,3},{1,2},{2,1},{3,0},{4,7},{5,6},{6,5},{7,4},{8,11},{9,10},{10,... | collective-permute-start | bytes 491528 | tf_op jit(solution)/shard_map/ppermute | solution.py:515
  31.9 11.4 %copy-start = (bf16[16,16,256]{2,1,0:T(8,128)(2,1)S(1)}, bf16[16,16,256]{2,1,0:T(8,128)(2,1)}, u32[]{:S(2)}) copy-start(bf16[16,16,256]{2,1,0:T(8,128)(2,1)} %constant.72.clone.pick_ref) | copy-start | bytes 393220
  31.9 11.4 %copy-start.1 = (bf16[16,16,128]{2,1,0:T(8,128)(2,1)S(1)}, bf16[16,16,128]{2,1,0:T(8,128)(2,1)}, u32[]{:S(2)}) copy-start(bf16[16,16,128]{2,1,0:T(8,128)(2,1)} %constant.73.clone.cut_ref) | copy-start | bytes 196612
  31.9 11.4 %copy-start.2 = (bf16[128,128]{1,0:T(8,128)(2,1)S(1)}, bf16[128,128]{1,0:T(8,128)(2,1)}, u32[]{:S(2)}) copy-start(bf16[128,128]{1,0:T(8,128)(2,1)} %constant.71.clone.turn_ref) | copy-start | bytes 98308
  33.0 10.3 %collective-permute-start.12 = (bf16[4,320,128]{2,1,0:T(8,128)(2,1)S(1)}, bf16[4,320,128]{2,1,0:T(8,128)(2,1)S(1)}, u32[]{:S(2)}, u32[]{:S(2)}) collective-permute-start(bf16[4,320,128]{2,1,0:T(8,128)(2,1)S(1)} %pad_maximum_fusion.1.own_ref), channel_id=1, source_target_pairs={{0,0},{1,1},{2,2},{3,3},{4,4},{5,5},{6,6},{7,7},{8,16},{9,17},{10,... | collective-permute-start | bytes 983048 | tf_op jit(solution)/shard_map/ppermute | solution.py:515
  36.2 7.1 %collective-permute-start.11 = (bf16[4,320,128]{2,1,0:T(8,128)(2,1)S(1)}, bf16[4,320,128]{2,1,0:T(8,128)(2,1)S(1)}, u32[]{:S(2)}, u32[]{:S(2)}) collective-permute-start(bf16[4,320,128]{2,1,0:T(8,128)(2,1)S(1)} %pad_maximum_fusion.1.own_ref), channel_id=1, source_target_pairs={{0,8},{1,9},{2,10},{3,11},{4,12},{5,13},{6,14},{7,15},{8,0},{9,1},... | collective-permute-start | bytes 983048 | tf_op jit(solution)/shard_map/ppermute | solution.py:515
  40.0 24.1 %collective-permute-start.14 = (bf16[4,640,128]{2,1,0:T(8,128)(2,1)S(1)}, bf16[4,640,128]{2,1,0:T(8,128)(2,1)S(1)}, u32[]{:S(2)}, u32[]{:S(2)}) collective-permute-start(bf16[4,640,128]{2,1,0:T(8,128)(2,1)S(1)} %pad_maximum_fusion.own_ref), channel_id=1, source_target_pairs={{0,0},{1,1},{2,2},{3,3},{4,4},{5,5},{6,6},{7,7},{8,16},{9,17},{10,... | collective-permute-start | bytes 1966088 | tf_op jit(solution)/shard_map/ppermute | solution.py:515
  43.2 20.9 %collective-permute-start.13 = (bf16[4,640,128]{2,1,0:T(8,128)(2,1)S(1)}, bf16[4,640,128]{2,1,0:T(8,128)(2,1)S(1)}, u32[]{:S(2)}, u32[]{:S(2)}) collective-permute-start(bf16[4,640,128]{2,1,0:T(8,128)(2,1)S(1)} %pad_maximum_fusion.own_ref), channel_id=1, source_target_pairs={{0,8},{1,9},{2,10},{3,11},{4,12},{5,13},{6,14},{7,15},{8,0},{9,1},... | collective-permute-start | bytes 1966088 | tf_op jit(solution)/shard_map/ppermute | solution.py:515
  56.0 32.1 %collective-permute-start.16 = (f32[2,10,16,128]{3,2,1,0:T(8,128)S(1)}, f32[2,10,16,128]{3,2,1,0:T(8,128)S(1)}, u32[]{:S(2)}, u32[]{:S(2)}) collective-permute-start(f32[2,10,16,128]{3,2,1,0:T(8,128)S(1)} %get-tuple-element.46), channel_id=1, source_target_pairs={{8,0},{9,1},{10,2},{11,3},{12,4},{13,5},{14,6},{15,7},{16,8},{17,9... | collective-permute-start | bytes 491528 | tf_op jit(solution)/shard_map/ppermute | solution.py:515
  59.4 28.8 %collective-permute-start.17 = (f32[2,10,16,128]{3,2,1,0:T(8,128)S(1)}, f32[2,10,16,128]{3,2,1,0:T(8,128)S(1)}, u32[]{:S(2)}, u32[]{:S(2)}) collective-permute-start(f32[2,10,16,128]{3,2,1,0:T(8,128)S(1)} %get-tuple-element.47), channel_id=1, source_target_pairs={{8,4},{9,5},{10,6},{11,7},{12,0},{13,1},{14,2},{15,3},{16,12},{17,... | collective-permute-start | bytes 491528 | tf_op jit(solution)/shard_map/ppermute | solution.py:515
  63.0 25.2 %collective-permute-start.15 = (f32[2,10,32,128]{3,2,1,0:T(8,128)S(1)}, f32[2,10,32,128]{3,2,1,0:T(8,128)S(1)}, u32[]{:S(2)}, u32[]{:S(2)}) collective-permute-start(f32[2,10,32,128]{3,2,1,0:T(8,128)S(1)} %get-tuple-element.45), channel_id=1, source_target_pairs={{0,4},{1,5},{2,6},{3,7},{4,0},{5,1},{6,2},{7,3},{8,12},{9,13},{10,... | collective-permute-start | bytes 983048 | tf_op jit(solution)/shard_map/ppermute | solution.py:515
  88.2 11.8 %collective-permute-start.18 = (f32[2,20,32,128]{3,2,1,0:T(8,128)S(1)}, f32[2,20,32,128]{3,2,1,0:T(8,128)S(1)}, u32[]{:S(2)}, u32[]{:S(2)}) collective-permute-start(f32[2,20,32,128]{3,2,1,0:T(8,128)S(1)} %get-tuple-element.52), channel_id=1, source_target_pairs={{0,4},{1,5},{2,6},{3,7},{4,0},{5,1},{6,2},{7,3},{8,12},{9,13},{10,... | collective-permute-start | bytes 1966088 | tf_op jit(solution)/shard_map/ppermute | solution.py:515
  88.3 7.9 %collective-permute-start.19 = (bf16[2,20,16,128]{3,2,1,0:T(8,128)(2,1)S(1)}, bf16[2,20,16,128]{3,2,1,0:T(8,128)(2,1)S(1)}, u32[]{:S(2)}, u32[]{:S(2)}) collective-permute-start(bf16[2,20,16,128]{3,2,1,0:T(8,128)(2,1)S(1)} %get-tuple-element.53), channel_id=1, source_target_pairs={{8,0},{9,1},{10,2},{11,3},{12,4},{13,5},{14,6},{15,7},{16,8},{17,9... | collective-permute-start | bytes 491528 | tf_op jit(solution)/shard_map/ppermute | solution.py:515
  90.2 9.7 %collective-permute-start.20 = (bf16[2,20,16,128]{3,2,1,0:T(8,128)(2,1)S(1)}, bf16[2,20,16,128]{3,2,1,0:T(8,128)(2,1)S(1)}, u32[]{:S(2)}, u32[]{:S(2)}) collective-permute-start(bf16[2,20,16,128]{3,2,1,0:T(8,128)(2,1)S(1)} %get-tuple-element.54), channel_id=1, source_target_pairs={{8,4},{9,5},{10,6},{11,7},{12,0},{13,1},{14,2},{15,3},{16,12},{17,... | collective-permute-start | bytes 491528 | tf_op jit(solution)/shard_map/ppermute | solution.py:515

commit v7 on v6

--- a/solution.py
+++ b/solution.py
@@ -395,7 +395,7 @@
     depth = n_seg * rb
     steps = rows // rb
     slabs = both // 8
-    per = max(n for n in (1, 2, 4) if steps % n == 0)
+    per = max(n for n in (1, 2, 4, 5) if steps % n == 0)
     lane = np.arange(depth)
     part = lane % rb // nb
     turn = np.zeros((depth, depth))

time: 102 us -> 104 us (1.020)
  Pallas kernels: 51.6 us -> 52.7 us
    pallas_call x2, Pallas kernels: 36.7 us -> 37.8 us  [cross(): pl.pallas_call(functools.partial(cross_kernel, per), grid=(steps // per,)...]
  transfers between devices with their start and end apart: 21 -> 21, of which waited for: 6 -> 6; matrix products, arithmetic and copies ran while one was open for 6% -> 5% of each run, Pallas kernels for 36% -> 37%
where the time goes in v7:
time: 104 us; the launch traced here: 103 us
  Pallas kernels  52.7 us (51%)
  starting transfers between devices  30.9 us (30%)
  waiting for transfers between devices  11.7 us (11%)
  other arithmetic  3.72 us (4%)
  local copies, waits for them, and re-layouts  3.48 us (3%)
    pallas_call x2, Pallas kernels, cross(): pl.pallas_call(functools.partial(cross_kernel, per), grid=(steps // per,)...  37.8 us
    ppermute x21, starting transfers between devices, moved(): return lax.ppermute(x, ('chan', 'freq'), pairs)  30.9 us
    pallas_call x1, Pallas kernels, spectra(): pl.pallas_call(functools.partial(spectra_kernel, count_a, n_freq, chunks)...  13.4 us
    ppermute x21, waiting for transfers between devices, moved(): return lax.ppermute(x, ('chan', 'freq'), pairs)  11.7 us
  transfers between devices with their start and end apart: 21, of which 6 were waited for; matrix products, arithmetic and copies ran while one was open for 5% of the time, Pallas kernels for 37%

profile of v7, /device:TPU:9, one launch (start us, length us, event | category | flops | bytes accessed | tf_op | source)
XLA Modules:
  0.0 102.7 jit_solution(8123327136333436925)
XLA Ops:
  0.0 0.7 collective-permute-start
  0.7 0.8 broadcast_select_fusion
  1.5 0.1 collective-permute-start.4
  1.5 0.7 collective-permute-start.3
  2.2 5.4 %collective-permute-start.2 = (bf16[64,256]{1,0:T(8,128)(2,1)S(1)}, bf16[64,256]{1,0:T(8,128)(2,1)S(1)}, u32[]{:S(2)}, u32[]{:S(2)}) collective-permute-start(bf16[64,256]{1,0:T(8,128)(2,1)S(1)} %get-tuple-element.56), channel_id=1, source_target_pairs={{0,5},{1,4},{2,7},{3,6},{4,1},{5,0},{6,3},{7,2},{8,13},{9,12},{10,... | collective-permute-start | bytes 98312 | tf_op jit(solution)/shard_map/ppermute | solution.py:515
  7.6 0.0 collective-permute-start.1
  7.6 0.8 pad_dynamic-slice_fusion
  8.4 0.1 reshape.10
  8.5 0.2 reshape.11
  8.7 0.8 dynamic_slice.18
  9.5 0.7 pad_convert_fusion
  10.2 0.1 fusion.2
  10.3 0.1 dynamic-slice_bitcast_fusion
  10.4 0.0 collective-permute-done.4.off_other
  10.4 0.0 collective-permute-done.3.off_own
  10.4 0.0 collective-permute-done.2.near_other
  10.4 0.4 collective-permute-done.1.near_own
  10.8 0.0 collective-permute-done.other
  10.9 0.1 copy-done.5
  11.0 0.0 copy-done.7
  11.0 0.4 copy-done.8
  11.5 0.9 copy-done.4
  12.4 13.4 %spectra.1 = (bf16[320,128]{1,0:T(8,128)(2,1)}, bf16[320,128]{1,0:T(8,128)(2,1)}, bf16[320,128]{1,0:T(8,128)(2,1)}, bf16[320,128]{1,0:T(8,128)(2,1)}, bf16[640,1...) custom-call(bf16[64,7680]{1,0:T(8,128)(2,1)} %own.1, ...), custom_call_target="tpu_custom_call" | custom-call | flops 6000000000 | bytes 4000000 | tf_op jit(solution)/shard_map/spectra/pallas_call | solution.py:196
  25.8 1.0 %collective-permute-start.8 = (bf16[320,128]{1,0:T(8,128)(2,1)}, bf16[320,128]{1,0:T(8,128)(2,1)S(1)}, u32[]{:S(2)}, u32[]{:S(2)}) collective-permute-start(bf16[320,128]{1,0:T(8,128)(2,1)} %get-tuple-element.35), channel_id=1, source_target_pairs={{0,1},{1,0},{2,3},{3,2},{4,5},{5,4},{6,7},{7,6},{8,9},{9,8},{10,11... | collective-permute-start | bytes 245768 | tf_op jit(solution)/shard_map/ppermute | solution.py:515
  26.8 0.5 collective-permute-start.9
  27.3 1.2 %collective-permute-start.10 = (bf16[320,128]{1,0:T(8,128)(2,1)}, bf16[320,128]{1,0:T(8,128)(2,1)S(1)}, u32[]{:S(2)}, u32[]{:S(2)}) collective-permute-start(bf16[320,128]{1,0:T(8,128)(2,1)} %get-tuple-element.37), channel_id=1, source_target_pairs={{0,3},{1,2},{2,1},{3,0},{4,7},{5,6},{6,5},{7,4},{8,11},{9,10},{10,... | collective-permute-start | bytes 245768 | tf_op jit(solution)/shard_map/ppermute | solution.py:515
  28.5 0.1 fusion.3
  28.5 1.0 %collective-permute-start.5 = (bf16[640,128]{1,0:T(8,128)(2,1)}, bf16[640,128]{1,0:T(8,128)(2,1)S(1)}, u32[]{:S(2)}, u32[]{:S(2)}) collective-permute-start(bf16[640,128]{1,0:T(8,128)(2,1)} %get-tuple-element.31), channel_id=1, source_target_pairs={{0,1},{1,0},{2,3},{3,2},{4,5},{5,4},{6,7},{7,6},{8,9},{9,8},{10,11... | collective-permute-start | bytes 491528 | tf_op jit(solution)/shard_map/ppermute | solution.py:515
  29.6 0.5 collective-permute-start.6
  30.0 0.0 collective-permute-done.8
  30.0 1.2 %collective-permute-start.7 = (bf16[640,128]{1,0:T(8,128)(2,1)}, bf16[640,128]{1,0:T(8,128)(2,1)S(1)}, u32[]{:S(2)}, u32[]{:S(2)}) collective-permute-start(bf16[640,128]{1,0:T(8,128)(2,1)} %get-tuple-element.33), channel_id=1, source_target_pairs={{0,3},{1,2},{2,1},{3,0},{4,7},{5,6},{6,5},{7,4},{8,11},{9,10},{10,... | collective-permute-start | bytes 491528 | tf_op jit(solution)/shard_map/ppermute | solution.py:515
  31.2 0.0 collective-permute-done.9
  31.2 0.8 collective-permute-done.10
  31.9 1.0 multiply_bitcast_fusion.7
  33.0 3.2 %collective-permute-start.12 = (bf16[4,320,128]{2,1,0:T(8,128)(2,1)S(1)}, bf16[4,320,128]{2,1,0:T(8,128)(2,1)S(1)}, u32[]{:S(2)}, u32[]{:S(2)}) collective-permute-start(bf16[4,320,128]{2,1,0:T(8,128)(2,1)S(1)} %pad_maximum_fusion.1.own_ref), channel_id=1, source_target_pairs={{0,0},{1,1},{2,2},{3,3},{4,4},{5,5},{6,6},{7,7},{8,16},{9,17},{10,... | collective-permute-start | bytes 983048 | tf_op jit(solution)/shard_map/ppermute | solution.py:515
  36.2 0.1 collective-permute-start.11
  36.3 0.0 collective-permute-done.5
  36.3 0.1 collective-permute-done.6
  36.4 2.5 %collective-permute-done.7 = bf16[640,128]{1,0:T(8,128)(2,1)S(1)} collective-permute-done((bf16[640,128]{1,0:T(8,128)(2,1)}, bf16[640,128]{1,0:T(8,128)(2,1)S(1)}, u32[]{:S(2)}, u32[]{:S(2)}) %collective-permute-start.7) | collective-permute-done | bytes 163872 | tf_op jit(solution)/shard_map/ppermute | solution.py:515
  38.9 1.0 multiply_bitcast_fusion.3
  39.9 0.1 pad_maximum_fusion.own_ref
  40.0 3.2 %collective-permute-start.14 = (bf16[4,640,128]{2,1,0:T(8,128)(2,1)S(1)}, bf16[4,640,128]{2,1,0:T(8,128)(2,1)S(1)}, u32[]{:S(2)}, u32[]{:S(2)}) collective-permute-start(bf16[4,640,128]{2,1,0:T(8,128)(2,1)S(1)} %pad_maximum_fusion.own_ref), channel_id=1, source_target_pairs={{0,0},{1,1},{2,2},{3,3},{4,4},{5,5},{6,6},{7,7},{8,16},{9,17},{10,... | collective-permute-start | bytes 1966088 | tf_op jit(solution)/shard_map/ppermute | solution.py:515
  43.2 0.1 collective-permute-start.13
  43.3 0.0 collective-permute-done.12.off_chip_ref
  43.3 0.0 collective-permute-done.11.near_chip_ref
  43.3 0.0 copy-done
  43.3 0.0 copy-done.1
  43.3 12.7 %cross.2 = (f32[2,10,32,128]{3,2,1,0:T(8,128)S(1)}, f32[2,10,32,128]{3,2,1,0:T(8,128)S(1)}, f32[2,10,16,128]{3,2,1,0:T(8,128)S(1)}, f32[2,10,16,128]{3,2,1,0:T(8,128)S(1)}) custom-call(f32[1,128]{1,0:T(1,128)S(1)} %get-tuple-element.58.reach_own, f32[1,128]{1,0:T(1,128)S(1)} %get-tuple-element.57.reach_prev, bf16[128,128]{1,0:T(8,128)(2,1)S(1)} %copy-done.2, ...), custom_call_target="tpu_custom_call" | custom-call | flops 10000000000 | bytes 2000000 | tf_op jit(solution)/shard_map/cross/pallas_call | solution.py:415
  56.0 3.3 %collective-permute-start.16 = (f32[2,10,16,128]{3,2,1,0:T(8,128)S(1)}, f32[2,10,16,128]{3,2,1,0:T(8,128)S(1)}, u32[]{:S(2)}, u32[]{:S(2)}) collective-permute-start(f32[2,10,16,128]{3,2,1,0:T(8,128)S(1)} %get-tuple-element.46), channel_id=1, source_target_pairs={{8,0},{9,1},{10,2},{11,3},{12,4},{13,5},{14,6},{15,7},{16,8},{17,9... | collective-permute-start | bytes 491528 | tf_op jit(solution)/shard_map/ppermute | solution.py:515
  59.4 3.8 %collective-permute-start.17 = (f32[2,10,16,128]{3,2,1,0:T(8,128)S(1)}, f32[2,10,16,128]{3,2,1,0:T(8,128)S(1)}, u32[]{:S(2)}, u32[]{:S(2)}) collective-permute-start(f32[2,10,16,128]{3,2,1,0:T(8,128)S(1)} %get-tuple-element.47), channel_id=1, source_target_pairs={{8,4},{9,5},{10,6},{11,7},{12,0},{13,1},{14,2},{15,3},{16,12},{17,... | collective-permute-start | bytes 491528 | tf_op jit(solution)/shard_map/ppermute | solution.py:515
  63.2 1.1 %collective-permute-start.15 = (f32[2,10,32,128]{3,2,1,0:T(8,128)S(1)}, f32[2,10,32,128]{3,2,1,0:T(8,128)S(1)}, u32[]{:S(2)}, u32[]{:S(2)}) collective-permute-start(f32[2,10,32,128]{3,2,1,0:T(8,128)S(1)} %get-tuple-element.45), channel_id=1, source_target_pairs={{0,4},{1,5},{2,6},{3,7},{4,0},{5,1},{6,2},{7,3},{8,12},{9,13},{10,... | collective-permute-start | bytes 983048 | tf_op jit(solution)/shard_map/ppermute | solution.py:515
  64.3 0.0 collective-permute-done.14.off_chip_ref
  64.3 0.0 collective-permute-done.13.near_chip_ref
  64.3 25.1 %cross.3 = (f32[2,20,32,128]{3,2,1,0:T(8,128)S(1)}, f32[2,20,32,128]{3,2,1,0:T(8,128)S(1)}, bf16[2,20,16,128]{3,2,1,0:T(8,128)(2,1)S(1)}, bf16[2,20,16,128]{3,2,1,0:T(8,128)(2,1)S(1)}) custom-call(f32[1,128]{1,0:T(1,128)S(1)} %get-tuple-element.58.reach_own, f32[1,128]{1,0:T(1,128)S(1)} %get-tuple-element.57.reach_prev, bf16[128,128]{1,0:T(8,128)(2,1)S(1)} %copy-done.2, ...), custom_call_target="tpu_custom_call" | custom-call | flops 20000000000 | bytes 4000000 | tf_op jit(solution)/shard_map/cross/pallas_call | solution.py:415
  89.5 0.0 collective-permute-done.16.rest_2_
  89.5 0.0 collective-permute-done.17.rest_3_
  89.5 0.0 collective-permute-done.15.rest_1_
  89.5 0.1 collective-permute-start.18
  89.6 1.9 %collective-permute-start.19 = (bf16[2,20,16,128]{3,2,1,0:T(8,128)(2,1)S(1)}, bf16[2,20,16,128]{3,2,1,0:T(8,128)(2,1)S(1)}, u32[]{:S(2)}, u32[]{:S(2)}) collective-permute-start(bf16[2,20,16,128]{3,2,1,0:T(8,128)(2,1)S(1)} %get-tuple-element.53), channel_id=1, source_target_pairs={{8,0},{9,1},{10,2},{11,3},{12,4},{13,5},{14,6},{15,7},{16,8},{17,9... | collective-permute-start | bytes 491528 | tf_op jit(solution)/shard_map/ppermute | solution.py:515
  91.5 1.9 %collective-permute-start.20 = (bf16[2,20,16,128]{3,2,1,0:T(8,128)(2,1)S(1)}, bf16[2,20,16,128]{3,2,1,0:T(8,128)(2,1)S(1)}, u32[]{:S(2)}, u32[]{:S(2)}) collective-permute-start(bf16[2,20,16,128]{3,2,1,0:T(8,128)(2,1)S(1)} %get-tuple-element.54), channel_id=1, source_target_pairs={{8,4},{9,5},{10,6},{11,7},{12,0},{13,1},{14,2},{15,3},{16,12},{17,... | collective-permute-start | bytes 491528 | tf_op jit(solution)/shard_map/ppermute | solution.py:515
  93.4 4.1 %collective-permute-done.19.rest_6_ = bf16[2,20,16,128]{3,2,1,0:T(8,128)(2,1)S(1)} collective-permute-done((bf16[2,20,16,128]{3,2,1,0:T(8,128)(2,1)S(1)}, bf16[2,20,16,128]{3,2,1,0:T(8,128)(2,1)S(1)}, u32[]{:S(2)}, u32[]{:S(2)}) %collective-permute-start.19) | collective-permute-done | bytes 163872 | tf_op jit(solution)/shard_map/ppermute | solution.py:515
  97.6 3.7 %collective-permute-done.20.rest_7_ = bf16[2,20,16,128]{3,2,1,0:T(8,128)(2,1)S(1)} collective-permute-done((bf16[2,20,16,128]{3,2,1,0:T(8,128)(2,1)S(1)}, bf16[2,20,16,128]{3,2,1,0:T(8,128)(2,1)S(1)}, u32[]{:S(2)}, u32[]{:S(2)}) %collective-permute-start.20) | collective-permute-done | bytes 163872 | tf_op jit(solution)/shard_map/ppermute | solution.py:515
  101.3 0.0 collective-permute-done.18.rest_5_
  101.3 1.5 %finish.1 = f32[2,960,256]{2,1,0:T(8,128)} custom-call(f32[1,256]{1,0:T(1,128)S(1)} %bitcast.22, f32[2,10,32,128]{3,2,1,0:T(8,128)S(1)} %get-tuple-element.40.rest_0_, f32[2,10,32,128]{3,2,1,0:T(8,128)S(1)} %collective-permute-done.15.rest_1_, f32[2,10,16,128]{3,2,1,0:T(8,128)S(1)} %collective-permute-done.16.rest_2_, ...), custom_call_target="tpu_custom_call" | custom-call | tf_op jit(solution)/shard_map/finish/pallas_call | solution.py:470
  (17 shorter events, 0.1 us)
Async XLA Ops:
  0.0 10.9 %collective-permute-start = (bf16[64,7680]{1,0:T(8,128)(2,1)}, bf16[64,7680]{1,0:T(8,128)(2,1)S(1)}, u32[]{:S(2)}, u32[]{:S(2)}) collective-permute-start(bf16[64,7680]{1,0:T(8,128)(2,1)} %own.1), channel_id=1, source_target_pairs={{0,4},{1,5},{2,6},{3,7},{4,0},{5,1},{6,2},{7,3},{8,12},{9,13},{10,... | collective-permute-start | bytes 2949128 | tf_op jit(solution)/shard_map/ppermute | solution.py:515
  1.5 8.9 %collective-permute-start.4 = (bf16[64,256]{1,0:T(8,128)(2,1)S(1)}, bf16[64,256]{1,0:T(8,128)(2,1)S(1)}, u32[]{:S(2)}, u32[]{:S(2)}) collective-permute-start(bf16[64,256]{1,0:T(8,128)(2,1)S(1)} %get-tuple-element.55), channel_id=1, source_target_pairs={{0,4},{1,6},{2,5},{3,7},{4,0},{5,2},{6,1},{7,3},{8,12},{9,14},{10,... | collective-permute-start | bytes 98312 | tf_op jit(solution)/shard_map/ppermute | solution.py:515
  1.5 8.8 %collective-permute-start.3 = (bf16[64,256]{1,0:T(8,128)(2,1)S(1)}, bf16[64,256]{1,0:T(8,128)(2,1)S(1)}, u32[]{:S(2)}, u32[]{:S(2)}) collective-permute-start(bf16[64,256]{1,0:T(8,128)(2,1)S(1)} %get-tuple-element.55), channel_id=1, source_target_pairs={{0,0},{1,2},{2,1},{3,3},{4,4},{5,6},{6,5},{7,7},{8,8},{9,10},{10,9... | collective-permute-start | bytes 98312 | tf_op jit(solution)/shard_map/ppermute | solution.py:515
  2.2 8.2 %collective-permute-start.2 = (bf16[64,256]{1,0:T(8,128)(2,1)S(1)}, bf16[64,256]{1,0:T(8,128)(2,1)S(1)}, u32[]{:S(2)}, u32[]{:S(2)}) collective-permute-start(bf16[64,256]{1,0:T(8,128)(2,1)S(1)} %get-tuple-element.56), channel_id=1, source_target_pairs={{0,5},{1,4},{2,7},{3,6},{4,1},{5,0},{6,3},{7,2},{8,13},{9,12},{10,... | collective-permute-start | bytes 98312 | tf_op jit(solution)/shard_map/ppermute | solution.py:515
  7.6 3.2 %collective-permute-start.1 = (bf16[64,256]{1,0:T(8,128)(2,1)S(1)}, bf16[64,256]{1,0:T(8,128)(2,1)S(1)}, u32[]{:S(2)}, u32[]{:S(2)}) collective-permute-start(bf16[64,256]{1,0:T(8,128)(2,1)S(1)} %get-tuple-element.56), channel_id=1, source_target_pairs={{0,1},{1,0},{2,3},{3,2},{4,5},{5,4},{6,7},{7,6},{8,9},{9,8},{10,11... | collective-permute-start | bytes 98312 | tf_op jit(solution)/shard_map/ppermute | solution.py:515
  10.4 18.1 %copy-start.3 = (s32[512]{0:T(512)S(1)}, s32[512]{0:T(512)}, u32[]{:S(2)}) copy-start(s32[512]{0:T(512)} %param.15) | copy-start | bytes 6148
  10.4 0.6 copy-start.5
  10.4 0.6 copy-start.6
  10.4 0.6 copy-start.7
  10.8 0.6 copy-start.8
  11.5 0.9 copy-start.4
  25.8 4.2 %collective-permute-start.8 = (bf16[320,128]{1,0:T(8,128)(2,1)}, bf16[320,128]{1,0:T(8,128)(2,1)S(1)}, u32[]{:S(2)}, u32[]{:S(2)}) collective-permute-start(bf16[320,128]{1,0:T(8,128)(2,1)} %get-tuple-element.35), channel_id=1, source_target_pairs={{0,1},{1,0},{2,3},{3,2},{4,5},{5,4},{6,7},{7,6},{8,9},{9,8},{10,11... | collective-permute-start | bytes 245768 | tf_op jit(solution)/shard_map/ppermute | solution.py:515
  26.8 4.3 %collective-permute-start.9 = (bf16[320,128]{1,0:T(8,128)(2,1)}, bf16[320,128]{1,0:T(8,128)(2,1)S(1)}, u32[]{:S(2)}, u32[]{:S(2)}) collective-permute-start(bf16[320,128]{1,0:T(8,128)(2,1)} %get-tuple-element.36), channel_id=1, source_target_pairs={{0,2},{1,3},{2,0},{3,1},{4,6},{5,7},{6,4},{7,5},{8,10},{9,11},{10,... | collective-permute-start | bytes 245768 | tf_op jit(solution)/shard_map/ppermute | solution.py:515
  27.3 4.6 %collective-permute-start.10 = (bf16[320,128]{1,0:T(8,128)(2,1)}, bf16[320,128]{1,0:T(8,128)(2,1)S(1)}, u32[]{:S(2)}, u32[]{:S(2)}) collective-permute-start(bf16[320,128]{1,0:T(8,128)(2,1)} %get-tuple-element.37), channel_id=1, source_target_pairs={{0,3},{1,2},{2,1},{3,0},{4,7},{5,6},{6,5},{7,4},{8,11},{9,10},{10,... | collective-permute-start | bytes 245768 | tf_op jit(solution)/shard_map/ppermute | solution.py:515
  28.5 7.7 %collective-permute-start.5 = (bf16[640,128]{1,0:T(8,128)(2,1)}, bf16[640,128]{1,0:T(8,128)(2,1)S(1)}, u32[]{:S(2)}, u32[]{:S(2)}) collective-permute-start(bf16[640,128]{1,0:T(8,128)(2,1)} %get-tuple-element.31), channel_id=1, source_target_pairs={{0,1},{1,0},{2,3},{3,2},{4,5},{5,4},{6,7},{7,6},{8,9},{9,8},{10,11... | collective-permute-start | bytes 491528 | tf_op jit(solution)/shard_map/ppermute | solution.py:515
  29.6 6.8 %collective-permute-start.6 = (bf16[640,128]{1,0:T(8,128)(2,1)}, bf16[640,128]{1,0:T(8,128)(2,1)S(1)}, u32[]{:S(2)}, u32[]{:S(2)}) collective-permute-start(bf16[640,128]{1,0:T(8,128)(2,1)} %get-tuple-element.32), channel_id=1, source_target_pairs={{0,2},{1,3},{2,0},{3,1},{4,6},{5,7},{6,4},{7,5},{8,10},{9,11},{10,... | collective-permute-start | bytes 491528 | tf_op jit(solution)/shard_map/ppermute | solution.py:515
  30.0 8.9 %collective-permute-start.7 = (bf16[640,128]{1,0:T(8,128)(2,1)}, bf16[640,128]{1,0:T(8,128)(2,1)S(1)}, u32[]{:S(2)}, u32[]{:S(2)}) collective-permute-start(bf16[640,128]{1,0:T(8,128)(2,1)} %get-tuple-element.33), channel_id=1, source_target_pairs={{0,3},{1,2},{2,1},{3,0},{4,7},{5,6},{6,5},{7,4},{8,11},{9,10},{10,... | collective-permute-start | bytes 491528 | tf_op jit(solution)/shard_map/ppermute | solution.py:515
  31.9 11.4 %copy-start = (bf16[16,16,256]{2,1,0:T(8,128)(2,1)S(1)}, bf16[16,16,256]{2,1,0:T(8,128)(2,1)}, u32[]{:S(2)}) copy-start(bf16[16,16,256]{2,1,0:T(8,128)(2,1)} %constant.72.clone.pick_ref) | copy-start | bytes 393220
  31.9 11.4 %copy-start.1 = (bf16[16,16,128]{2,1,0:T(8,128)(2,1)S(1)}, bf16[16,16,128]{2,1,0:T(8,128)(2,1)}, u32[]{:S(2)}) copy-start(bf16[16,16,128]{2,1,0:T(8,128)(2,1)} %constant.73.clone.cut_ref) | copy-start | bytes 196612
  31.9 11.4 %copy-start.2 = (bf16[128,128]{1,0:T(8,128)(2,1)S(1)}, bf16[128,128]{1,0:T(8,128)(2,1)}, u32[]{:S(2)}) copy-start(bf16[128,128]{1,0:T(8,128)(2,1)} %constant.71.clone.turn_ref) | copy-start | bytes 98308
  33.0 10.3 %collective-permute-start.12 = (bf16[4,320,128]{2,1,0:T(8,128)(2,1)S(1)}, bf16[4,320,128]{2,1,0:T(8,128)(2,1)S(1)}, u32[]{:S(2)}, u32[]{:S(2)}) collective-permute-start(bf16[4,320,128]{2,1,0:T(8,128)(2,1)S(1)} %pad_maximum_fusion.1.own_ref), channel_id=1, source_target_pairs={{0,0},{1,1},{2,2},{3,3},{4,4},{5,5},{6,6},{7,7},{8,16},{9,17},{10,... | collective-permute-start | bytes 983048 | tf_op jit(solution)/shard_map/ppermute | solution.py:515
  36.2 7.1 %collective-permute-start.11 = (bf16[4,320,128]{2,1,0:T(8,128)(2,1)S(1)}, bf16[4,320,128]{2,1,0:T(8,128)(2,1)S(1)}, u32[]{:S(2)}, u32[]{:S(2)}) collective-permute-start(bf16[4,320,128]{2,1,0:T(8,128)(2,1)S(1)} %pad_maximum_fusion.1.own_ref), channel_id=1, source_target_pairs={{0,8},{1,9},{2,10},{3,11},{4,12},{5,13},{6,14},{7,15},{8,0},{9,1},... | collective-permute-start | bytes 983048 | tf_op jit(solution)/shard_map/ppermute | solution.py:515
  40.0 24.3 %collective-permute-start.14 = (bf16[4,640,128]{2,1,0:T(8,128)(2,1)S(1)}, bf16[4,640,128]{2,1,0:T(8,128)(2,1)S(1)}, u32[]{:S(2)}, u32[]{:S(2)}) collective-permute-start(bf16[4,640,128]{2,1,0:T(8,128)(2,1)S(1)} %pad_maximum_fusion.own_ref), channel_id=1, source_target_pairs={{0,0},{1,1},{2,2},{3,3},{4,4},{5,5},{6,6},{7,7},{8,16},{9,17},{10,... | collective-permute-start | bytes 1966088 | tf_op jit(solution)/shard_map/ppermute | solution.py:515
  43.2 21.1 %collective-permute-start.13 = (bf16[4,640,128]{2,1,0:T(8,128)(2,1)S(1)}, bf16[4,640,128]{2,1,0:T(8,128)(2,1)S(1)}, u32[]{:S(2)}, u32[]{:S(2)}) collective-permute-start(bf16[4,640,128]{2,1,0:T(8,128)(2,1)S(1)} %pad_maximum_fusion.own_ref), channel_id=1, source_target_pairs={{0,8},{1,9},{2,10},{3,11},{4,12},{5,13},{6,14},{7,15},{8,0},{9,1},... | collective-permute-start | bytes 1966088 | tf_op jit(solution)/shard_map/ppermute | solution.py:515
  56.0 33.4 %collective-permute-start.16 = (f32[2,10,16,128]{3,2,1,0:T(8,128)S(1)}, f32[2,10,16,128]{3,2,1,0:T(8,128)S(1)}, u32[]{:S(2)}, u32[]{:S(2)}) collective-permute-start(f32[2,10,16,128]{3,2,1,0:T(8,128)S(1)} %get-tuple-element.46), channel_id=1, source_target_pairs={{8,0},{9,1},{10,2},{11,3},{12,4},{13,5},{14,6},{15,7},{16,8},{17,9... | collective-permute-start | bytes 491528 | tf_op jit(solution)/shard_map/ppermute | solution.py:515
  59.4 30.1 %collective-permute-start.17 = (f32[2,10,16,128]{3,2,1,0:T(8,128)S(1)}, f32[2,10,16,128]{3,2,1,0:T(8,128)S(1)}, u32[]{:S(2)}, u32[]{:S(2)}) collective-permute-start(f32[2,10,16,128]{3,2,1,0:T(8,128)S(1)} %get-tuple-element.47), channel_id=1, source_target_pairs={{8,4},{9,5},{10,6},{11,7},{12,0},{13,1},{14,2},{15,3},{16,12},{17,... | collective-permute-start | bytes 491528 | tf_op jit(solution)/shard_map/ppermute | solution.py:515
  63.2 26.2 %collective-permute-start.15 = (f32[2,10,32,128]{3,2,1,0:T(8,128)S(1)}, f32[2,10,32,128]{3,2,1,0:T(8,128)S(1)}, u32[]{:S(2)}, u32[]{:S(2)}) collective-permute-start(f32[2,10,32,128]{3,2,1,0:T(8,128)S(1)} %get-tuple-element.45), channel_id=1, source_target_pairs={{0,4},{1,5},{2,6},{3,7},{4,0},{5,1},{6,2},{7,3},{8,12},{9,13},{10,... | collective-permute-start | bytes 983048 | tf_op jit(solution)/shard_map/ppermute | solution.py:515
  89.5 11.8 %collective-permute-start.18 = (f32[2,20,32,128]{3,2,1,0:T(8,128)S(1)}, f32[2,20,32,128]{3,2,1,0:T(8,128)S(1)}, u32[]{:S(2)}, u32[]{:S(2)}) collective-permute-start(f32[2,20,32,128]{3,2,1,0:T(8,128)S(1)} %get-tuple-element.52), channel_id=1, source_target_pairs={{0,4},{1,5},{2,6},{3,7},{4,0},{5,1},{6,2},{7,3},{8,12},{9,13},{10,... | collective-permute-start | bytes 1966088 | tf_op jit(solution)/shard_map/ppermute | solution.py:515
  89.6 8.0 %collective-permute-start.19 = (bf16[2,20,16,128]{3,2,1,0:T(8,128)(2,1)S(1)}, bf16[2,20,16,128]{3,2,1,0:T(8,128)(2,1)S(1)}, u32[]{:S(2)}, u32[]{:S(2)}) collective-permute-start(bf16[2,20,16,128]{3,2,1,0:T(8,128)(2,1)S(1)} %get-tuple-element.53), channel_id=1, source_target_pairs={{8,0},{9,1},{10,2},{11,3},{12,4},{13,5},{14,6},{15,7},{16,8},{17,9... | collective-permute-start | bytes 491528 | tf_op jit(solution)/shard_map/ppermute | solution.py:515
  91.5 9.8 %collective-permute-start.20 = (bf16[2,20,16,128]{3,2,1,0:T(8,128)(2,1)S(1)}, bf16[2,20,16,128]{3,2,1,0:T(8,128)(2,1)S(1)}, u32[]{:S(2)}, u32[]{:S(2)}) collective-permute-start(bf16[2,20,16,128]{3,2,1,0:T(8,128)(2,1)S(1)} %get-tuple-element.54), channel_id=1, source_target_pairs={{8,4},{9,5},{10,6},{11,7},{12,0},{13,1},{14,2},{15,3},{16,12},{17,... | collective-permute-start | bytes 491528 | tf_op jit(solution)/shard_map/ppermute | solution.py:515
